TPU v7x, 32 devices: a whole 2x2x4 slice. The times are simulated.
32 devices in a mesh: section: 2 (over core), seq: 4 (over z), chan: 4 (over y, x).
Axes of the slice: x: 2, y: 2, z: 4, core: 2. Of those that a mesh axis runs over, the one named last changes fastest.
Arguments:
- layer_inputs: bfloat16 [2, 4, 256, 4096], P('section', None, 'seq', 'chan')
- out_grad: bfloat16 [4, 256, 4096], P(None, 'seq', 'chan')
- rate_weight: bfloat16 [2, 16, 256, 256], P('section', 'chan'), may hold values from -0.375 to 0.375
- input_weight: bfloat16 [2, 16, 256, 256], P('section', 'chan'), may hold values from -0.375 to 0.375
- rate_bias: float32 [2, 4096], P('section', 'chan'), may hold values from -4 to 4
- input_bias: float32 [2, 4096], P('section', 'chan'), may hold values from -4 to 4
- decay_param: float32 [2, 4096], P('section', 'chan')
- norm_gain: float32 [2, 4096], P('section', 'chan'), may hold values from 0.1 to 1.9
- doc_starts: int32 [4, 3], replicated, may hold values from 1 to 255
Outputs:
- input_grads: bfloat16 [2, 4, 256, 4096], P('section', None, 'seq', 'chan')
- rate_weight_grad: float32 [2, 16, 256, 256], P('section', 'chan')
- input_weight_grad: float32 [2, 16, 256, 256], P('section', 'chan')
- vector_grads: float32 [2, 3, 4096], P('section', None, 'chan')
All inputs are finite; a program needn't handle non-finite values.
Results may differ from a plain program's by a relative error of at most 0.0055.
Values may be sent and summed in bfloat16 or wider, within the bound.
No kernel may reach another device: no remote copies, remote signals or barrier semaphores. Data moves between devices by JAX's collectives and lax.ppermute only.
A program may use at most 64 MiB of HBM per device.

v0:
```python
import math

import jax
import jax.numpy as jnp
from jax import lax
from jax.sharding import PartitionSpec as P


def prefix(value, axis, combine, identity, reverse):
    devices, here = (lax.axis_size(axis), lax.axis_index(axis))
    everything = jax.tree.map(lambda part: lax.all_gather(part, axis), value)
    start = jax.tree.map(
        lambda part, zero: jnp.broadcast_to(jnp.asarray(zero, part.dtype), part.shape),
        value,
        identity,
    )

    def turn(k, before):
        at = devices - 1 - k if reverse else k
        reached = at > here if reverse else at < here
        new = combine(before, jax.tree.map(lambda part: part[at], everything))
        return jax.tree.map(lambda a, b: jnp.where(reached, a, b), new, before)

    return lax.fori_loop(0, devices, turn, start)


def from_behind(block, axis, distance):
    devices = range(lax.axis_size(axis))
    route = [(i - distance, i) for i in devices if i - distance in devices]
    return lax.ppermute(block, axis, route)


def pair_combine(first_pair, second_pair):
    return (first_pair[0] * second_pair[0], second_pair[0] * first_pair[1] + second_pair[1])


def on_device(
    layer_inputs,
    out_grad,
    rate_weight,
    input_weight,
    rate_bias,
    input_bias,
    decay_param,
    norm_gain,
    doc_starts,
):
    section_count = lax.axis_size("section")
    section_at = lax.axis_index("section")
    seq_count = lax.axis_size("seq")
    seq_at = lax.axis_index("seq")
    micro_count, tok_rows, chan_width = out_grad.shape
    head_count = rate_weight.shape[1]
    head_size = rate_weight.shape[2]
    full_width = chan_width * lax.axis_size("chan")
    seq_total = tok_rows * seq_count
    position = seq_at * tok_rows + jnp.arange(tok_rows, dtype=jnp.int32)
    ones_row = jnp.ones((chan_width,), jnp.float32)
    zero_row = jnp.zeros((chan_width,), jnp.float32)
    grad_scale = 1.0 / math.sqrt(micro_count * seq_total)

    def layer_step(
        inputs, upstream, starts, weights_both, rate_row, input_row, soft_rate, gain_row
    ):
        xfloat = inputs.astype(jnp.float32)
        square_sum = lax.psum(jnp.sum(xfloat * xfloat, axis=1), "chan")
        inv_rms = lax.rsqrt(square_sum / full_width + 1e-06)[:, None]
        normed = (xfloat * inv_rms * gain_row).astype(jnp.bfloat16)
        normed_wide = normed.astype(jnp.float32)
        by_head = normed.reshape(tok_rows, head_count, head_size)
        pre_both = jnp.einsum(
            "shb,hbc->shc", by_head, weights_both, preferred_element_type=jnp.float32
        )
        pre_rate = pre_both[:, :, :head_size].reshape(tok_rows, chan_width) + rate_row
        pre_input = pre_both[:, :, head_size:].reshape(tok_rows, chan_width) + input_row
        rate_gate = jax.nn.sigmoid(pre_rate)
        input_gate = jax.nn.sigmoid(pre_input)
        log_decay = -8.0 * rate_gate * soft_rate
        is_reset = jnp.logical_or(
            position == 0, jnp.any(position[:, None] == starts[None, :], axis=1)
        )[:, None]
        decay_eff = jnp.where(is_reset, 0.0, jnp.exp(log_decay))
        square_gap = jnp.exp(2.0 * log_decay)
        base_mult = jnp.sqrt(jnp.maximum(-jnp.expm1(2.0 * log_decay), 1e-06))
        multiplier = jnp.where(is_reset, 1.0, base_mult)
        lru_drive = multiplier * input_gate * normed_wide
        decay_prod, local_states = lax.associative_scan(
            pair_combine, (decay_eff, lru_drive), axis=0
        )
        upstream_wide = upstream.astype(jnp.float32)
        next_decay = jnp.concatenate([decay_eff[1:], ones_row[None, :]], axis=0)
        flip_decay, flip_grad = lax.associative_scan(
            pair_combine, (next_decay[::-1], upstream_wide[::-1]), axis=0
        )
        tail_decay = flip_decay[::-1]
        local_grad = flip_grad[::-1]
        shard_decay = decay_prod[-1]
        last_state = local_states[-1]
        first_out = decay_eff[0] * local_grad[0]
        state_in = prefix(
            (shard_decay, last_state), "seq", pair_combine, (ones_row, zero_row), False
        )[1]
        carry_grad = prefix(
            (shard_decay, first_out), "seq", pair_combine, (ones_row, zero_row), True
        )[1]
        states = local_states + decay_prod * state_in
        prev_state = jnp.concatenate([state_in[None, :], states[:-1]], axis=0)
        state_grad = local_grad + tail_decay * carry_grad
        grad_mult = state_grad * input_gate * normed_wide
        grad_log = state_grad * prev_state * decay_eff - jnp.where(
            is_reset, 0.0, grad_mult * square_gap / base_mult
        )
        grad_rate = (grad_log * (-8.0 * soft_rate) * rate_gate * (1.0 - rate_gate)).astype(
            jnp.bfloat16
        )
        grad_input = (
            state_grad * multiplier * normed_wide * input_gate * (1.0 - input_gate)
        ).astype(jnp.bfloat16)
        grad_both = jnp.concatenate(
            [
                grad_rate.reshape(tok_rows, head_count, head_size),
                grad_input.reshape(tok_rows, head_count, head_size),
            ],
            axis=2,
        )
        back_proj = jnp.einsum(
            "shc,hbc->shb", grad_both, weights_both, preferred_element_type=jnp.float32
        ).reshape(tok_rows, chan_width)
        grad_normed = state_grad * multiplier * input_gate + back_proj
        scaled = grad_normed * gain_row
        cross_sum = lax.psum(jnp.sum(xfloat * scaled, axis=1), "chan")[:, None] / full_width
        input_grad = (upstream_wide + inv_rms * scaled - xfloat * inv_rms**3 * cross_sum).astype(
            jnp.bfloat16
        )
        weight_term = jnp.einsum(
            "shb,shc->hbc", by_head, grad_both, preferred_element_type=jnp.float32
        )
        vector_term = jnp.stack(
            [
                jnp.sum(grad_rate.astype(jnp.float32), axis=0),
                jnp.sum(grad_input.astype(jnp.float32), axis=0),
                jnp.sum(grad_normed * xfloat * inv_rms, axis=0),
            ]
        )
        return (input_grad, weight_term, vector_term)

    weights_own = jnp.concatenate([rate_weight[0], input_weight[0]], axis=2)
    soft_own = jax.nn.softplus(-decay_param[0])

    def tick_body(tick_index, loop_state):
        sent_grad, grads_out, weight_acc, vector_acc = loop_state
        arrived = from_behind(sent_grad, "section", -1)
        micro_index = tick_index - (section_count - 1 - section_at)
        is_valid = jnp.logical_and(micro_index >= 0, micro_index < micro_count)
        micro_slot = jnp.clip(micro_index, 0, micro_count - 1)
        inputs = lax.dynamic_index_in_dim(layer_inputs[0], micro_slot, 0, keepdims=False)
        top_grad = lax.dynamic_index_in_dim(out_grad, micro_slot, 0, keepdims=False)
        upstream = jnp.where(section_at == section_count - 1, top_grad, arrived)
        starts = lax.dynamic_index_in_dim(doc_starts, micro_slot, 0, keepdims=False)
        input_grad, weight_term, vector_term = layer_step(
            inputs,
            upstream,
            starts,
            weights_own,
            rate_bias[0],
            input_bias[0],
            soft_own,
            norm_gain[0],
        )
        kept_rows = lax.dynamic_index_in_dim(grads_out, micro_slot, 0, keepdims=False)
        grads_out = lax.dynamic_update_index_in_dim(
            grads_out, jnp.where(is_valid, input_grad, kept_rows), micro_slot, 0
        )
        weight_factor = is_valid.astype(jnp.float32)
        weight_acc = weight_acc + weight_term * weight_factor
        vector_acc = vector_acc + vector_term * weight_factor
        return (input_grad, grads_out, weight_acc, vector_acc)

    weight_init = jnp.zeros((head_count, head_size, 2 * head_size), jnp.float32)
    vector_init = jnp.zeros((3, chan_width), jnp.float32)
    sent_init = jnp.zeros((tok_rows, chan_width), jnp.bfloat16)
    grads_init = jnp.zeros((micro_count, tok_rows, chan_width), jnp.bfloat16)
    tick_count = micro_count + section_count - 1
    loop_out = lax.fori_loop(
        0, tick_count, tick_body, (sent_init, grads_init, weight_init, vector_init)
    )
    weight_sum, vector_sum = lax.psum((loop_out[2], loop_out[3]), "seq")
    weight_sum = weight_sum * grad_scale
    return (
        loop_out[1][None],
        weight_sum[:, :, :head_size][None],
        weight_sum[:, :, head_size:][None],
        (vector_sum * grad_scale)[None],
    )


def solution(mesh):
    in_specs = (
        P("section", None, "seq", "chan"),
        P(None, "seq", "chan"),
        P("section", "chan", None, None),
        P("section", "chan", None, None),
        P("section", "chan"),
        P("section", "chan"),
        P("section", "chan"),
        P("section", "chan"),
        P(),
    )
    out_specs = (
        P("section", None, "seq", "chan"),
        P("section", "chan", None, None),
        P("section", "chan", None, None),
        P("section", None, "chan"),
    )
    return jax.shard_map(
        on_device, mesh=mesh, in_specs=in_specs, out_specs=out_specs, check_vma=False
    )
```

profile of v0, /device:TPU:0, one launch (start us, length us, event | category | flops | bytes accessed | tf_op | source)
XLA Modules:
  0.0 931.6 jit_solution(12191051975030418305)
XLA Ops:
  10.8 823.6 %while.95 = (s32[]{:T(128)}, bf16[64,1024]{1,0:T(8,128)(2,1)S(1)}, bf16[4,64,1024]{2,1,0:T(8,128)(2,1)}, f32[4,256,512]{2,1,0:T(8,128)}, f32[3,1024]{1,0:T(4,128...) while((s32[]{:T(128)}, bf16[64,1024]{1,0:T(8,128)(2,1)S(1)}, ...), condition=%wide.region_13.14_spmd.clone, body=%wide.region_0.13_spmd.clone.sunk | while | flops 211380128 | bytes 57551708 | solution.py:184
  13.0 11.4 %psum.48 = f32[64]{0:T(128)S(1)} all-reduce(f32[64]{0:T(128)S(1)} %fusion.103), channel_id=1, replica_groups=mesh['section'=2,'seq'=4,'chan'=4] {'chan'}, use_global_device_ids=true, to_apply=%region_2.2 | all-reduce | flops 64 | bytes 512 | tf_op jit(solution)/shard_map/while/body/eval_jaxpr/psum | solution.py:66
  51.3 13.3 %all-gather.11 = f32[4,1,1024]{2,1,0:T(1,128)S(1)} all-gather(f32[1,1,1024]{2,1,0:T(1,128)S(1)} %add_bitcast_fusion.5), channel_id=1, replica_groups=mesh['section'=2,'seq'=4,'chan'=4] {'seq'}, dimensions={0}, use_global_device_ids=true | all-gather | bytes 20480 | tf_op jit(solution)/shard_map/while/body/eval_jaxpr/all_gather | solution.py:11
  113.5 13.1 %all-gather.9 = f32[4,1,1024]{2,1,0:T(1,128)S(1)} all-gather(f32[1,1,1024]{2,1,0:T(1,128)S(1)} %add_bitcast_fusion.4), channel_id=1, replica_groups=mesh['section'=2,'seq'=4,'chan'=4] {'seq'}, dimensions={0}, use_global_device_ids=true | all-gather | bytes 20480 | tf_op jit(solution)/shard_map/while/body/eval_jaxpr/all_gather | solution.py:11
  127.3 3.1 while.97
  130.4 13.3 %all-gather.10 = f32[4,1,1024]{2,1,0:T(1,128)S(1)} all-gather(f32[1,1,1024]{2,1,0:T(1,128)} %get-tuple-element.1188), channel_id=1, replica_groups=mesh['section'=2,'seq'=4,'chan'=4] {'seq'}, dimensions={0}, use_global_device_ids=true | all-gather | bytes 20480 | tf_op jit(solution)/shard_map/while/body/eval_jaxpr/all_gather | solution.py:11
  144.3 3.2 while.96
  153.0 4.3 rev.31
  157.4 4.3 rev.30
  165.2 8.0 psum.49
  178.1 9.0 psum.48
  214.0 13.1 %all-gather.11 = f32[4,1,1024]{2,1,0:T(1,128)S(1)} all-gather(f32[1,1,1024]{2,1,0:T(1,128)S(1)} %add_bitcast_fusion.5), channel_id=1, replica_groups=mesh['section'=2,'seq'=4,'chan'=4] {'seq'}, dimensions={0}, use_global_device_ids=true | all-gather | bytes 20480 | tf_op jit(solution)/shard_map/while/body/eval_jaxpr/all_gather | solution.py:11
  276.1 13.1 %all-gather.9 = f32[4,1,1024]{2,1,0:T(1,128)S(1)} all-gather(f32[1,1,1024]{2,1,0:T(1,128)S(1)} %add_bitcast_fusion.4), channel_id=1, replica_groups=mesh['section'=2,'seq'=4,'chan'=4] {'seq'}, dimensions={0}, use_global_device_ids=true | all-gather | bytes 20480 | tf_op jit(solution)/shard_map/while/body/eval_jaxpr/all_gather | solution.py:11
  293.0 13.3 %all-gather.10 = f32[4,1,1024]{2,1,0:T(1,128)S(1)} all-gather(f32[1,1,1024]{2,1,0:T(1,128)} %get-tuple-element.1188), channel_id=1, replica_groups=mesh['section'=2,'seq'=4,'chan'=4] {'seq'}, dimensions={0}, use_global_device_ids=true | all-gather | bytes 20480 | tf_op jit(solution)/shard_map/while/body/eval_jaxpr/all_gather | solution.py:11
  306.8 3.2 while.96
  315.6 4.3 rev.31
  319.9 4.3 rev.30
  327.8 8.0 psum.49
  335.8 3.6 select_add_fusion.2
  342.4 9.8 %psum.48 = f32[64]{0:T(128)S(1)} all-reduce(f32[64]{0:T(128)S(1)} %fusion.103), channel_id=1, replica_groups=mesh['section'=2,'seq'=4,'chan'=4] {'chan'}, use_global_device_ids=true, to_apply=%region_2.2 | all-reduce | flops 64 | bytes 512 | tf_op jit(solution)/shard_map/while/body/eval_jaxpr/psum | solution.py:66
  379.1 13.1 %all-gather.11 = f32[4,1,1024]{2,1,0:T(1,128)S(1)} all-gather(f32[1,1,1024]{2,1,0:T(1,128)S(1)} %add_bitcast_fusion.5), channel_id=1, replica_groups=mesh['section'=2,'seq'=4,'chan'=4] {'seq'}, dimensions={0}, use_global_device_ids=true | all-gather | bytes 20480 | tf_op jit(solution)/shard_map/while/body/eval_jaxpr/all_gather | solution.py:11
  441.1 13.1 %all-gather.9 = f32[4,1,1024]{2,1,0:T(1,128)S(1)} all-gather(f32[1,1,1024]{2,1,0:T(1,128)S(1)} %add_bitcast_fusion.4), channel_id=1, replica_groups=mesh['section'=2,'seq'=4,'chan'=4] {'seq'}, dimensions={0}, use_global_device_ids=true | all-gather | bytes 20480 | tf_op jit(solution)/shard_map/while/body/eval_jaxpr/all_gather | solution.py:11
  458.0 13.3 %all-gather.10 = f32[4,1,1024]{2,1,0:T(1,128)S(1)} all-gather(f32[1,1,1024]{2,1,0:T(1,128)} %get-tuple-element.1188), channel_id=1, replica_groups=mesh['section'=2,'seq'=4,'chan'=4] {'seq'}, dimensions={0}, use_global_device_ids=true | all-gather | bytes 20480 | tf_op jit(solution)/shard_map/while/body/eval_jaxpr/all_gather | solution.py:11
  471.9 3.2 while.96
  480.6 4.3 rev.31
  485.0 4.3 rev.30
  492.8 8.0 psum.49
  500.8 3.6 select_add_fusion.2
  507.4 9.0 psum.48
  543.3 13.1 %all-gather.11 = f32[4,1,1024]{2,1,0:T(1,128)S(1)} all-gather(f32[1,1,1024]{2,1,0:T(1,128)S(1)} %add_bitcast_fusion.5), channel_id=1, replica_groups=mesh['section'=2,'seq'=4,'chan'=4] {'seq'}, dimensions={0}, use_global_device_ids=true | all-gather | bytes 20480 | tf_op jit(solution)/shard_map/while/body/eval_jaxpr/all_gather | solution.py:11
  605.3 13.1 %all-gather.9 = f32[4,1,1024]{2,1,0:T(1,128)S(1)} all-gather(f32[1,1,1024]{2,1,0:T(1,128)S(1)} %add_bitcast_fusion.4), channel_id=1, replica_groups=mesh['section'=2,'seq'=4,'chan'=4] {'seq'}, dimensions={0}, use_global_device_ids=true | all-gather | bytes 20480 | tf_op jit(solution)/shard_map/while/body/eval_jaxpr/all_gather | solution.py:11
  622.2 13.3 %all-gather.10 = f32[4,1,1024]{2,1,0:T(1,128)S(1)} all-gather(f32[1,1,1024]{2,1,0:T(1,128)} %get-tuple-element.1188), channel_id=1, replica_groups=mesh['section'=2,'seq'=4,'chan'=4] {'seq'}, dimensions={0}, use_global_device_ids=true | all-gather | bytes 20480 | tf_op jit(solution)/shard_map/while/body/eval_jaxpr/all_gather | solution.py:11
  636.1 3.2 while.96
  644.8 4.3 rev.31
  649.2 4.3 rev.30
  657.0 8.0 psum.49
  665.0 3.6 select_add_fusion.2
  671.6 9.8 %psum.48 = f32[64]{0:T(128)S(1)} all-reduce(f32[64]{0:T(128)S(1)} %fusion.103), channel_id=1, replica_groups=mesh['section'=2,'seq'=4,'chan'=4] {'chan'}, use_global_device_ids=true, to_apply=%region_2.2 | all-reduce | flops 64 | bytes 512 | tf_op jit(solution)/shard_map/while/body/eval_jaxpr/psum | solution.py:66
  708.3 13.1 %all-gather.11 = f32[4,1,1024]{2,1,0:T(1,128)S(1)} all-gather(f32[1,1,1024]{2,1,0:T(1,128)S(1)} %add_bitcast_fusion.5), channel_id=1, replica_groups=mesh['section'=2,'seq'=4,'chan'=4] {'seq'}, dimensions={0}, use_global_device_ids=true | all-gather | bytes 20480 | tf_op jit(solution)/shard_map/while/body/eval_jaxpr/all_gather | solution.py:11
  770.4 13.1 %all-gather.9 = f32[4,1,1024]{2,1,0:T(1,128)S(1)} all-gather(f32[1,1,1024]{2,1,0:T(1,128)S(1)} %add_bitcast_fusion.4), channel_id=1, replica_groups=mesh['section'=2,'seq'=4,'chan'=4] {'seq'}, dimensions={0}, use_global_device_ids=true | all-gather | bytes 20480 | tf_op jit(solution)/shard_map/while/body/eval_jaxpr/all_gather | solution.py:11
  787.2 13.3 %all-gather.10 = f32[4,1,1024]{2,1,0:T(1,128)S(1)} all-gather(f32[1,1,1024]{2,1,0:T(1,128)} %get-tuple-element.1188), channel_id=1, replica_groups=mesh['section'=2,'seq'=4,'chan'=4] {'seq'}, dimensions={0}, use_global_device_ids=true | all-gather | bytes 20480 | tf_op jit(solution)/shard_map/while/body/eval_jaxpr/all_gather | solution.py:11
  801.1 3.2 while.96
  809.9 4.3 rev.31
  814.2 4.3 rev.30
  822.0 7.9 psum.49
  830.0 3.6 select_add_fusion.2
  835.2 19.3 %psum.43 = f32[3,1024]{1,0:T(4,128)S(1)} all-reduce(f32[3,1024]{1,0:T(4,128)S(1)} %copy-done.18), channel_id=1, replica_groups=mesh['section'=2,'seq'=4,'chan'=4] {'seq'}, use_global_device_ids=true, to_apply=%region_15.16 | all-reduce | flops 3072 | bytes 24576 | tf_op jit(solution)/shard_map/psum | solution.py:187
  855.1 66.3 %all-reduce.52.cloned.1.call-done = f32[4,256,512]{2,1,0:T(8,128)} async-done(((f32[4,256,512]{2,1,0:T(8,128)}), f32[4,256,512]{2,1,0:T(8,128)}) %all-reduce.52.cloned.1.call-update) | async-done | bytes 2097168 | tf_op jit(solution)/shard_map/psum | solution.py:187
  (1458 shorter events, 494.2 us)
Async XLA Ops:
  7.2 914.2 %all-reduce.52.cloned.1.call-start = ((), (), s32[]{:S(2)}) async-start(), calls=%async_computation | async-start | bytes 4194304 | tf_op jit(solution)/shard_map/psum | solution.py:187
  11.5 64.5 %collective-permute-start = (bf16[64,1024]{1,0:T(8,128)(2,1)}, bf16[64,1024]{1,0:T(8,128)(2,1)}, u32[]{:S(2)}, u32[]{:S(2)}) collective-permute-start(bf16[64,1024]{1,0:T(8,128)(2,1)} %broadcast_select_fusion.2), channel_id=1, source_target_pairs={{16,0},{17,1},{18,2},{19,3},{20,4},{21,5},{22,6},{23,7},{24,8},{25... | collective-permute-start | bytes 393224 | tf_op jit(solution)/shard_map/while/body/eval_jaxpr/ppermute | solution.py:30
  70.5 9.3 copy-start.6
  89.6 8.8 copy-start.25
  93.4 10.9 %copy-start.23 = (f32[1,1024]{1,0:T(1,128)S(1)}, f32[1,1024]{1,0:T(1,128)}, u32[]{:S(2)}) copy-start(f32[1,1024]{1,0:T(1,128)} %slice.1705) | copy-start | bytes 12292 | tf_op jit(solution)/shard_map/while
  112.6 49.0 %copy-start.3 = (f32[64,1024]{1,0:T(8,128)S(1)}, f32[64,1024]{1,0:T(8,128)}, u32[]{:S(2)}) copy-start(f32[64,1024]{1,0:T(8,128)} %copy-done.2) | copy-start | bytes 786436 | tf_op jit(solution)/shard_map/while
  112.7 49.0 %copy-start.4 = (f32[64,1024]{1,0:T(8,128)S(1)}, f32[64,1024]{1,0:T(8,128)}, u32[]{:S(2)}) copy-start(f32[64,1024]{1,0:T(8,128)} %pad.856) | copy-start | bytes 786436 | tf_op jit(solution)/shard_map/while
  112.7 49.0 %copy-start.5 = (f32[63,1024]{1,0:T(8,128)S(1)}, f32[63,1024]{1,0:T(8,128)}, u32[]{:S(2)}) copy-start(f32[63,1024]{1,0:T(8,128)} %pad.860) | copy-start | bytes 774148 | tf_op jit(solution)/shard_map/while
  147.4 15.3 %copy-start.15 = (f32[1024]{0:T(1024)S(1)}, f32[1024]{0:T(1024)}, u32[]{:S(2)}) copy-start(f32[1024]{0:T(1024)} %copy-done.14) | copy-start | bytes 12292 | tf_op jit(solution)/shard_map/while
  147.5 15.3 %copy-start.20 = (f32[64]{0:T(128)S(1)}, f32[64]{0:T(128)}, u32[]{:S(2)}) copy-start(f32[64]{0:T(128)} %copy-done.19) | copy-start | bytes 772 | tf_op jit(solution)/shard_map/while
  151.3 11.5 %copy-start.28 = (pred[64]{0:T(512)(128)(4,1)S(1)}, pred[64]{0:T(512)(128)(4,1)}, u32[]{:S(2)}) copy-start(pred[64]{0:T(512)(128)(4,1)} %copy-done.27) | copy-start | bytes 196 | tf_op jit(solution)/shard_map/while
  176.7 61.9 %collective-permute-start = (bf16[64,1024]{1,0:T(8,128)(2,1)}, bf16[64,1024]{1,0:T(8,128)(2,1)}, u32[]{:S(2)}, u32[]{:S(2)}) collective-permute-start(bf16[64,1024]{1,0:T(8,128)(2,1)} %broadcast_select_fusion.2), channel_id=1, source_target_pairs={{16,0},{17,1},{18,2},{19,3},{20,4},{21,5},{22,6},{23,7},{24,8},{25... | collective-permute-start | bytes 393224 | tf_op jit(solution)/shard_map/while/body/eval_jaxpr/ppermute | solution.py:30
  233.1 9.3 copy-start.6
  252.1 8.8 copy-start.25
  255.9 10.9 %copy-start.23 = (f32[1,1024]{1,0:T(1,128)S(1)}, f32[1,1024]{1,0:T(1,128)}, u32[]{:S(2)}) copy-start(f32[1,1024]{1,0:T(1,128)} %slice.1705) | copy-start | bytes 12292 | tf_op jit(solution)/shard_map/while
  275.2 49.0 %copy-start.3 = (f32[64,1024]{1,0:T(8,128)S(1)}, f32[64,1024]{1,0:T(8,128)}, u32[]{:S(2)}) copy-start(f32[64,1024]{1,0:T(8,128)} %copy-done.2) | copy-start | bytes 786436 | tf_op jit(solution)/shard_map/while
  275.2 49.0 %copy-start.4 = (f32[64,1024]{1,0:T(8,128)S(1)}, f32[64,1024]{1,0:T(8,128)}, u32[]{:S(2)}) copy-start(f32[64,1024]{1,0:T(8,128)} %pad.856) | copy-start | bytes 786436 | tf_op jit(solution)/shard_map/while
  275.2 49.0 %copy-start.5 = (f32[63,1024]{1,0:T(8,128)S(1)}, f32[63,1024]{1,0:T(8,128)}, u32[]{:S(2)}) copy-start(f32[63,1024]{1,0:T(8,128)} %pad.860) | copy-start | bytes 774148 | tf_op jit(solution)/shard_map/while
  310.0 15.3 %copy-start.15 = (f32[1024]{0:T(1024)S(1)}, f32[1024]{0:T(1024)}, u32[]{:S(2)}) copy-start(f32[1024]{0:T(1024)} %copy-done.14) | copy-start | bytes 12292 | tf_op jit(solution)/shard_map/while
  310.0 15.3 %copy-start.20 = (f32[64]{0:T(128)S(1)}, f32[64]{0:T(128)}, u32[]{:S(2)}) copy-start(f32[64]{0:T(128)} %copy-done.19) | copy-start | bytes 772 | tf_op jit(solution)/shard_map/while
  313.8 11.5 %copy-start.28 = (pred[64]{0:T(512)(128)(4,1)S(1)}, pred[64]{0:T(512)(128)(4,1)}, u32[]{:S(2)}) copy-start(pred[64]{0:T(512)(128)(4,1)} %copy-done.27) | copy-start | bytes 196 | tf_op jit(solution)/shard_map/while
  340.9 62.8 %collective-permute-start = (bf16[64,1024]{1,0:T(8,128)(2,1)}, bf16[64,1024]{1,0:T(8,128)(2,1)}, u32[]{:S(2)}, u32[]{:S(2)}) collective-permute-start(bf16[64,1024]{1,0:T(8,128)(2,1)} %broadcast_select_fusion.2), channel_id=1, source_target_pairs={{16,0},{17,1},{18,2},{19,3},{20,4},{21,5},{22,6},{23,7},{24,8},{25... | collective-permute-start | bytes 393224 | tf_op jit(solution)/shard_map/while/body/eval_jaxpr/ppermute | solution.py:30
  398.1 9.3 copy-start.6
  421.0 10.9 %copy-start.23 = (f32[1,1024]{1,0:T(1,128)S(1)}, f32[1,1024]{1,0:T(1,128)}, u32[]{:S(2)}) copy-start(f32[1,1024]{1,0:T(1,128)} %slice.1705) | copy-start | bytes 12292 | tf_op jit(solution)/shard_map/while
  440.3 49.0 %copy-start.3 = (f32[64,1024]{1,0:T(8,128)S(1)}, f32[64,1024]{1,0:T(8,128)}, u32[]{:S(2)}) copy-start(f32[64,1024]{1,0:T(8,128)} %copy-done.2) | copy-start | bytes 786436 | tf_op jit(solution)/shard_map/while
  440.3 49.0 %copy-start.4 = (f32[64,1024]{1,0:T(8,128)S(1)}, f32[64,1024]{1,0:T(8,128)}, u32[]{:S(2)}) copy-start(f32[64,1024]{1,0:T(8,128)} %pad.856) | copy-start | bytes 786436 | tf_op jit(solution)/shard_map/while
  440.3 49.0 %copy-start.5 = (f32[63,1024]{1,0:T(8,128)S(1)}, f32[63,1024]{1,0:T(8,128)}, u32[]{:S(2)}) copy-start(f32[63,1024]{1,0:T(8,128)} %pad.860) | copy-start | bytes 774148 | tf_op jit(solution)/shard_map/while
  475.0 15.3 %copy-start.15 = (f32[1024]{0:T(1024)S(1)}, f32[1024]{0:T(1024)}, u32[]{:S(2)}) copy-start(f32[1024]{0:T(1024)} %copy-done.14) | copy-start | bytes 12292 | tf_op jit(solution)/shard_map/while
  475.1 15.3 %copy-start.20 = (f32[64]{0:T(128)S(1)}, f32[64]{0:T(128)}, u32[]{:S(2)}) copy-start(f32[64]{0:T(128)} %copy-done.19) | copy-start | bytes 772 | tf_op jit(solution)/shard_map/while
  478.9 11.5 %copy-start.28 = (pred[64]{0:T(512)(128)(4,1)S(1)}, pred[64]{0:T(512)(128)(4,1)}, u32[]{:S(2)}) copy-start(pred[64]{0:T(512)(128)(4,1)} %copy-done.27) | copy-start | bytes 196 | tf_op jit(solution)/shard_map/while
  505.9 62.0 %collective-permute-start = (bf16[64,1024]{1,0:T(8,128)(2,1)}, bf16[64,1024]{1,0:T(8,128)(2,1)}, u32[]{:S(2)}, u32[]{:S(2)}) collective-permute-start(bf16[64,1024]{1,0:T(8,128)(2,1)} %broadcast_select_fusion.2), channel_id=1, source_target_pairs={{16,0},{17,1},{18,2},{19,3},{20,4},{21,5},{22,6},{23,7},{24,8},{25... | collective-permute-start | bytes 393224 | tf_op jit(solution)/shard_map/while/body/eval_jaxpr/ppermute | solution.py:30
  562.4 9.3 copy-start.6
  585.2 10.9 %copy-start.23 = (f32[1,1024]{1,0:T(1,128)S(1)}, f32[1,1024]{1,0:T(1,128)}, u32[]{:S(2)}) copy-start(f32[1,1024]{1,0:T(1,128)} %slice.1705) | copy-start | bytes 12292 | tf_op jit(solution)/shard_map/while
  604.5 49.0 %copy-start.3 = (f32[64,1024]{1,0:T(8,128)S(1)}, f32[64,1024]{1,0:T(8,128)}, u32[]{:S(2)}) copy-start(f32[64,1024]{1,0:T(8,128)} %copy-done.2) | copy-start | bytes 786436 | tf_op jit(solution)/shard_map/while
  604.5 49.0 %copy-start.4 = (f32[64,1024]{1,0:T(8,128)S(1)}, f32[64,1024]{1,0:T(8,128)}, u32[]{:S(2)}) copy-start(f32[64,1024]{1,0:T(8,128)} %pad.856) | copy-start | bytes 786436 | tf_op jit(solution)/shard_map/while
  604.5 49.0 %copy-start.5 = (f32[63,1024]{1,0:T(8,128)S(1)}, f32[63,1024]{1,0:T(8,128)}, u32[]{:S(2)}) copy-start(f32[63,1024]{1,0:T(8,128)} %pad.860) | copy-start | bytes 774148 | tf_op jit(solution)/shard_map/while
  639.3 15.3 %copy-start.15 = (f32[1024]{0:T(1024)S(1)}, f32[1024]{0:T(1024)}, u32[]{:S(2)}) copy-start(f32[1024]{0:T(1024)} %copy-done.14) | copy-start | bytes 12292 | tf_op jit(solution)/shard_map/while
  639.3 15.3 %copy-start.20 = (f32[64]{0:T(128)S(1)}, f32[64]{0:T(128)}, u32[]{:S(2)}) copy-start(f32[64]{0:T(128)} %copy-done.19) | copy-start | bytes 772 | tf_op jit(solution)/shard_map/while
  643.1 11.5 %copy-start.28 = (pred[64]{0:T(512)(128)(4,1)S(1)}, pred[64]{0:T(512)(128)(4,1)}, u32[]{:S(2)}) copy-start(pred[64]{0:T(512)(128)(4,1)} %copy-done.27) | copy-start | bytes 196 | tf_op jit(solution)/shard_map/while
  670.1 62.8 %collective-permute-start = (bf16[64,1024]{1,0:T(8,128)(2,1)}, bf16[64,1024]{1,0:T(8,128)(2,1)}, u32[]{:S(2)}, u32[]{:S(2)}) collective-permute-start(bf16[64,1024]{1,0:T(8,128)(2,1)} %broadcast_select_fusion.2), channel_id=1, source_target_pairs={{16,0},{17,1},{18,2},{19,3},{20,4},{21,5},{22,6},{23,7},{24,8},{25... | collective-permute-start | bytes 393224 | tf_op jit(solution)/shard_map/while/body/eval_jaxpr/ppermute | solution.py:30
  727.4 9.3 copy-start.6
  750.2 10.9 %copy-start.23 = (f32[1,1024]{1,0:T(1,128)S(1)}, f32[1,1024]{1,0:T(1,128)}, u32[]{:S(2)}) copy-start(f32[1,1024]{1,0:T(1,128)} %slice.1705) | copy-start | bytes 12292 | tf_op jit(solution)/shard_map/while
  769.5 49.0 %copy-start.3 = (f32[64,1024]{1,0:T(8,128)S(1)}, f32[64,1024]{1,0:T(8,128)}, u32[]{:S(2)}) copy-start(f32[64,1024]{1,0:T(8,128)} %copy-done.2) | copy-start | bytes 786436 | tf_op jit(solution)/shard_map/while
  769.5 49.0 %copy-start.4 = (f32[64,1024]{1,0:T(8,128)S(1)}, f32[64,1024]{1,0:T(8,128)}, u32[]{:S(2)}) copy-start(f32[64,1024]{1,0:T(8,128)} %pad.856) | copy-start | bytes 786436 | tf_op jit(solution)/shard_map/while
  769.5 49.0 %copy-start.5 = (f32[63,1024]{1,0:T(8,128)S(1)}, f32[63,1024]{1,0:T(8,128)}, u32[]{:S(2)}) copy-start(f32[63,1024]{1,0:T(8,128)} %pad.860) | copy-start | bytes 774148 | tf_op jit(solution)/shard_map/while
  804.3 15.3 %copy-start.15 = (f32[1024]{0:T(1024)S(1)}, f32[1024]{0:T(1024)}, u32[]{:S(2)}) copy-start(f32[1024]{0:T(1024)} %copy-done.14) | copy-start | bytes 12292 | tf_op jit(solution)/shard_map/while
  804.3 15.3 %copy-start.20 = (f32[64]{0:T(128)S(1)}, f32[64]{0:T(128)}, u32[]{:S(2)}) copy-start(f32[64]{0:T(128)} %copy-done.19) | copy-start | bytes 772 | tf_op jit(solution)/shard_map/while
  808.1 11.5 %copy-start.28 = (pred[64]{0:T(512)(128)(4,1)S(1)}, pred[64]{0:T(512)(128)(4,1)}, u32[]{:S(2)}) copy-start(pred[64]{0:T(512)(128)(4,1)} %copy-done.27) | copy-start | bytes 196 | tf_op jit(solution)/shard_map/while
  (88 other events, 341.5 us)
Sparse Core Ops, SparseCore 0:
  834.6 86.7 all-reduce.51
where the time goes:
time: 946 us; the launch traced here: 932 us
  local copies, waits for them, and re-layouts  325 us (34%)
  blocking collectives  306 us (32%)
  other arithmetic  188 us (20%)
  waiting for transfers between devices  66.3 us (7%)
  matrix products  20 us (2%)
  between operations  14.1 us (1%)
    all_gather x15, blocking collectives, prefix(): everything = jax.tree.map(lambda part: lax.all_gather(part, axis), value)  198 us
    slice x205, local copies, waits for them, and re-layouts, layer_step(): lax.associative_scan(pair_combine, (next_decay[::-1], upstream_wide[::-1]...  98.9 us
    psum x1, waiting for transfers between devices, on_device(): weight_sum, vector_sum = lax.psum((loop_out[2], loop_out[3]), 'seq')  66.3 us
    psum x5, blocking collectives, layer_step(): square_sum = lax.psum(jnp.sum(xfloat * xfloat, axis=1), 'chan')  49 us
    pad x100, local copies, waits for them, and re-layouts, layer_step(): lax.associative_scan(pair_combine, (next_decay[::-1], upstream_wide[::-1]...  42.1 us
    mul x90, other arithmetic, pair_combine(): first_pair[0] * second_pair[0]  40.3 us
    psum x5, blocking collectives, layer_step(): lax.psum(jnp.sum(xfloat * scaled, axis=1), 'chan')[:, None] / full_width  39.8 us
    slice x175, local copies, waits for them, and re-layouts, layer_step(): lax.associative_scan(pair_combine, (decay_eff, lru_drive), axis=0)  34.3 us
  transfers between devices with their start and end apart: 6, of which 1 were waited for; matrix products, arithmetic and copies ran while one was open for 20% of the time, Pallas kernels for 0%

commit v1 on v0

v1 whole, which is shorter than its diff:
```python
import functools
import math

import jax
import jax.numpy as jnp
from jax import lax
from jax.experimental import pallas as pl
from jax.experimental.pallas import tpu as pltpu
from jax.sharding import PartitionSpec as P

F32 = jnp.float32
BF16 = jnp.bfloat16
HIGH = lax.Precision.HIGHEST
VECTOR_ROWS = 16
DIRECT_RANKS = 4


def params(limit=24):
    return pltpu.CompilerParams(vmem_limit_bytes=limit * 1024 * 1024)


def cost(flops, size):
    return pl.CostEstimate(flops=flops, bytes_accessed=size, transcendentals=0)


def contract(a, b, dims, precision=None):
    return lax.dot_general(
        a, b, ((dims[:1], dims[1:]), ((), ())), precision=precision, preferred_element_type=F32
    )


def row_order(rows, tok_rows):
    shift = tok_rows.bit_length() - 1
    at = lax.broadcasted_iota(jnp.int32, (rows, rows), 0)
    source = lax.broadcasted_iota(jnp.int32, (rows, rows), 1)
    inner = jnp.bitwise_and(at, tok_rows - 1)
    wanted = (
        jnp.left_shift(jnp.right_shift(at, shift), shift)
        + jnp.bitwise_and(inner, 7) * (tok_rows // 8)
        + jnp.right_shift(inner, 3)
    )
    return jnp.where(wanted == source, 1.0, 0.0).astype(F32)


def to_column(parts):
    total = parts[0]
    for part in parts[1:]:
        total = total + part
    return contract(total, jnp.full((8, 128), 0.125, F32), (0, 0), HIGH)


def to_row(folded):
    return contract(jnp.ones((8, folded.shape[1]), F32), folded, (1, 1), HIGH)


def fold_lanes(value):
    total = value[:, :128]
    for at in range(128, value.shape[1], 128):
        total = total + value[:, at : at + 128]
    return total


def widen(column, width):
    return jnp.concatenate([column] * (width // 128), axis=1)


def square_kernel(x_ref, out_ref):
    total = None
    for at in range(0, x_ref.shape[1], 128):
        part = x_ref[:, at : at + 128].astype(F32)
        total = part * part if total is None else total + part * part
    out_ref[...] = to_row(total)


def permute_kernel(tok_rows, x_ref, up_ref, xp_ref, upp_ref):
    order = row_order(x_ref.shape[0], tok_rows).astype(BF16)
    width = 256
    for at in range(0, x_ref.shape[1], width):
        cols = slice(at, at + width)
        xp_ref[:, cols] = contract(order, x_ref[:, cols], (1, 0)).astype(BF16)
        upp_ref[:, cols] = contract(order, up_ref[:, cols], (1, 0)).astype(BF16)


def sublane_scan(decay, value, reverse):
    at = lax.broadcasted_iota(jnp.int32, decay.shape, 0)
    for step in (1, 2, 4):
        shift = 8 - step if reverse else step
        inside = at < 8 - step if reverse else at >= step
        value_far = pltpu.roll(value, shift, 0)
        decay_far = pltpu.roll(decay, shift, 0)
        value = jnp.where(inside, value + decay * value_far, value)
        decay = jnp.where(inside, decay * decay_far, decay)
    return decay, value


def reverse_blocks(decay_ref, up_ref, base, tok_rows, width):
    carry = jnp.zeros((8, width), F32)
    for pair in reversed(range(tok_rows // 16)):
        rows = pl.ds(base + 16 * pair, 16)
        decay = decay_ref[rows, :]
        upstream = up_ref[rows, :].astype(F32)
        carry = decay[8:] * (upstream[8:] + carry)
        carry = decay[:8] * (upstream[:8] + carry)
    return carry


def forward_kernel(
    micro_count,
    tok_rows,
    full_width,
    square_count,
    seq_at,
    starts,
    *refs,
):
    squares = refs[:square_count]
    (
        x_ref, up_ref, rw_ref, iw_ref, rb_ref, ib_ref, soft_ref, gain_ref,
        normed_ref, decay_ref, p1_ref, p2_ref, p3_ref, p4_ref,
        fdecay_ref, fstate_ref, rdecay_ref, rgrad_ref, pay_ref, inv_ref,
        keep_ref, prer_ref, prei_ref,
    ) = refs[square_count:]
    rows_total, width = x_ref.shape
    shift = tok_rows.bit_length() - 1

    @pl.when(pl.program_id(0) == 0)
    def _():
        column = to_column([part[...] for part in squares])
        order = row_order(rows_total, tok_rows)
        column = contract(order, column, (1, 0), HIGH)
        inv_ref[...] = lax.rsqrt(column / full_width + 1e-06)
        at = lax.broadcasted_iota(jnp.int32, (rows_total, 128), 0)
        inner = jnp.bitwise_and(at, tok_rows - 1)
        micro = jnp.right_shift(at, shift)
        position = (
            seq_at[0] * tok_rows
            + jnp.bitwise_and(inner, 7) * (tok_rows // 8)
            + jnp.right_shift(inner, 3)
        )
        reset = position == 0
        for m in range(micro_count):
            for d in range(starts.shape[1]):
                hit = jnp.logical_and(micro == m, position == starts[m, d])
                reset = jnp.logical_or(reset, hit)
        keep_ref[...] = jnp.where(reset, 0.0, 1.0)

    gain = gain_ref[...]
    normed = (x_ref[...].astype(F32) * widen(inv_ref[...], width) * gain).astype(BF16)
    normed_ref[...] = normed
    prer_ref[...] = contract(normed, rw_ref[0], (1, 0)) + rb_ref[...]
    prei_ref[...] = contract(normed, iw_ref[0], (1, 0)) + ib_ref[...]
    rate_scale = -8.0 * soft_ref[...]

    def per_micro(m, _):
        base = pl.multiple_of(m * tok_rows, tok_rows)
        state = jnp.zeros((8, width), F32)
        product = jnp.ones((8, width), F32)
        for pair in range(tok_rows // 16):
            rows = pl.ds(base + 16 * pair, 16)
            x_norm = normed_ref[rows, :].astype(F32)
            keep = widen(keep_ref[rows, :], width)
            rate_gate = 1.0 / (1.0 + jnp.exp(-prer_ref[rows, :]))
            input_gate = 1.0 / (1.0 + jnp.exp(-prei_ref[rows, :]))
            log_decay = rate_gate * rate_scale
            decay = jnp.exp(log_decay)
            square_gap = decay * decay
            twice = 2.0 * log_decay
            small = -twice * (
                1.0 + twice * (1 / 2 + twice * (1 / 6 + twice * (1 / 24 + twice * (1 / 120))))
            )
            gap = jnp.where(twice > -0.1, small, 1.0 - square_gap)
            gap = jnp.maximum(gap, 1e-06)
            inv_mult = lax.rsqrt(gap)
            multiplier = jnp.where(keep > 0.0, gap * inv_mult, 1.0)
            decay_eff = decay * keep
            rate_slope = rate_scale * rate_gate * (1.0 - rate_gate)
            gated = input_gate * x_norm
            passed = multiplier * input_gate
            drive = passed * x_norm
            decay_ref[rows, :] = decay_eff
            p1_ref[rows, :] = decay_eff * rate_slope
            p2_ref[rows, :] = keep * gated * square_gap * inv_mult * rate_slope
            p3_ref[rows, :] = drive * (1.0 - input_gate)
            p4_ref[rows, :] = passed
            for half in (slice(0, 8), slice(8, 16)):
                state = decay_eff[half] * state + drive[half]
                product = decay_eff[half] * product
        leaving = reverse_blocks(decay_ref, up_ref, base, tok_rows, width)
        fdecay, fstate = sublane_scan(product, state, False)
        rdecay, rgrad = sublane_scan(product, leaving, True)
        block_rows = pl.ds(pl.multiple_of(m * 8, 8), 8)
        fdecay_ref[block_rows, :] = fdecay
        fstate_ref[block_rows, :] = fstate
        rdecay_ref[block_rows, :] = rdecay
        rgrad_ref[block_rows, :] = rgrad
        pay_ref[pl.ds(m, 1), :] = fdecay[7:8]
        pay_ref[pl.ds(micro_count + m, 1), :] = fstate[7:8]
        pay_ref[pl.ds(2 * micro_count + m, 1), :] = rgrad[0:1]
        return 0

    lax.fori_loop(0, micro_count, per_micro, 0)


def leaving_kernel(micro_count, tok_rows, up_ref, decay_ref, rdecay_in, rgrad_ref, pay_ref):
    width = up_ref.shape[1]

    def per_micro(m, _):
        base = pl.multiple_of(m * tok_rows, tok_rows)
        carry = jnp.zeros((8, width), F32)
        product = jnp.ones((8, width), F32)
        for pair in reversed(range(tok_rows // 16)):
            rows = pl.ds(base + 16 * pair, 16)
            decay = decay_ref[rows, :]
            upstream = up_ref[rows, :].astype(F32)
            carry = decay[8:] * (upstream[8:] + carry)
            carry = decay[:8] * (upstream[:8] + carry)
            product = product * decay[8:] * decay[:8]
        _, rgrad = sublane_scan(product, carry, True)
        rgrad_ref[pl.ds(pl.multiple_of(m * 8, 8), 8), :] = rgrad
        pay_ref[pl.ds(m, 1), :] = rgrad[0:1]
        return 0

    lax.fori_loop(0, micro_count, per_micro, 0)


def ranked(refs, rank, at):
    if len(refs) == 1:
        return refs[0][at]
    chosen = refs[0][...]
    for k in range(1, len(refs)):
        chosen = jnp.where(jnp.bitwise_xor(rank, at) == k, refs[k][...], chosen)
    return chosen


def backward_kernel(
    micro_count,
    tok_rows,
    seq_count,
    pay_count,
    late_count,
    seq_at,
    *refs,
):
    pays = refs[:pay_count]
    lates = refs[pay_count : pay_count + late_count]
    (
        x_ref, up_ref, normed_ref, decay_ref, p1_ref, p2_ref, p3_ref, p4_ref,
        fdecay_ref, fstate_ref, rdecay_ref, rgrad_ref, inv_ref, gain_ref, rw_ref, iw_ref,
        part_ref, cross_ref, wr_ref, wi_ref,
        enter_ref, leave_ref, slope_ref, direct_ref, gr_ref, gi_ref, fold_ref,
    ) = refs[pay_count + late_count :]
    rows_total, width = x_ref.shape
    rank = seq_at[0]
    micro = micro_count

    state_in = jnp.zeros((micro, width), F32)
    grad_in = jnp.zeros((micro, width), F32)
    for at in range(seq_count):
        pay = ranked(pays, rank, at)
        state_in = jnp.where(
            at < rank, pay[micro : 2 * micro] + pay[:micro] * state_in, state_in
        )
    for at in reversed(range(seq_count)):
        pay = ranked(pays, rank, at)
        first = ranked(lates, rank, at) if late_count else pay[2 * micro :]
        grad_in = jnp.where(at > rank, first + pay[:micro] * grad_in, grad_in)
    enter_ref[...] = state_in
    leave_ref[...] = grad_in

    sub = lax.broadcasted_iota(jnp.int32, (8, width), 0)

    def per_micro(m, sums):
        sum_rate, sum_input = sums
        base = pl.multiple_of(m * tok_rows, tok_rows)
        block_rows = pl.ds(pl.multiple_of(m * 8, 8), 8)
        enter = enter_ref[pl.ds(m, 1), :]
        leave = leave_ref[pl.ds(m, 1), :]
        after = fstate_ref[block_rows, :] + fdecay_ref[block_rows, :] * enter
        state = jnp.where(sub == 0, enter, pltpu.roll(after, 1, 0))
        before = rgrad_ref[block_rows, :] + rdecay_ref[block_rows, :] * leave
        carry = jnp.where(sub == 7, leave, pltpu.roll(before, 7, 0))
        for pair in range(tok_rows // 16):
            rows = pl.ds(base + 16 * pair, 16)
            decay = decay_ref[rows, :]
            drive = p4_ref[rows, :] * normed_ref[rows, :].astype(F32)
            middle = decay[:8] * state + drive[:8]
            previous = jnp.concatenate([state, middle], axis=0)
            state = decay[8:] * middle + drive[8:]
            slope_ref[pl.ds(16 * pair, 16), :] = previous * p1_ref[rows, :] - p2_ref[rows, :]
        for pair in reversed(range(tok_rows // 16)):
            rows = pl.ds(base + 16 * pair, 16)
            decay = decay_ref[rows, :]
            upstream = up_ref[rows, :].astype(F32)
            late = upstream[8:] + carry
            early = upstream[:8] + decay[8:] * late
            carry = decay[:8] * early
            grad = jnp.concatenate([early, late], axis=0)
            grad_rate = (grad * slope_ref[pl.ds(16 * pair, 16), :]).astype(BF16)
            grad_input = (grad * p3_ref[rows, :]).astype(BF16)
            gr_ref[rows, :] = grad_rate
            gi_ref[rows, :] = grad_input
            direct_ref[rows, :] = grad * p4_ref[rows, :]
            wide_rate = grad_rate.astype(F32)
            wide_input = grad_input.astype(F32)
            sum_rate = sum_rate + wide_rate[:8] + wide_rate[8:]
            sum_input = sum_input + wide_input[:8] + wide_input[8:]
        return sum_rate, sum_input

    zero = jnp.zeros((8, width), F32)
    sum_rate, sum_input = lax.fori_loop(0, micro, per_micro, (zero, zero))

    normed = normed_ref[...]
    wr_ref[0, :width, :] = contract(normed, gr_ref[...], (0, 0)).astype(BF16)
    wi_ref[0, :width, :] = contract(normed, gi_ref[...], (0, 0)).astype(BF16)
    direct_ref[...] += contract(gr_ref[...], rw_ref[0], (1, 1)) + contract(
        gi_ref[...], iw_ref[0], (1, 1)
    )
    gain = gain_ref[...]

    def per_part(m, carry):
        sum_gain = carry
        rows = pl.ds(pl.multiple_of(m * tok_rows, tok_rows), tok_rows)
        inv = widen(inv_ref[rows, :], width)
        x = x_ref[rows, :].astype(F32)
        grad_normed = direct_ref[rows, :]
        scaled = grad_normed * gain
        part_ref[rows, :] = up_ref[rows, :].astype(F32) + inv * scaled
        weighted = grad_normed * x * inv
        folded = fold_lanes(x * scaled)

        @pl.when(pl.program_id(0) == 0)
        def _():
            fold_ref[rows, :] = folded

        @pl.when(pl.program_id(0) > 0)
        def _():
            fold_ref[rows, :] += folded

        for at in range(0, tok_rows, 8):
            sum_gain = sum_gain + weighted[at : at + 8]
        return sum_gain

    sum_gain = lax.fori_loop(0, micro, per_part, zero)
    vector = jnp.concatenate(
        [
            jnp.sum(sum_rate, axis=0, keepdims=True),
            jnp.sum(sum_input, axis=0, keepdims=True),
            jnp.sum(sum_gain, axis=0, keepdims=True),
            jnp.zeros((VECTOR_ROWS - 3, width), F32),
        ],
        axis=0,
    )
    high = vector.astype(BF16)
    wr_ref[0, width:, :] = high
    wi_ref[0, width:, :] = (vector - high.astype(F32)).astype(BF16)

    @pl.when(pl.program_id(0) == pl.num_programs(0) - 1)
    def _():
        cross_ref[...] = to_row(fold_ref[...])


def finish_block(part_ref, x_ref, inv, scale):
    return part_ref[...] - x_ref[...].astype(F32) * scale


def finish_kernel(full_width, cross_count, part_ref, x_ref, inv_ref, *refs):
    column = to_column([part[...] for part in refs[:cross_count]]) / full_width
    out_ref = refs[cross_count]
    inv = inv_ref[...]
    scale = inv * inv * inv * column
    for at in range(0, x_ref.shape[1], 128):
        cols = slice(at, at + 128)
        out_ref[:, cols] = (part_ref[:, cols] - x_ref[:, cols].astype(F32) * scale).astype(BF16)


def last_kernel(
    full_width, tok_rows, cross_count, section_at, part_ref, x_ref, inv_ref, early_ref, *refs
):
    column = to_column([part[...] for part in refs[:cross_count]]) / full_width
    out_ref = refs[cross_count]
    inv = inv_ref[...]
    scale = inv * inv * inv * column
    order = row_order(x_ref.shape[0], tok_rows).astype(BF16)
    bottom = section_at[0] == 0
    for at in range(0, x_ref.shape[1], 256):
        cols = slice(at, at + 256)
        value = part_ref[:, cols] - x_ref[:, cols].astype(F32) * widen(scale, 256)
        value = jnp.where(bottom, value.astype(BF16), early_ref[:, cols])
        out_ref[:, cols] = contract(order, value, (0, 0)).astype(BF16)


def owner_kernel(own_ref, *refs):
    total = own_ref[...].astype(F32)
    for part in refs[:-1]:
        total = total + part[...].astype(F32)
    refs[-1][...] = total.astype(BF16)


def exchange(value, axis):
    count = lax.axis_size(axis)
    if count != DIRECT_RANKS:
        return [lax.all_gather(value, axis)]
    return [value] + [
        lax.ppermute(value, axis, [(i, i ^ k) for i in range(count)]) for k in (3, 2, 1)[::-1]
    ]


def swap_sections(value):
    return lax.ppermute(value, "section", [(0, 1), (1, 0)])


def total_over_seq(value):
    count = lax.axis_size("seq")
    heads = value.shape[0]
    if count != DIRECT_RANKS or heads != count:
        return lax.psum(value.astype(F32), "seq").astype(BF16)
    rank = lax.axis_index("seq")
    taken = [
        lax.dynamic_index_in_dim(value, jnp.bitwise_xor(rank, k), 0, keepdims=False)
        for k in range(count)
    ]
    arrived = [
        lax.ppermute(taken[k], "seq", [(i, i ^ k) for i in range(count)]) for k in range(1, count)
    ]
    shape = value.shape[1:]
    owned = pl.pallas_call(
        owner_kernel, out_shape=jax.ShapeDtypeStruct(shape, BF16), compiler_params=params()
    )(taken[0], *arrived)
    back = [owned] + [
        lax.ppermute(owned, "seq", [(i, i ^ k) for i in range(count)]) for k in range(1, count)
    ]
    full = jnp.stack(back)
    return jnp.stack(
        [
            lax.dynamic_index_in_dim(full, jnp.bitwise_xor(rank, h), 0, keepdims=False)
            for h in range(count)
        ]
    )


def on_device(
    layer_inputs,
    out_grad,
    rate_weight,
    input_weight,
    rate_bias,
    input_bias,
    decay_param,
    norm_gain,
    doc_starts,
):
    micro, tok_rows, chan_width = out_grad.shape
    seq_count = lax.axis_size("seq")
    heads, size = rate_weight.shape[1:3]
    rows = micro * tok_rows
    full_width = chan_width * lax.axis_size("chan")
    grad_scale = 1.0 / math.sqrt(micro * tok_rows * seq_count)
    seq_at = lax.axis_index("seq").reshape(1).astype(jnp.int32)
    section = lax.axis_index("section")
    section_at = section.reshape(1).astype(jnp.int32)

    x_raw = layer_inputs.reshape(rows, chan_width)
    up_raw = out_grad.reshape(rows, chan_width)
    rate_weight, input_weight = rate_weight[0], input_weight[0]
    soft = jax.nn.softplus(-decay_param)

    def shape(dims, dtype=F32):
        return jax.ShapeDtypeStruct(dims, dtype)

    smem = pl.BlockSpec(memory_space=pltpu.SMEM)
    whole = pl.BlockSpec(memory_space=pltpu.VMEM)

    def col(lead):
        return pl.BlockSpec((lead, size), lambda h: (0, h))

    def fixed(dims):
        return pl.BlockSpec(dims, lambda h: (0,) * len(dims))

    head_block = pl.BlockSpec((1, size, size), lambda h: (h, 0, 0))

    squares = exchange(
        pl.pallas_call(
            square_kernel, out_shape=shape((8, rows)), compiler_params=params(),
            cost_estimate=cost(2 * rows * chan_width, 2 * rows * chan_width),
        )(x_raw),
        "chan",
    )
    if len(squares) == 1:
        squares = [squares[0][k] for k in range(lax.axis_size("chan"))]
    x, upstream = pl.pallas_call(
        functools.partial(permute_kernel, tok_rows),
        out_shape=(shape((rows, chan_width), BF16),) * 2,
        compiler_params=params(),
        cost_estimate=cost(4 * rows * rows * chan_width, 8 * rows * chan_width),
    )(x_raw, up_raw)

    row_vectors = [rate_bias, input_bias, soft, norm_gain]
    big = shape((rows, chan_width))
    blocks = shape((micro * 8, chan_width))
    forward = pl.pallas_call(
        functools.partial(forward_kernel, micro, tok_rows, full_width, len(squares)),
        grid=(heads,),
        in_specs=[smem, smem]
        + [fixed((8, rows))] * len(squares)
        + [col(rows)] * 2
        + [head_block] * 2
        + [col(1)] * 4,
        out_specs=[col(rows)] * 6 + [col(micro * 8)] * 4 + [col(3 * micro), fixed((rows, 128))],
        out_shape=[shape((rows, chan_width), BF16)]
        + [big] * 5
        + [blocks] * 4
        + [shape((3 * micro, chan_width)), shape((rows, 128))],
        scratch_shapes=[
            pltpu.VMEM((rows, 128), F32),
            pltpu.VMEM((rows, size), F32),
            pltpu.VMEM((rows, size), F32),
        ],
        compiler_params=params(),
        cost_estimate=cost(4 * rows * size * chan_width, 24 * rows * chan_width),
    )
    (
        normed, decay, p1, p2, p3, p4, fdecay, fstate, rdecay, rgrad, pay, inv,
    ) = forward(seq_at, doc_starts, *squares, x, upstream, rate_weight, input_weight, *row_vectors)
    pays = exchange(pay, "seq")

    def pay_spec(array):
        if array.ndim == 3:
            return pl.BlockSpec(array.shape[:2] + (size,), lambda h: (0, 0, h))
        return col(array.shape[0])

    def backward(upstream, rgrad, lates):
        wrows = size + VECTOR_ROWS
        wide = pl.BlockSpec((1, wrows, size), lambda h: (h, 0, 0))
        return pl.pallas_call(
            functools.partial(
                backward_kernel, micro, tok_rows, seq_count, len(pays), len(lates)
            ),
            grid=(heads,),
            in_specs=[smem]
            + [pay_spec(array) for array in pays + lates]
            + [col(rows)] * 8
            + [col(micro * 8)] * 4
            + [fixed((rows, 128)), col(1), head_block, head_block],
            out_specs=[col(rows), fixed((8, rows)), wide, wide],
            out_shape=[
                big,
                shape((8, rows)),
                shape((heads, wrows, size), BF16),
                shape((heads, wrows, size), BF16),
            ],
            scratch_shapes=[
                pltpu.VMEM((micro, size), F32),
                pltpu.VMEM((micro, size), F32),
                pltpu.VMEM((tok_rows, size), F32),
                pltpu.VMEM((rows, size), F32),
                pltpu.VMEM((rows, size), BF16),
                pltpu.VMEM((rows, size), BF16),
                pltpu.VMEM((rows, 128), F32),
            ],
            compiler_params=params(),
            cost_estimate=cost(8 * rows * size * chan_width, 30 * rows * chan_width),
        )(
            seq_at, *pays, *lates, x, upstream, normed, decay, p1, p2, p3, p4,
            fdecay, fstate, rdecay, rgrad, inv, norm_gain, rate_weight, input_weight,
        )

    def crossed(cross):
        parts = exchange(cross, "chan")
        if len(parts) == 1:
            parts = [parts[0][k] for k in range(lax.axis_size("chan"))]
        return parts

    part, cross, rate_top, input_top = backward(upstream, rgrad, [])
    cross_parts = crossed(cross)
    early = pl.pallas_call(
        functools.partial(finish_kernel, full_width, len(cross_parts)),
        in_specs=[whole] * (3 + len(cross_parts)),
        out_specs=whole,
        out_shape=shape((rows, chan_width), BF16),
        compiler_params=params(),
        cost_estimate=cost(4 * rows * chan_width, 8 * rows * chan_width),
    )(part, x, inv, *cross_parts)
    arrived = swap_sections(early)

    late_rgrad, late_pay = pl.pallas_call(
        functools.partial(leaving_kernel, micro, tok_rows),
        grid=(heads,),
        in_specs=[col(rows), col(rows), col(micro * 8)],
        out_specs=[col(micro * 8), col(micro)],
        out_shape=[blocks, shape((micro, chan_width))],
        compiler_params=params(),
        cost_estimate=cost(4 * rows * chan_width, 6 * rows * chan_width),
    )(arrived, decay, rdecay)
    lates = exchange(late_pay, "seq")
    part, cross, rate_low, input_low = backward(arrived, late_rgrad, lates)

    top = section == 1
    mine_top = jnp.where(top, input_top, swap_sections(rate_top))
    total_top = total_over_seq(mine_top)
    mine_low = jnp.where(top, swap_sections(input_low), rate_low)
    total_low = total_over_seq(mine_low)
    kept = jnp.where(top, total_top, total_low)
    other = swap_sections(jnp.where(top, total_low, total_top))
    rate_total = jnp.where(top, other, kept).astype(F32) * grad_scale
    input_total = jnp.where(top, kept, other).astype(F32) * grad_scale

    cross_parts = crossed(cross)
    grads = pl.pallas_call(
        functools.partial(last_kernel, full_width, tok_rows, len(cross_parts)),
        in_specs=[smem] + [whole] * (4 + len(cross_parts)),
        out_specs=whole,
        out_shape=shape((rows, chan_width), BF16),
        compiler_params=params(),
        cost_estimate=cost(2 * rows * rows * chan_width, 10 * rows * chan_width),
    )(section_at, part, x, inv, early, *cross_parts)

    vector = rate_total[:, size : size + 3] + input_total[:, size : size + 3]
    vector = jnp.swapaxes(vector, 0, 1).reshape(3, chan_width)
    return (
        grads.reshape(1, micro, tok_rows, chan_width),
        rate_total[None, :, :size],
        input_total[None, :, :size],
        vector[None],
    )


def solution(mesh):
    in_specs = (
        P("section", None, "seq", "chan"),
        P(None, "seq", "chan"),
        P("section", "chan", None, None),
        P("section", "chan", None, None),
        P("section", "chan"),
        P("section", "chan"),
        P("section", "chan"),
        P("section", "chan"),
        P(),
    )
    out_specs = (
        P("section", None, "seq", "chan"),
        P("section", "chan", None, None),
        P("section", "chan", None, None),
        P("section", None, "chan"),
    )
    return jax.shard_map(
        on_device, mesh=mesh, in_specs=in_specs, out_specs=out_specs, check_vma=False
    )
```

time: 946 us -> 120 us (0.13); the launches traced: 932 us -> 120 us
  local copies, waits for them, and re-layouts: 325 us -> 8.05 us
  blocking collectives: 306 us -> 0 us
  other arithmetic: 188 us -> 2.57 us
  starting transfers between devices: 6.44 us -> 54.4 us
  waiting for transfers between devices: 66.3 us -> 34.6 us
  matrix products: 20 us -> 0 us
  Pallas kernels: 0 us -> 19.2 us
  between operations: 14.1 us -> 0.89 us
    all_gather x15 -> x0, blocking collectives: 198 us -> none  [prefix(): everything = jax.tree.map(lambda part: lax.all_gather(part, axis), value)]
    slice x395 -> x0, local copies, waits for them, and re-layouts: 148 us -> none  [the longest x205 98.9 us: layer_step(): lax.associative_scan(pair_combine, (next_decay[::-1], upstream_wide[::-1]...]
    psum x11 -> x0, blocking collectives: 108 us -> none  [the longest x5 49 us: layer_step(): square_sum = lax.psum(jnp.sum(xfloat * xfloat, axis=1), 'chan')]
    psum x1 -> x0, waiting for transfers between devices: 66.3 us -> none  [on_device(): weight_sum, vector_sum = lax.psum((loop_out[2], loop_out[3]), 'seq')]
    pad x190 -> x0, local copies, waits for them, and re-layouts: 62 us -> none  [the longest x100 42.1 us: layer_step(): lax.associative_scan(pair_combine, (next_decay[::-1], upstream_wide[::-1]...]
    concatenate x86 -> x0, other arithmetic: 56.5 us -> none  [the longest x45 30 us: layer_step(): lax.associative_scan(pair_combine, (decay_eff, lru_drive), axis=0)]
    ppermute x5 -> x31, starting transfers between devices: 6.4 us -> 54.4 us  [the longest x6 23.9 us: total_over_seq(): lax.ppermute(owned, 'seq', [(i, i ^ k) for i in range(count)])]
    mul x97 -> x1, other arithmetic: 45.6 us -> 0.31 us  [on_device(): input_total = jnp.where(top, kept, other).astype(F32) * grad_scale]
  transfers between devices with their start and end apart: 6 -> 31, of which waited for: 1 -> 16; matrix products, arithmetic and copies ran while one was open for 20% -> 2% of each run, Pallas kernels for 0% -> 7%
where the time goes in v1:
time: 120 us
  starting transfers between devices  54.4 us (45%)
  waiting for transfers between devices  34.6 us (29%)
  Pallas kernels  19.2 us (16%)
  local copies, waits for them, and re-layouts  8.05 us (7%)
  other arithmetic  2.57 us (2%)
    ppermute x6, starting transfers between devices, total_over_seq(): lax.ppermute(owned, 'seq', [(i, i ^ k) for i in range(count)])  23.9 us
    ppermute x15, starting transfers between devices, exchange(): lax.ppermute(value, axis, [(i, i ^ k) for i in range(count)])  20.4 us
    ppermute x15, waiting for transfers between devices, exchange(): lax.ppermute(value, axis, [(i, i ^ k) for i in range(count)])  17 us
    ppermute x6, waiting for transfers between devices, total_over_seq(): lax.ppermute(owned, 'seq', [(i, i ^ k) for i in range(count)])  11.7 us
    pallas_call x2, Pallas kernels, backward(): pl.pallas_call(functools.partial(backward_kernel, micro, tok_rows, seq_co...  9.79 us
    ppermute x6, starting transfers between devices, total_over_seq(): lax.ppermute(taken[k], 'seq', [(i, i ^ k) for i in range(count)])  9.42 us
    unnamed x25, local copies, waits for them, and re-layouts  6.33 us
    pallas_call x1, Pallas kernels, on_device(): forward(seq_at, doc_starts, *squares, x, upstream, rate_weight, input_wei...  5.72 us
  transfers between devices with their start and end apart: 31, of which 16 were waited for; matrix products, arithmetic and copies ran while one was open for 2% of the time, Pallas kernels for 7%

profile of v1, /device:TPU:0, one launch (start us, length us, event | category | flops | bytes accessed | tf_op | source)
XLA Modules:
  0.0 119.6 jit_solution(13648108717662006903)
XLA Ops:
  0.7 1.1 copy-done.2
  2.0 3.0 %collective-permute-start = (f32[8,256]{1,0:T(8,128)S(1)}, f32[8,256]{1,0:T(8,128)S(1)}, u32[]{:S(2)}, u32[]{:S(2)}) collective-permute-start(f32[8,256]{1,0:T(8,128)S(1)} %shard_map.120.refs_0_), channel_id=1, source_target_pairs={{0,1},{1,0},{2,3},{3,2},{4,5},{5,4},{6,7},{7,6},{8,9},{9,8},{10,11... | collective-permute-start | bytes 24584 | tf_op jit(solution)/shard_map/ppermute | solution.py:404
  5.0 1.5 %collective-permute-start.1 = (f32[8,256]{1,0:T(8,128)S(1)}, f32[8,256]{1,0:T(8,128)S(1)}, u32[]{:S(2)}, u32[]{:S(2)}) collective-permute-start(f32[8,256]{1,0:T(8,128)S(1)} %shard_map.120.refs_0_), channel_id=1, source_target_pairs={{0,2},{1,3},{2,0},{3,1},{4,6},{5,7},{6,4},{7,5},{8,10},{9,11},{10,... | collective-permute-start | bytes 24584 | tf_op jit(solution)/shard_map/ppermute | solution.py:404
  6.5 0.7 compare_select_fusion.refs_10_
  7.3 1.0 copy-done.6
  8.8 2.3 %collective-permute-done.2.refs_3_ = f32[8,256]{1,0:T(8,128)S(1)} collective-permute-done((f32[8,256]{1,0:T(8,128)S(1)}, f32[8,256]{1,0:T(8,128)S(1)}, u32[]{:S(2)}, u32[]{:S(2)}) %collective-permute-start.2) | collective-permute-done | bytes 8224 | tf_op jit(solution)/shard_map/ppermute | solution.py:404
  11.1 0.7 copy-done.7
  11.8 0.7 copy-done.9
  12.5 0.7 copy-done.10
  13.2 0.7 copy-done.11
  13.8 5.7 %shard_map.122 = (bf16[256,1024]{1,0:T(8,128)(2,1)S(1)}, f32[256,1024]{1,0:T(8,128)S(1)}, f32[256,1024]{1,0:T(8,128)S(1)}, f32[256,1024]{1,0:T(8,128)S(1)}, f32[...) custom-call(s32[1]{0:T(128)} %bitcast.1.seq_at, ...), custom_call_target="tpu_custom_call" | custom-call | flops 268435456 | bytes 6291456 | tf_op jit(solution)/shard_map/pallas_call | solution.py:523
  19.6 1.6 %collective-permute-start.3 = (f32[12,1024]{1,0:T(8,128)S(1)}, f32[12,1024]{1,0:T(8,128)S(1)}, u32[]{:S(2)}, u32[]{:S(2)}) collective-permute-start(f32[12,1024]{1,0:T(8,128)S(1)} %get-tuple-element.30.refs_0_), channel_id=1, source_target_pairs={{0,4},{4,0},{8,12},{12,8},{1,5},{5,1},{9,13},{13,9},{2,6},{6,2},{1... | collective-permute-start | bytes 147464 | tf_op jit(solution)/shard_map/ppermute | solution.py:404
  21.2 2.6 %collective-permute-start.4 = (f32[12,1024]{1,0:T(8,128)S(1)}, f32[12,1024]{1,0:T(8,128)S(1)}, u32[]{:S(2)}, u32[]{:S(2)}) collective-permute-start(f32[12,1024]{1,0:T(8,128)S(1)} %get-tuple-element.30.refs_0_), channel_id=1, source_target_pairs={{0,8},{4,12},{8,0},{12,4},{1,9},{5,13},{9,1},{13,5},{2,10},{6,14},... | collective-permute-start | bytes 147464 | tf_op jit(solution)/shard_map/ppermute | solution.py:404
  24.0 3.8 %collective-permute-done.4.refs_2_ = f32[12,1024]{1,0:T(8,128)S(1)} collective-permute-done((f32[12,1024]{1,0:T(8,128)S(1)}, f32[12,1024]{1,0:T(8,128)S(1)}, u32[]{:S(2)}, u32[]{:S(2)}) %collective-permute-start.4) | collective-permute-done | bytes 49184 | tf_op jit(solution)/shard_map/ppermute | solution.py:404
  27.8 2.1 %collective-permute-done.5.refs_3_ = f32[12,1024]{1,0:T(8,128)S(1)} collective-permute-done((f32[12,1024]{1,0:T(8,128)S(1)}, f32[12,1024]{1,0:T(8,128)S(1)}, u32[]{:S(2)}, u32[]{:S(2)}) %collective-permute-start.5) | collective-permute-done | bytes 49184 | tf_op jit(solution)/shard_map/ppermute | solution.py:404
  29.9 4.9 %shard_map.123 = (f32[256,1024]{1,0:T(8,128)S(1)}, f32[8,256]{1,0:T(8,128)S(1)}, bf16[4,272,256]{2,1,0:T(8,128)(2,1)}, bf16[4,272,256]{2,1,0:T(8,128)(2,1)S(1)}) custom-call(s32[1]{0:T(128)} %bitcast.1.seq_at, f32[12,1024]{1,0:T(8,128)S(1)} %get-tuple-element.30.refs_0_, f32[12,1024]{1,0:T(8,128)S(1)} %collective-permute-done.3.refs_1_, ...), custom_call_target="tpu_custom_call" | custom-call | flops 536870912 | bytes 7864320 | tf_op jit(solution)/shard_map/pallas_call | solution.py:534
  35.3 0.7 collective-permute-start.7
  36.0 2.3 %collective-permute-start.8 = (f32[8,256]{1,0:T(8,128)S(1)}, f32[8,256]{1,0:T(8,128)S(1)}, u32[]{:S(2)}, u32[]{:S(2)}) collective-permute-start(f32[8,256]{1,0:T(8,128)S(1)} %get-tuple-element.43.refs_0_), channel_id=1, source_target_pairs={{0,3},{1,2},{2,1},{3,0},{4,7},{5,6},{6,5},{7,4},{8,11},{9,10},{10,... | collective-permute-start | bytes 24584 | tf_op jit(solution)/shard_map/ppermute | solution.py:404
  38.9 1.6 %collective-permute-done.8.refs_3_ = f32[8,256]{1,0:T(8,128)S(1)} collective-permute-done((f32[8,256]{1,0:T(8,128)S(1)}, f32[8,256]{1,0:T(8,128)S(1)}, u32[]{:S(2)}, u32[]{:S(2)}) %collective-permute-start.8) | collective-permute-done | bytes 8224 | tf_op jit(solution)/shard_map/ppermute | solution.py:404
  41.6 1.4 %collective-permute-done.9.up_ref.refs_9_ = bf16[256,1024]{1,0:T(8,128)(2,1)S(1)} collective-permute-done((bf16[256,1024]{1,0:T(8,128)(2,1)S(1)}, bf16[256,1024]{1,0:T(8,128)(2,1)S(1)}, u32[]{:S(2)}, u32[]{:S(2)}) %collective-permute-start.9) | collective-permute-done | bytes 524320 | tf_op jit(solution)/shard_map/ppermute | solution.py:409
  43.0 0.8 shard_map.125
  43.8 1.5 %collective-permute-start.11 = (f32[4,1024]{1,0:T(4,128)S(1)}, f32[4,1024]{1,0:T(4,128)S(1)}, u32[]{:S(2)}, u32[]{:S(2)}) collective-permute-start(f32[4,1024]{1,0:T(4,128)S(1)} %get-tuple-element.44.refs_4_), channel_id=1, source_target_pairs={{0,8},{4,12},{8,0},{12,4},{1,9},{5,13},{9,1},{13,5},{2,10},{6,14},... | collective-permute-start | bytes 49160 | tf_op jit(solution)/shard_map/ppermute | solution.py:404
  45.3 2.9 %collective-permute-start.12 = (f32[4,1024]{1,0:T(4,128)S(1)}, f32[4,1024]{1,0:T(4,128)S(1)}, u32[]{:S(2)}, u32[]{:S(2)}) collective-permute-start(f32[4,1024]{1,0:T(4,128)S(1)} %get-tuple-element.44.refs_4_), channel_id=1, source_target_pairs={{0,12},{4,8},{8,4},{12,0},{1,13},{5,9},{9,5},{13,1},{2,14},{6,10},... | collective-permute-start | bytes 49160 | tf_op jit(solution)/shard_map/ppermute | solution.py:404
  48.5 2.3 %collective-permute-done.12.refs_7_ = f32[4,1024]{1,0:T(4,128)S(1)} collective-permute-done((f32[4,1024]{1,0:T(4,128)S(1)}, f32[4,1024]{1,0:T(4,128)S(1)}, u32[]{:S(2)}, u32[]{:S(2)}) %collective-permute-start.12) | collective-permute-done | bytes 16416 | tf_op jit(solution)/shard_map/ppermute | solution.py:404
  50.9 4.9 %shard_map.126 = (f32[256,1024]{1,0:T(8,128)S(1)}, f32[8,256]{1,0:T(8,128)S(1)}, bf16[4,272,256]{2,1,0:T(8,128)(2,1)S(1)}, bf16[4,272,256]{2,1,0:T(8,128)(2,1)}) custom-call(s32[1]{0:T(128)} %bitcast.1.seq_at, f32[12,1024]{1,0:T(8,128)S(1)} %get-tuple-element.30.refs_0_, f32[12,1024]{1,0:T(8,128)S(1)} %collective-permute-done.3.refs_1_, ...), custom_call_target="tpu_custom_call" | custom-call | flops 536870912 | bytes 7864320 | tf_op jit(solution)/shard_map/pallas_call | solution.py:534
  55.8 0.8 copy-done.4
  56.6 1.2 broadcast_select_fusion.2
  57.9 3.4 %collective-permute-start.25 = (bf16[272,256]{1,0:T(8,128)(2,1)S(1)}, bf16[272,256]{1,0:T(8,128)(2,1)S(1)}, u32[]{:S(2)}, u32[]{:S(2)}) collective-permute-start(bf16[272,256]{1,0:T(8,128)(2,1)S(1)} %get-tuple-element.71), channel_id=1, source_target_pairs={{0,8},{4,12},{8,0},{12,4},{1,9},{5,13},{9,1},{13,5},{2,10},{6,14},... | collective-permute-start | bytes 417800 | tf_op jit(solution)/shard_map/ppermute | solution.py:423
  61.3 0.9 collective-permute-start.26
  62.5 3.4 %collective-permute-start.18 = (bf16[272,256]{1,0:T(8,128)(2,1)S(1)}, bf16[272,256]{1,0:T(8,128)(2,1)S(1)}, u32[]{:S(2)}, u32[]{:S(2)}) collective-permute-start(bf16[272,256]{1,0:T(8,128)(2,1)S(1)} %get-tuple-element.63), channel_id=1, source_target_pairs={{0,8},{4,12},{8,0},{12,4},{1,9},{5,13},{9,1},{13,5},{2,10},{6,14},... | collective-permute-start | bytes 417800 | tf_op jit(solution)/shard_map/ppermute | solution.py:423
  65.9 1.1 collective-permute-done.24.refs_0_
  67.0 1.5 %collective-permute-start.19 = (bf16[272,256]{1,0:T(8,128)(2,1)S(1)}, bf16[272,256]{1,0:T(8,128)(2,1)S(1)}, u32[]{:S(2)}, u32[]{:S(2)}) collective-permute-start(bf16[272,256]{1,0:T(8,128)(2,1)S(1)} %get-tuple-element.62), channel_id=1, source_target_pairs={{0,12},{4,8},{8,4},{12,0},{1,13},{5,9},{9,5},{13,1},{2,14},{6,10},... | collective-permute-start | bytes 417800 | tf_op jit(solution)/shard_map/ppermute | solution.py:423
  68.5 3.3 %collective-permute-done.25.refs_1_ = bf16[272,256]{1,0:T(8,128)(2,1)S(1)} collective-permute-done((bf16[272,256]{1,0:T(8,128)(2,1)S(1)}, bf16[272,256]{1,0:T(8,128)(2,1)S(1)}, u32[]{:S(2)}, u32[]{:S(2)}) %collective-permute-start.25) | collective-permute-done | bytes 139296 | tf_op jit(solution)/shard_map/ppermute | solution.py:423
  71.9 9.6 %collective-permute-start.27 = (bf16[272,256]{1,0:T(8,128)(2,1)S(1)}, bf16[272,256]{1,0:T(8,128)(2,1)S(1)}, u32[]{:S(2)}, u32[]{:S(2)}) collective-permute-start(bf16[272,256]{1,0:T(8,128)(2,1)S(1)} %shard_map.129), channel_id=1, source_target_pairs={{0,4},{4,0},{8,12},{12,8},{1,5},{5,1},{9,13},{13,9},{2,6},{6,2},{1... | collective-permute-start | bytes 417800 | tf_op jit(solution)/shard_map/ppermute | solution.py:430
  81.5 1.1 collective-permute-start.28
  82.6 1.4 %collective-permute-start.29 = (bf16[272,256]{1,0:T(8,128)(2,1)S(1)}, bf16[272,256]{1,0:T(8,128)(2,1)S(1)}, u32[]{:S(2)}, u32[]{:S(2)}) collective-permute-start(bf16[272,256]{1,0:T(8,128)(2,1)S(1)} %shard_map.129), channel_id=1, source_target_pairs={{0,12},{4,8},{8,4},{12,0},{1,13},{5,9},{9,5},{13,1},{2,14},{6,10},... | collective-permute-start | bytes 417800 | tf_op jit(solution)/shard_map/ppermute | solution.py:430
  84.0 8.5 %collective-permute-start.20 = (bf16[272,256]{1,0:T(8,128)(2,1)S(1)}, bf16[272,256]{1,0:T(8,128)(2,1)S(1)}, u32[]{:S(2)}, u32[]{:S(2)}) collective-permute-start(bf16[272,256]{1,0:T(8,128)(2,1)S(1)} %shard_map.128), channel_id=1, source_target_pairs={{0,4},{4,0},{8,12},{12,8},{1,5},{5,1},{9,13},{13,9},{2,6},{6,2},{1... | collective-permute-start | bytes 417800 | tf_op jit(solution)/shard_map/ppermute | solution.py:430
  92.5 2.0 %collective-permute-start.21 = (bf16[272,256]{1,0:T(8,128)(2,1)S(1)}, bf16[272,256]{1,0:T(8,128)(2,1)S(1)}, u32[]{:S(2)}, u32[]{:S(2)}) collective-permute-start(bf16[272,256]{1,0:T(8,128)(2,1)S(1)} %shard_map.128), channel_id=1, source_target_pairs={{0,8},{4,12},{8,0},{12,4},{1,9},{5,13},{9,1},{13,5},{2,10},{6,14},... | collective-permute-start | bytes 417800 | tf_op jit(solution)/shard_map/ppermute | solution.py:430
  94.5 1.4 %collective-permute-start.22 = (bf16[272,256]{1,0:T(8,128)(2,1)S(1)}, bf16[272,256]{1,0:T(8,128)(2,1)S(1)}, u32[]{:S(2)}, u32[]{:S(2)}) collective-permute-start(bf16[272,256]{1,0:T(8,128)(2,1)S(1)} %shard_map.128), channel_id=1, source_target_pairs={{0,12},{4,8},{8,4},{12,0},{1,13},{5,9},{9,5},{13,1},{2,14},{6,10},... | collective-permute-start | bytes 417800 | tf_op jit(solution)/shard_map/ppermute | solution.py:430
  96.0 2.3 %collective-permute-done.20 = bf16[272,256]{1,0:T(8,128)(2,1)S(1)} collective-permute-done((bf16[272,256]{1,0:T(8,128)(2,1)S(1)}, bf16[272,256]{1,0:T(8,128)(2,1)S(1)}, u32[]{:S(2)}, u32[]{:S(2)}) %collective-permute-start.20) | collective-permute-done | bytes 139296 | tf_op jit(solution)/shard_map/ppermute | solution.py:430
  98.4 9.4 %collective-permute-done.21 = bf16[272,256]{1,0:T(8,128)(2,1)S(1)} collective-permute-done((bf16[272,256]{1,0:T(8,128)(2,1)S(1)}, bf16[272,256]{1,0:T(8,128)(2,1)S(1)}, u32[]{:S(2)}, u32[]{:S(2)}) %collective-permute-start.21) | collective-permute-done | bytes 139296 | tf_op jit(solution)/shard_map/ppermute | solution.py:430
  108.1 1.4 %collective-permute-start.13 = (f32[8,256]{1,0:T(8,128)S(1)}, f32[8,256]{1,0:T(8,128)S(1)}, u32[]{:S(2)}, u32[]{:S(2)}) collective-permute-start(f32[8,256]{1,0:T(8,128)S(1)} %get-tuple-element.47.refs_0_), channel_id=1, source_target_pairs={{0,1},{1,0},{2,3},{3,2},{4,5},{5,4},{6,7},{7,6},{8,9},{9,8},{10,11... | collective-permute-start | bytes 24584 | tf_op jit(solution)/shard_map/ppermute | solution.py:404
  109.5 1.5 %collective-permute-start.14 = (f32[8,256]{1,0:T(8,128)S(1)}, f32[8,256]{1,0:T(8,128)S(1)}, u32[]{:S(2)}, u32[]{:S(2)}) collective-permute-start(f32[8,256]{1,0:T(8,128)S(1)} %get-tuple-element.47.refs_0_), channel_id=1, source_target_pairs={{0,2},{1,3},{2,0},{3,1},{4,6},{5,7},{6,4},{7,5},{8,10},{9,11},{10,... | collective-permute-start | bytes 24584 | tf_op jit(solution)/shard_map/ppermute | solution.py:404
  111.0 0.6 collective-permute-start.15
  111.8 1.3 %collective-permute-done.14.refs_2_ = f32[8,256]{1,0:T(8,128)S(1)} collective-permute-done((f32[8,256]{1,0:T(8,128)S(1)}, f32[8,256]{1,0:T(8,128)S(1)}, u32[]{:S(2)}, u32[]{:S(2)}) %collective-permute-start.14) | collective-permute-done | bytes 8224 | tf_op jit(solution)/shard_map/ppermute | solution.py:404
  113.1 2.4 %collective-permute-done.15.refs_3_ = f32[8,256]{1,0:T(8,128)S(1)} collective-permute-done((f32[8,256]{1,0:T(8,128)S(1)}, f32[8,256]{1,0:T(8,128)S(1)}, u32[]{:S(2)}, u32[]{:S(2)}) %collective-permute-start.15) | collective-permute-done | bytes 8224 | tf_op jit(solution)/shard_map/ppermute | solution.py:404
  115.6 1.6 %shard_map.127 = bf16[256,1024]{1,0:T(8,128)(2,1)} custom-call(s32[1]{0:T(128)} %bitcast.section_at, f32[256,1024]{1,0:T(8,128)S(1)} %get-tuple-element.46.part_ref, bf16[256,1024]{1,0:T(8,128)(2,1)S(1)} %get-tuple-element.28.refs_4_.x_ref.refs_8_, f32[256,128]{1,0:T(8,128)S(1)} %get-tuple-element.41.refs_16_.inv_ref.refs_20_, ...), custom_call_target="tpu_custom_call" | custom-call | flops 134217728 | bytes 2621440 | tf_op jit(solution)/shard_map/pallas_call | solution.py:608
  117.5 1.5 %slice_bitcast_fusion = (f32[1,4,256,256]{3,2,1,0:T(8,128)}, f32[1,4,256,256]{3,2,1,0:T(8,128)}) fusion(f32[4,272,256]{2,1,0:T(8,128)S(1)} %get-tuple-element.56, f32[4,272,256]{2,1,0:T(8,128)S(1)} %get-tuple-element.57), kind=kLoop, calls=%fused_computation.2 | loop fusion | bytes 4194304 | tf_op jit(solution)/shard_map/broadcast_in_dim | solution.py:622
  (62 shorter events, 5.6 us)
Async XLA Ops:
  0.6 10.5 %copy-start = (bf16[1,4,256,256]{3,2,1,0:T(8,128)(2,1)S(1)}, bf16[1,4,256,256]{3,2,1,0:T(8,128)(2,1)}, u32[]{:S(2)}) copy-start(bf16[1,4,256,256]{3,2,1,0:T(8,128)(2,1)} %param.11) | copy-start | bytes 1572868
  0.6 10.5 %copy-start.1 = (bf16[1,4,256,256]{3,2,1,0:T(8,128)(2,1)S(1)}, bf16[1,4,256,256]{3,2,1,0:T(8,128)(2,1)}, u32[]{:S(2)}) copy-start(bf16[1,4,256,256]{3,2,1,0:T(8,128)(2,1)} %param.12) | copy-start | bytes 1572868
  0.7 1.1 copy-start.2
  2.0 6.7 %collective-permute-start = (f32[8,256]{1,0:T(8,128)S(1)}, f32[8,256]{1,0:T(8,128)S(1)}, u32[]{:S(2)}, u32[]{:S(2)}) collective-permute-start(f32[8,256]{1,0:T(8,128)S(1)} %shard_map.120.refs_0_), channel_id=1, source_target_pairs={{0,1},{1,0},{2,3},{3,2},{4,5},{5,4},{6,7},{7,6},{8,9},{9,8},{10,11... | collective-permute-start | bytes 24584 | tf_op jit(solution)/shard_map/ppermute | solution.py:404
  5.0 3.8 %collective-permute-start.1 = (f32[8,256]{1,0:T(8,128)S(1)}, f32[8,256]{1,0:T(8,128)S(1)}, u32[]{:S(2)}, u32[]{:S(2)}) collective-permute-start(f32[8,256]{1,0:T(8,128)S(1)} %shard_map.120.refs_0_), channel_id=1, source_target_pairs={{0,2},{1,3},{2,0},{3,1},{4,6},{5,7},{6,4},{7,5},{8,10},{9,11},{10,... | collective-permute-start | bytes 24584 | tf_op jit(solution)/shard_map/ppermute | solution.py:404
  6.5 4.5 %collective-permute-start.2 = (f32[8,256]{1,0:T(8,128)S(1)}, f32[8,256]{1,0:T(8,128)S(1)}, u32[]{:S(2)}, u32[]{:S(2)}) collective-permute-start(f32[8,256]{1,0:T(8,128)S(1)} %shard_map.120.refs_0_), channel_id=1, source_target_pairs={{0,3},{1,2},{2,1},{3,0},{4,7},{5,6},{6,5},{7,4},{8,11},{9,10},{10,... | collective-permute-start | bytes 24584 | tf_op jit(solution)/shard_map/ppermute | solution.py:404
  7.3 1.0 copy-start.6
  8.8 21.1 %copy-start.8 = (f32[1,1024]{1,0:T(1,128)S(1)}, f32[1,1024]{1,0:T(1,128)}, u32[]{:S(2)}) copy-start(f32[1,1024]{1,0:T(1,128)} %refs_21_.1) | copy-start | bytes 12292
  11.1 0.7 copy-start.7
  11.8 0.7 copy-start.9
  12.5 0.7 copy-start.10
  13.2 0.7 copy-start.11
  19.6 4.5 %collective-permute-start.3 = (f32[12,1024]{1,0:T(8,128)S(1)}, f32[12,1024]{1,0:T(8,128)S(1)}, u32[]{:S(2)}, u32[]{:S(2)}) collective-permute-start(f32[12,1024]{1,0:T(8,128)S(1)} %get-tuple-element.30.refs_0_), channel_id=1, source_target_pairs={{0,4},{4,0},{8,12},{12,8},{1,5},{5,1},{9,13},{13,9},{2,6},{6,2},{1... | collective-permute-start | bytes 147464 | tf_op jit(solution)/shard_map/ppermute | solution.py:404
  21.2 6.6 %collective-permute-start.4 = (f32[12,1024]{1,0:T(8,128)S(1)}, f32[12,1024]{1,0:T(8,128)S(1)}, u32[]{:S(2)}, u32[]{:S(2)}) collective-permute-start(f32[12,1024]{1,0:T(8,128)S(1)} %get-tuple-element.30.refs_0_), channel_id=1, source_target_pairs={{0,8},{4,12},{8,0},{12,4},{1,9},{5,13},{9,1},{13,5},{2,10},{6,14},... | collective-permute-start | bytes 147464 | tf_op jit(solution)/shard_map/ppermute | solution.py:404
  23.8 6.1 %collective-permute-start.5 = (f32[12,1024]{1,0:T(8,128)S(1)}, f32[12,1024]{1,0:T(8,128)S(1)}, u32[]{:S(2)}, u32[]{:S(2)}) collective-permute-start(f32[12,1024]{1,0:T(8,128)S(1)} %get-tuple-element.30.refs_0_), channel_id=1, source_target_pairs={{0,12},{4,8},{8,4},{12,0},{1,13},{5,9},{9,5},{13,1},{2,14},{6,10},... | collective-permute-start | bytes 147464 | tf_op jit(solution)/shard_map/ppermute | solution.py:404
  34.8 6.2 %copy-start.3 = (bf16[4,272,256]{2,1,0:T(8,128)(2,1)}, bf16[4,272,256]{2,1,0:T(8,128)(2,1)S(1)}, u32[]{:S(2)}) copy-start(bf16[4,272,256]{2,1,0:T(8,128)(2,1)S(1)} %get-tuple-element.50) | copy-start | bytes 1671172
  34.8 3.7 %collective-permute-start.6 = (f32[8,256]{1,0:T(8,128)S(1)}, f32[8,256]{1,0:T(8,128)S(1)}, u32[]{:S(2)}, u32[]{:S(2)}) collective-permute-start(f32[8,256]{1,0:T(8,128)S(1)} %get-tuple-element.43.refs_0_), channel_id=1, source_target_pairs={{0,1},{1,0},{2,3},{3,2},{4,5},{5,4},{6,7},{7,6},{8,9},{9,8},{10,11... | collective-permute-start | bytes 24584 | tf_op jit(solution)/shard_map/ppermute | solution.py:404
  35.3 3.7 %collective-permute-start.7 = (f32[8,256]{1,0:T(8,128)S(1)}, f32[8,256]{1,0:T(8,128)S(1)}, u32[]{:S(2)}, u32[]{:S(2)}) collective-permute-start(f32[8,256]{1,0:T(8,128)S(1)} %get-tuple-element.43.refs_0_), channel_id=1, source_target_pairs={{0,2},{1,3},{2,0},{3,1},{4,6},{5,7},{6,4},{7,5},{8,10},{9,11},{10,... | collective-permute-start | bytes 24584 | tf_op jit(solution)/shard_map/ppermute | solution.py:404
  36.0 4.5 %collective-permute-start.8 = (f32[8,256]{1,0:T(8,128)S(1)}, f32[8,256]{1,0:T(8,128)S(1)}, u32[]{:S(2)}, u32[]{:S(2)}) collective-permute-start(f32[8,256]{1,0:T(8,128)S(1)} %get-tuple-element.43.refs_0_), channel_id=1, source_target_pairs={{0,3},{1,2},{2,1},{3,0},{4,7},{5,6},{6,5},{7,4},{8,11},{9,10},{10,... | collective-permute-start | bytes 24584 | tf_op jit(solution)/shard_map/ppermute | solution.py:404
  41.0 2.0 %collective-permute-start.9 = (bf16[256,1024]{1,0:T(8,128)(2,1)S(1)}, bf16[256,1024]{1,0:T(8,128)(2,1)S(1)}, u32[]{:S(2)}, u32[]{:S(2)}) collective-permute-start(bf16[256,1024]{1,0:T(8,128)(2,1)S(1)} %shard_map.124.early_ref), channel_id=1, source_target_pairs={{0,16},{16,0},{1,17},{17,1},{2,18},{18,2},{3,19},{19,3},{4,20},{20... | collective-permute-start | bytes 1572872 | tf_op jit(solution)/shard_map/ppermute | solution.py:409
  41.1 15.5 %collective-permute-start.23 = (bf16[4,272,256]{2,1,0:T(8,128)(2,1)}, bf16[4,272,256]{2,1,0:T(8,128)(2,1)}, u32[]{:S(2)}, u32[]{:S(2)}) collective-permute-start(bf16[4,272,256]{2,1,0:T(8,128)(2,1)} %get-tuple-element.51), channel_id=1, source_target_pairs={{0,16},{16,0},{1,17},{17,1},{2,18},{18,2},{3,19},{19,3},{4,20},{20... | collective-permute-start | bytes 1671176 | tf_op jit(solution)/shard_map/ppermute | solution.py:409
  43.8 4.5 %collective-permute-start.10 = (f32[4,1024]{1,0:T(4,128)S(1)}, f32[4,1024]{1,0:T(4,128)S(1)}, u32[]{:S(2)}, u32[]{:S(2)}) collective-permute-start(f32[4,1024]{1,0:T(4,128)S(1)} %get-tuple-element.44.refs_4_), channel_id=1, source_target_pairs={{0,4},{4,0},{8,12},{12,8},{1,5},{5,1},{9,13},{13,9},{2,6},{6,2},{1... | collective-permute-start | bytes 49160 | tf_op jit(solution)/shard_map/ppermute | solution.py:404
  43.8 4.7 %collective-permute-start.11 = (f32[4,1024]{1,0:T(4,128)S(1)}, f32[4,1024]{1,0:T(4,128)S(1)}, u32[]{:S(2)}, u32[]{:S(2)}) collective-permute-start(f32[4,1024]{1,0:T(4,128)S(1)} %get-tuple-element.44.refs_4_), channel_id=1, source_target_pairs={{0,8},{4,12},{8,0},{12,4},{1,9},{5,13},{9,1},{13,5},{2,10},{6,14},... | collective-permute-start | bytes 49160 | tf_op jit(solution)/shard_map/ppermute | solution.py:404
  45.3 5.5 %collective-permute-start.12 = (f32[4,1024]{1,0:T(4,128)S(1)}, f32[4,1024]{1,0:T(4,128)S(1)}, u32[]{:S(2)}, u32[]{:S(2)}) collective-permute-start(f32[4,1024]{1,0:T(4,128)S(1)} %get-tuple-element.44.refs_4_), channel_id=1, source_target_pairs={{0,12},{4,8},{8,4},{12,0},{1,13},{5,9},{9,5},{13,1},{2,14},{6,10},... | collective-permute-start | bytes 49160 | tf_op jit(solution)/shard_map/ppermute | solution.py:404
  55.8 0.8 copy-start.4
  56.6 5.7 %collective-permute-start.16 = (bf16[4,272,256]{2,1,0:T(8,128)(2,1)}, bf16[4,272,256]{2,1,0:T(8,128)(2,1)S(1)}, u32[]{:S(2)}, u32[]{:S(2)}) collective-permute-start(bf16[4,272,256]{2,1,0:T(8,128)(2,1)} %get-tuple-element.48), channel_id=1, source_target_pairs={{0,16},{16,0},{1,17},{17,1},{2,18},{18,2},{3,19},{19,3},{4,20},{20... | collective-permute-start | bytes 1671176 | tf_op jit(solution)/shard_map/ppermute | solution.py:409
  56.6 5.7 %copy-start.5 = (bf16[4,272,256]{2,1,0:T(8,128)(2,1)S(1)}, bf16[4,272,256]{2,1,0:T(8,128)(2,1)}, u32[]{:S(2)}) copy-start(bf16[4,272,256]{2,1,0:T(8,128)(2,1)} %copy-done.4) | copy-start | bytes 1671172
  57.8 9.2 %collective-permute-start.24 = (bf16[272,256]{1,0:T(8,128)(2,1)S(1)}, bf16[272,256]{1,0:T(8,128)(2,1)S(1)}, u32[]{:S(2)}, u32[]{:S(2)}) collective-permute-start(bf16[272,256]{1,0:T(8,128)(2,1)S(1)} %get-tuple-element.72), channel_id=1, source_target_pairs={{0,4},{4,0},{8,12},{12,8},{1,5},{5,1},{9,13},{13,9},{2,6},{6,2},{1... | collective-permute-start | bytes 417800 | tf_op jit(solution)/shard_map/ppermute | solution.py:423
  57.9 13.9 %collective-permute-start.25 = (bf16[272,256]{1,0:T(8,128)(2,1)S(1)}, bf16[272,256]{1,0:T(8,128)(2,1)S(1)}, u32[]{:S(2)}, u32[]{:S(2)}) collective-permute-start(bf16[272,256]{1,0:T(8,128)(2,1)S(1)} %get-tuple-element.71), channel_id=1, source_target_pairs={{0,8},{4,12},{8,0},{12,4},{1,9},{5,13},{9,1},{13,5},{2,10},{6,14},... | collective-permute-start | bytes 417800 | tf_op jit(solution)/shard_map/ppermute | solution.py:423
  61.3 10.5 %collective-permute-start.26 = (bf16[272,256]{1,0:T(8,128)(2,1)S(1)}, bf16[272,256]{1,0:T(8,128)(2,1)S(1)}, u32[]{:S(2)}, u32[]{:S(2)}) collective-permute-start(bf16[272,256]{1,0:T(8,128)(2,1)S(1)} %get-tuple-element.70), channel_id=1, source_target_pairs={{0,12},{4,8},{8,4},{12,0},{1,13},{5,9},{9,5},{13,1},{2,14},{6,10},... | collective-permute-start | bytes 417800 | tf_op jit(solution)/shard_map/ppermute | solution.py:423
  62.4 20.1 %collective-permute-start.17 = (bf16[272,256]{1,0:T(8,128)(2,1)S(1)}, bf16[272,256]{1,0:T(8,128)(2,1)S(1)}, u32[]{:S(2)}, u32[]{:S(2)}) collective-permute-start(bf16[272,256]{1,0:T(8,128)(2,1)S(1)} %get-tuple-element.64), channel_id=1, source_target_pairs={{0,4},{4,0},{8,12},{12,8},{1,5},{5,1},{9,13},{13,9},{2,6},{6,2},{1... | collective-permute-start | bytes 417800 | tf_op jit(solution)/shard_map/ppermute | solution.py:423
  62.5 21.5 %collective-permute-start.18 = (bf16[272,256]{1,0:T(8,128)(2,1)S(1)}, bf16[272,256]{1,0:T(8,128)(2,1)S(1)}, u32[]{:S(2)}, u32[]{:S(2)}) collective-permute-start(bf16[272,256]{1,0:T(8,128)(2,1)S(1)} %get-tuple-element.63), channel_id=1, source_target_pairs={{0,8},{4,12},{8,0},{12,4},{1,9},{5,13},{9,1},{13,5},{2,10},{6,14},... | collective-permute-start | bytes 417800 | tf_op jit(solution)/shard_map/ppermute | solution.py:423
  67.0 16.9 %collective-permute-start.19 = (bf16[272,256]{1,0:T(8,128)(2,1)S(1)}, bf16[272,256]{1,0:T(8,128)(2,1)S(1)}, u32[]{:S(2)}, u32[]{:S(2)}) collective-permute-start(bf16[272,256]{1,0:T(8,128)(2,1)S(1)} %get-tuple-element.62), channel_id=1, source_target_pairs={{0,12},{4,8},{8,4},{12,0},{1,13},{5,9},{9,5},{13,1},{2,14},{6,10},... | collective-permute-start | bytes 417800 | tf_op jit(solution)/shard_map/ppermute | solution.py:423
  71.9 22.6 %collective-permute-start.27 = (bf16[272,256]{1,0:T(8,128)(2,1)S(1)}, bf16[272,256]{1,0:T(8,128)(2,1)S(1)}, u32[]{:S(2)}, u32[]{:S(2)}) collective-permute-start(bf16[272,256]{1,0:T(8,128)(2,1)S(1)} %shard_map.129), channel_id=1, source_target_pairs={{0,4},{4,0},{8,12},{12,8},{1,5},{5,1},{9,13},{13,9},{2,6},{6,2},{1... | collective-permute-start | bytes 417800 | tf_op jit(solution)/shard_map/ppermute | solution.py:430
  81.5 14.4 %collective-permute-start.28 = (bf16[272,256]{1,0:T(8,128)(2,1)S(1)}, bf16[272,256]{1,0:T(8,128)(2,1)S(1)}, u32[]{:S(2)}, u32[]{:S(2)}) collective-permute-start(bf16[272,256]{1,0:T(8,128)(2,1)S(1)} %shard_map.129), channel_id=1, source_target_pairs={{0,8},{4,12},{8,0},{12,4},{1,9},{5,13},{9,1},{13,5},{2,10},{6,14},... | collective-permute-start | bytes 417800 | tf_op jit(solution)/shard_map/ppermute | solution.py:430
  82.6 13.3 %collective-permute-start.29 = (bf16[272,256]{1,0:T(8,128)(2,1)S(1)}, bf16[272,256]{1,0:T(8,128)(2,1)S(1)}, u32[]{:S(2)}, u32[]{:S(2)}) collective-permute-start(bf16[272,256]{1,0:T(8,128)(2,1)S(1)} %shard_map.129), channel_id=1, source_target_pairs={{0,12},{4,8},{8,4},{12,0},{1,13},{5,9},{9,5},{13,1},{2,14},{6,10},... | collective-permute-start | bytes 417800 | tf_op jit(solution)/shard_map/ppermute | solution.py:430
  84.0 14.3 %collective-permute-start.20 = (bf16[272,256]{1,0:T(8,128)(2,1)S(1)}, bf16[272,256]{1,0:T(8,128)(2,1)S(1)}, u32[]{:S(2)}, u32[]{:S(2)}) collective-permute-start(bf16[272,256]{1,0:T(8,128)(2,1)S(1)} %shard_map.128), channel_id=1, source_target_pairs={{0,4},{4,0},{8,12},{12,8},{1,5},{5,1},{9,13},{13,9},{2,6},{6,2},{1... | collective-permute-start | bytes 417800 | tf_op jit(solution)/shard_map/ppermute | solution.py:430
  92.5 15.2 %collective-permute-start.21 = (bf16[272,256]{1,0:T(8,128)(2,1)S(1)}, bf16[272,256]{1,0:T(8,128)(2,1)S(1)}, u32[]{:S(2)}, u32[]{:S(2)}) collective-permute-start(bf16[272,256]{1,0:T(8,128)(2,1)S(1)} %shard_map.128), channel_id=1, source_target_pairs={{0,8},{4,12},{8,0},{12,4},{1,9},{5,13},{9,1},{13,5},{2,10},{6,14},... | collective-permute-start | bytes 417800 | tf_op jit(solution)/shard_map/ppermute | solution.py:430
  94.5 13.2 %collective-permute-start.22 = (bf16[272,256]{1,0:T(8,128)(2,1)S(1)}, bf16[272,256]{1,0:T(8,128)(2,1)S(1)}, u32[]{:S(2)}, u32[]{:S(2)}) collective-permute-start(bf16[272,256]{1,0:T(8,128)(2,1)S(1)} %shard_map.128), channel_id=1, source_target_pairs={{0,12},{4,8},{8,4},{12,0},{1,13},{5,9},{9,5},{13,1},{2,14},{6,10},... | collective-permute-start | bytes 417800 | tf_op jit(solution)/shard_map/ppermute | solution.py:430
  108.0 9.1 %collective-permute-start.30 = (bf16[4,272,256]{2,1,0:T(8,128)(2,1)S(1)}, bf16[4,272,256]{2,1,0:T(8,128)(2,1)S(1)}, u32[]{:S(2)}, u32[]{:S(2)}) collective-permute-start(bf16[4,272,256]{2,1,0:T(8,128)(2,1)S(1)} %broadcast_select_fusion.1), channel_id=1, source_target_pairs={{0,16},{16,0},{1,17},{17,1},{2,18},{18,2},{3,19},{19,3},{4,20},{20... | collective-permute-start | bytes 1671176 | tf_op jit(solution)/shard_map/ppermute | solution.py:409
  108.1 3.7 %collective-permute-start.13 = (f32[8,256]{1,0:T(8,128)S(1)}, f32[8,256]{1,0:T(8,128)S(1)}, u32[]{:S(2)}, u32[]{:S(2)}) collective-permute-start(f32[8,256]{1,0:T(8,128)S(1)} %get-tuple-element.47.refs_0_), channel_id=1, source_target_pairs={{0,1},{1,0},{2,3},{3,2},{4,5},{5,4},{6,7},{7,6},{8,9},{9,8},{10,11... | collective-permute-start | bytes 24584 | tf_op jit(solution)/shard_map/ppermute | solution.py:404
  109.5 3.7 %collective-permute-start.14 = (f32[8,256]{1,0:T(8,128)S(1)}, f32[8,256]{1,0:T(8,128)S(1)}, u32[]{:S(2)}, u32[]{:S(2)}) collective-permute-start(f32[8,256]{1,0:T(8,128)S(1)} %get-tuple-element.47.refs_0_), channel_id=1, source_target_pairs={{0,2},{1,3},{2,0},{3,1},{4,6},{5,7},{6,4},{7,5},{8,10},{9,11},{10,... | collective-permute-start | bytes 24584 | tf_op jit(solution)/shard_map/ppermute | solution.py:404
  111.0 4.5 %collective-permute-start.15 = (f32[8,256]{1,0:T(8,128)S(1)}, f32[8,256]{1,0:T(8,128)S(1)}, u32[]{:S(2)}, u32[]{:S(2)}) collective-permute-start(f32[8,256]{1,0:T(8,128)S(1)} %get-tuple-element.47.refs_0_), channel_id=1, source_target_pairs={{0,3},{1,2},{2,1},{3,0},{4,7},{5,6},{6,5},{7,4},{8,11},{9,10},{10,... | collective-permute-start | bytes 24584 | tf_op jit(solution)/shard_map/ppermute | solution.py:404

commit v2 on v0

v2 whole, which is shorter than its diff:
```python
import functools
import math

import jax
import jax.numpy as jnp
from jax import lax
from jax.experimental import pallas as pl
from jax.experimental.pallas import tpu as pltpu
from jax.sharding import PartitionSpec as P

F32 = jnp.float32
BF16 = jnp.bfloat16
HIGH = lax.Precision.HIGHEST
VECTOR_ROWS = 16
DIRECT_RANKS = 4


def params(limit=8):
    return pltpu.CompilerParams(vmem_limit_bytes=limit * 1024 * 1024)


def cost(flops, size):
    return pl.CostEstimate(flops=flops, bytes_accessed=size, transcendentals=0)


def contract(a, b, dims, precision=None):
    return lax.dot_general(
        a, b, ((dims[:1], dims[1:]), ((), ())), precision=precision, preferred_element_type=F32
    )


def row_order(rows, tok_rows):
    shift = tok_rows.bit_length() - 1
    at = lax.broadcasted_iota(jnp.int32, (rows, rows), 0)
    source = lax.broadcasted_iota(jnp.int32, (rows, rows), 1)
    inner = jnp.bitwise_and(at, tok_rows - 1)
    wanted = (
        jnp.left_shift(jnp.right_shift(at, shift), shift)
        + jnp.bitwise_and(inner, 7) * (tok_rows // 8)
        + jnp.right_shift(inner, 3)
    )
    return jnp.where(wanted == source, 1.0, 0.0).astype(F32)


def to_column(parts):
    total = parts[0]
    for part in parts[1:]:
        total = total + part
    return contract(total, jnp.full((8, 128), 0.125, F32), (0, 0), HIGH)


def to_row(folded):
    return contract(jnp.ones((8, folded.shape[1]), F32), folded, (1, 1), HIGH)


def fold_lanes(value):
    total = value[:, :128]
    for at in range(128, value.shape[1], 128):
        total = total + value[:, at : at + 128]
    return total


def widen(column, width):
    return jnp.concatenate([column] * (width // 128), axis=1)


def prepare_kernel(
    micro_count, tok_rows, section_at, seq_at, raw_starts, raw_x_ref, up_ref, rw_ref, iw_ref,
    rb_ref, ib_ref, dp_ref, gain_ref, square_ref, xk_ref, xs_ref, upp_ref, wk_ref, ws_ref,
    vk_ref, vs_ref, open_ref, starts, x_ref, raw_up_ref, raw_ref, sems,
):
    half = x_ref.shape[1] // 2
    heads = rw_ref.shape[0] // 2
    section = section_at[0]

    def columns(side):
        return pl.ds(pl.multiple_of(side * half, 128), half)

    moves = [(raw_x_ref, x_ref), (raw_starts, starts), (up_ref.at[:, columns(section)], raw_up_ref)]
    moves += [
        (source, raw_ref.at[k]) for k, source in enumerate((rb_ref, ib_ref, dp_ref, gain_ref))
    ]
    for side, w_out in ((section, wk_ref), (1 - section, ws_ref)):
        picked = pl.ds(side * heads, heads)
        moves += [
            (rw_ref.at[picked], w_out.at[pl.ds(0, heads)]),
            (iw_ref.at[picked], w_out.at[pl.ds(heads, heads)]),
        ]
    copies = [
        pltpu.make_async_copy(source, target, sems.at[k])
        for k, (source, target) in enumerate(moves)
    ]
    for copy in copies:
        copy.start()
    order = row_order(x_ref.shape[0], tok_rows).astype(BF16)
    copies[0].wait()
    total = None
    for side, x_out in ((section, xk_ref), (1 - section, xs_ref)):
        x = contract(order, x_ref[:, columns(side)], (1, 0))
        x_out[...] = x.astype(BF16)
        part = fold_lanes(x * x)
        total = part if total is None else total + part
    square_ref[...] = to_row(total)
    for copy in copies[1:]:
        copy.wait()
    upp_ref[...] = contract(order, raw_up_ref[...], (1, 0)).astype(BF16)
    for side, v_out in ((section, vk_ref), (1 - section, vs_ref)):
        rate_bias, input_bias, decay_param, gain = (
            raw_ref[k, :, columns(side)] for k in range(4)
        )
        slow = -decay_param
        soft = jnp.maximum(slow, 0.0) + jnp.log1p(jnp.exp(-jnp.abs(slow)))
        v_out[...] = jnp.concatenate(
            [rate_bias, input_bias, -8.0 * soft, gain, jnp.zeros((4, half), F32)], axis=0
        )
    shift = tok_rows.bit_length() - 1
    at = lax.broadcasted_iota(jnp.int32, open_ref.shape, 0)
    inner = jnp.bitwise_and(at, tok_rows - 1)
    micro = jnp.right_shift(at, shift)
    position = (
        seq_at[0] * tok_rows
        + jnp.bitwise_and(inner, 7) * (tok_rows // 8)
        + jnp.right_shift(inner, 3)
    )
    reset = position == 0
    for m in range(micro_count):
        for d in range(starts.shape[1]):
            hit = jnp.logical_and(micro == m, position == starts[m : m + 1, d : d + 1])
            reset = jnp.logical_or(reset, hit)
    open_ref[...] = jnp.where(reset, 0.0, 1.0)


def sublane_scan(decay, value, reverse):
    at = lax.broadcasted_iota(jnp.int32, decay.shape, 0)
    for step in (1, 2, 4):
        shift = 8 - step if reverse else step
        inside = at < 8 - step if reverse else at >= step
        value_far = pltpu.roll(value, shift, 0)
        decay_far = pltpu.roll(decay, shift, 0)
        value = jnp.where(inside, value + decay * value_far, value)
        decay = jnp.where(inside, decay * decay_far, decay)
    return decay, value


def reverse_blocks(decay_ref, up_ref, base, cols, tok_rows, width):
    carry = jnp.zeros((8, width), F32)
    for pair in reversed(range(tok_rows // 16)):
        rows = pl.ds(base + 16 * pair, 16)
        decay = decay_ref[rows, cols]
        upstream = up_ref[rows, cols].astype(F32)
        carry = decay[8:] * (upstream[8:] + carry)
        carry = decay[:8] * (upstream[:8] + carry)
    return carry


def send_rows(rank, ahead, behind, near_ref, far_ref):
    near_ref[...] = jnp.where(jnp.bitwise_and(rank, 1) == 0, ahead, behind)
    far_ref[...] = jnp.where(jnp.bitwise_and(rank, 2) == 0, ahead, behind)


def head_columns(head, width):
    return pl.ds(pl.multiple_of(head * width, width), width)


def forward_kernel(micro_count, tok_rows, full_width, layer, square_count, seq_at, section_at, *refs):
    own_squares, other_squares = refs[:square_count], refs[square_count]
    refs = refs[square_count + 1 :]
    open_ref, xk_ref, xr_ref, wk_ref, wr_ref, vk_ref, vr_ref = refs[:7]
    refs = refs[7:]
    if layer:
        up_ref, *refs = refs
    else:
        _above, *refs = refs
    normed_ref, factor_ref, block_ref, ahead_ref, inv_ref, *refs = refs
    decay_ref, p1_ref, p2_ref, p3_ref, p4_ref = (factor_ref.at[k] for k in range(5))
    fdecay_ref, fstate_ref, rdecay_ref = (block_ref.at[k] for k in range(3))
    if layer:
        rgrad_ref, behind_ref, near_ref, far_ref, *refs = refs
    prer_ref, prei_ref = refs
    width = wk_ref.shape[2]
    heads = xk_ref.shape[1] // width
    own = section_at[0] == layer

    total = jnp.where(own, sum(part[...] for part in own_squares), other_squares[...])
    inv_ref[...] = lax.rsqrt(to_column([total]) / full_width + 1e-06)

    def per_head(head, _):
        cols = head_columns(head, width)
        vectors = jnp.where(own, vk_ref[:, cols], vr_ref[:, cols])
        rate_scale, gain = vectors[2:3], vectors[3:4]
        x = jnp.where(own, xk_ref[:, cols], xr_ref[:, cols])
        normed = (x.astype(F32) * widen(inv_ref[...], width) * gain).astype(BF16)
        normed_ref[:, cols] = normed
        rate_weight = jnp.where(own, wk_ref[head], wr_ref[head])
        input_weight = jnp.where(own, wk_ref[heads + head], wr_ref[heads + head])
        prer_ref[...] = contract(normed, rate_weight, (1, 0)) + vectors[0:1]
        prei_ref[...] = contract(normed, input_weight, (1, 0)) + vectors[1:2]

        def per_micro(m, _):
            base = pl.multiple_of(m * tok_rows, tok_rows)
            state = jnp.zeros((8, width), F32)
            product = jnp.ones((8, width), F32)
            for pair in range(tok_rows // 16):
                rows = pl.ds(base + 16 * pair, 16)
                x_norm = normed_ref[rows, cols].astype(F32)
                keep = widen(open_ref[rows, :], width)
                rate_gate = 1.0 / (1.0 + jnp.exp(-prer_ref[rows, :]))
                input_gate = 1.0 / (1.0 + jnp.exp(-prei_ref[rows, :]))
                log_decay = rate_gate * rate_scale
                decay = jnp.exp(log_decay)
                square_gap = decay * decay
                twice = 2.0 * log_decay
                small = -twice * (
                    1.0 + twice * (1 / 2 + twice * (1 / 6 + twice * (1 / 24 + twice * (1 / 120))))
                )
                gap = jnp.where(twice > -0.1, small, 1.0 - square_gap)
                gap = jnp.maximum(gap, 1e-06)
                inv_mult = lax.rsqrt(gap)
                multiplier = jnp.where(keep > 0.0, gap * inv_mult, 1.0)
                decay_eff = decay * keep
                rate_slope = rate_scale * rate_gate * (1.0 - rate_gate)
                gated = input_gate * x_norm
                passed = multiplier * input_gate
                drive = passed * x_norm
                decay_ref[rows, cols] = decay_eff
                p1_ref[rows, cols] = decay_eff * rate_slope
                p2_ref[rows, cols] = keep * gated * square_gap * inv_mult * rate_slope
                p3_ref[rows, cols] = drive * (1.0 - input_gate)
                p4_ref[rows, cols] = passed
                for part in (slice(0, 8), slice(8, 16)):
                    state = decay_eff[part] * state + drive[part]
                    product = decay_eff[part] * product
            fdecay, fstate = sublane_scan(product, state, False)
            block_rows = pl.ds(pl.multiple_of(m * 8, 8), 8)
            fdecay_ref[block_rows, cols] = fdecay
            fstate_ref[block_rows, cols] = fstate
            ahead_ref[pl.ds(m, 1), cols] = fdecay[7:8]
            ahead_ref[pl.ds(micro_count + m, 1), cols] = fstate[7:8]
            if layer:
                leaving = reverse_blocks(decay_ref, up_ref, base, cols, tok_rows, width)
                rdecay, rgrad = sublane_scan(product, leaving, True)
                rgrad_ref[block_rows, cols] = rgrad
                behind_ref[pl.ds(m, 1), cols] = fdecay[7:8]
                behind_ref[pl.ds(micro_count + m, 1), cols] = rgrad[0:1]
            else:
                rdecay, _unused = sublane_scan(product, product, True)
            rdecay_ref[block_rows, cols] = rdecay
            return 0

        lax.fori_loop(0, micro_count, per_micro, 0)
        return 0

    lax.fori_loop(0, heads, per_head, 0)
    if layer:
        send_rows(seq_at[0], ahead_ref[...], behind_ref[...], near_ref, far_ref)


def late_kernel(
    micro_count, tok_rows, full_width, cross_count, seq_at, section_at, part_ref, xk_ref, xr_ref,
    inv_ref, factor_ref, ahead_ref, *refs
):
    crosses = refs[:cross_count]
    early_ref, rgrad_ref, behind_ref, near_ref, far_ref, scale_ref = refs[cross_count:]
    decay_ref = factor_ref.at[0]
    width = 256
    column = to_column([part[...] for part in crosses]) / full_width
    inv = inv_ref[...]
    scale_ref[...] = inv * inv * inv * column
    own = section_at[0] == 1

    def per_head(head, _):
        cols = head_columns(head, width)

        def per_micro(m, _):
            base = pl.multiple_of(m * tok_rows, tok_rows)
            carry = jnp.zeros((8, width), F32)
            product = jnp.ones((8, width), F32)
            for pair in reversed(range(tok_rows // 16)):
                rows = pl.ds(base + 16 * pair, 16)
                decay = decay_ref[rows, cols]
                x = jnp.where(own, xk_ref[rows, cols], xr_ref[rows, cols]).astype(F32)
                scale = widen(scale_ref[rows, :], width)
                early = (part_ref[rows, cols] - x * scale).astype(BF16)
                early_ref[rows, cols] = early
                upstream = early.astype(F32)
                carry = decay[8:] * (upstream[8:] + carry)
                carry = decay[:8] * (upstream[:8] + carry)
                product = product * decay[8:] * decay[:8]
            _, rgrad = sublane_scan(product, carry, True)
            rgrad_ref[pl.ds(pl.multiple_of(m * 8, 8), 8), cols] = rgrad
            behind_ref[pl.ds(m, 1), cols] = ahead_ref[pl.ds(m, 1), cols]
            behind_ref[pl.ds(micro_count + m, 1), cols] = rgrad[0:1]
            return 0

        lax.fori_loop(0, micro_count, per_micro, 0)
        return 0

    lax.fori_loop(0, part_ref.shape[1] // width, per_head, 0)
    send_rows(seq_at[0], ahead_ref[...], behind_ref[...], near_ref, far_ref)


def ranked(refs, rank, at):
    if len(refs) == 1:
        return refs[0][at]
    chosen = refs[0][...]
    for k in range(2, len(refs) + 1):
        chosen = jnp.where(jnp.bitwise_xor(rank, at) == k, refs[k - 1][...], chosen)
    return chosen


def backward_kernel(
    micro_count, tok_rows, seq_count, layer, direct, pay_count, seq_at, section_at, *refs
):
    pays = refs[:pay_count]
    (
        xk_ref, xr_ref, up_ref, normed_ref, factor_ref, block_ref, rgrad_ref, inv_ref,
        vk_ref, vr_ref, wk_ref, wr_ref, _before,
        part_ref, cross_ref, *unit_refs,
        enter_ref, leave_ref, slope_ref, direct_ref, gr_ref, gi_ref, fold_ref, weight_ref,
    ) = refs[pay_count:]
    decay_ref, p1_ref, p2_ref, p3_ref, p4_ref = (factor_ref.at[k] for k in range(5))
    fdecay_ref, fstate_ref, rdecay_ref = (block_ref.at[k] for k in range(3))
    width = wk_ref.shape[2]
    heads = xk_ref.shape[1] // width
    rank = seq_at[0]
    micro = micro_count
    own = section_at[0] == layer
    behind = 2 * micro if pay_count == 1 else 0

    state_in = jnp.zeros(enter_ref.shape, F32)
    grad_in = jnp.zeros(leave_ref.shape, F32)
    for at in range(seq_count - 1):
        pay = ranked(pays, rank, at)
        state_in = jnp.where(
            at < rank, pay[micro : 2 * micro] + pay[:micro] * state_in, state_in
        )
    for at in reversed(range(1, seq_count)):
        pay = ranked(pays, rank, at)[behind:]
        grad_in = jnp.where(
            at > rank, pay[micro : 2 * micro] + pay[:micro] * grad_in, grad_in
        )
    enter_ref[...] = state_in
    leave_ref[...] = grad_in
    fold_ref[...] = jnp.zeros(fold_ref.shape, F32)

    sub = lax.broadcasted_iota(jnp.int32, (8, width), 0)
    zero = jnp.zeros((8, width), F32)

    def per_head(head, _):
        cols = head_columns(head, width)

        def per_micro(m, sums):
            sum_rate, sum_input = sums
            base = pl.multiple_of(m * tok_rows, tok_rows)
            block_rows = pl.ds(pl.multiple_of(m * 8, 8), 8)
            enter = enter_ref[pl.ds(m, 1), cols]
            leave = leave_ref[pl.ds(m, 1), cols]
            after = fstate_ref[block_rows, cols] + fdecay_ref[block_rows, cols] * enter
            state = jnp.where(sub == 0, enter, pltpu.roll(after, 1, 0))
            before = rgrad_ref[block_rows, cols] + rdecay_ref[block_rows, cols] * leave
            carry = jnp.where(sub == 7, leave, pltpu.roll(before, 7, 0))
            for pair in range(tok_rows // 16):
                rows = pl.ds(base + 16 * pair, 16)
                decay = decay_ref[rows, cols]
                drive = p4_ref[rows, cols] * normed_ref[rows, cols].astype(F32)
                middle = decay[:8] * state + drive[:8]
                previous = jnp.concatenate([state, middle], axis=0)
                state = decay[8:] * middle + drive[8:]
                slope_ref[pl.ds(16 * pair, 16), :] = (
                    previous * p1_ref[rows, cols] - p2_ref[rows, cols]
                )
            for pair in reversed(range(tok_rows // 16)):
                rows = pl.ds(base + 16 * pair, 16)
                decay = decay_ref[rows, cols]
                upstream = up_ref[rows, cols].astype(F32)
                late = upstream[8:] + carry
                early = upstream[:8] + decay[8:] * late
                carry = decay[:8] * early
                grad = jnp.concatenate([early, late], axis=0)
                grad_rate = (grad * slope_ref[pl.ds(16 * pair, 16), :]).astype(BF16)
                grad_input = (grad * p3_ref[rows, cols]).astype(BF16)
                gr_ref[rows, :] = grad_rate
                gi_ref[rows, :] = grad_input
                direct_ref[rows, :] = grad * p4_ref[rows, cols]
                wide_rate = grad_rate.astype(F32)
                wide_input = grad_input.astype(F32)
                sum_rate = sum_rate + wide_rate[:8] + wide_rate[8:]
                sum_input = sum_input + wide_input[:8] + wide_input[8:]
            return sum_rate, sum_input

        sum_rate, sum_input = lax.fori_loop(0, micro, per_micro, (zero, zero))

        normed = normed_ref[:, cols]
        places = [jnp.bitwise_xor(2 * head + gate, rank if direct else 0) for gate in range(2)]
        for place, grad_ref in zip(places, (gr_ref, gi_ref)):
            unit_ref = weight_ref.at[place]
            unit_ref[:width, :] = contract(normed, grad_ref[...], (0, 0)).astype(BF16)
        rate_weight = jnp.where(own, wk_ref[head], wr_ref[head])
        input_weight = jnp.where(own, wk_ref[heads + head], wr_ref[heads + head])
        direct_ref[...] += contract(gr_ref[...], rate_weight, (1, 1)) + contract(
            gi_ref[...], input_weight, (1, 1)
        )
        gain = jnp.where(own, vk_ref[3:4, cols], vr_ref[3:4, cols])

        def per_part(m, sum_gain):
            rows = pl.ds(pl.multiple_of(m * tok_rows, tok_rows), tok_rows)
            inv = widen(inv_ref[rows, :], width)
            x = jnp.where(own, xk_ref[rows, cols], xr_ref[rows, cols]).astype(F32)
            grad_normed = direct_ref[rows, :]
            scaled = grad_normed * gain
            part_ref[rows, cols] = up_ref[rows, cols].astype(F32) + inv * scaled
            weighted = grad_normed * x * inv
            fold_ref[rows, :] += fold_lanes(x * scaled)
            for at in range(0, tok_rows, 8):
                sum_gain = sum_gain + weighted[at : at + 8]
            return sum_gain

        sum_gain = lax.fori_loop(0, micro, per_part, zero)
        vector = jnp.concatenate(
            [
                jnp.sum(sum_rate, axis=0, keepdims=True),
                jnp.sum(sum_input, axis=0, keepdims=True),
                jnp.sum(sum_gain, axis=0, keepdims=True),
                jnp.zeros((VECTOR_ROWS - 3, width), F32),
            ],
            axis=0,
        )
        high = vector.astype(BF16)
        weight_ref[places[0], width:, :] = high
        weight_ref[places[1], width:, :] = (vector - high.astype(F32)).astype(BF16)
        return 0

    lax.fori_loop(0, heads, per_head, 0)
    cross_ref[...] = to_row(fold_ref[...])
    if not direct:
        unit_refs[0][...] = weight_ref[...]
    elif layer:
        keep_ref, send_ref = unit_refs
        for k in range(4):
            (send_ref if k % 2 else keep_ref)[k // 2] = weight_ref[k]
    else:
        for k, unit_ref in enumerate(unit_refs):
            unit_ref[...] = weight_ref[k]


def last_kernel(
    full_width, tok_rows, cross_count, section_at, part_ref, xk_ref, xr_ref, inv_ref, early_ref,
    *refs
):
    column = to_column([part[...] for part in refs[:cross_count]]) / full_width
    keep_ref, send_ref = refs[cross_count:]
    inv = inv_ref[...]
    scale = inv * inv * inv * column
    order = row_order(xk_ref.shape[0], tok_rows).astype(BF16)
    bottom = section_at[0] == 0
    for at in range(0, xk_ref.shape[1], 256):
        cols = slice(at, at + 256)
        x = jnp.where(bottom, xk_ref[:, cols], xr_ref[:, cols]).astype(F32)
        value = (part_ref[:, cols] - x * widen(scale, 256)).astype(BF16)
        early = early_ref[:, cols]
        keep_ref[:, cols] = contract(order, jnp.where(bottom, value, early), (0, 0)).astype(BF16)
        send_ref[:, cols] = contract(order, jnp.where(bottom, early, value), (0, 0)).astype(BF16)


def join_kernel(section_at, keep_ref, arrived_ref, out_ref):
    half = keep_ref.shape[1]
    mine = section_at[0] * half
    out_ref[:, pl.ds(pl.multiple_of(mine, 128), half)] = keep_ref[...]
    out_ref[:, pl.ds(pl.multiple_of(half - mine, 128), half)] = arrived_ref[...]


def add_kernel(*refs):
    total = refs[0][...].astype(F32)
    for part in refs[1:-1]:
        total = total + part[...].astype(F32)
    refs[-1][...] = total.astype(refs[-1].dtype)


def add_pairs_kernel(a_ref, b_ref, *outs):
    for k, out_ref in enumerate(outs):
        out_ref[...] = (a_ref[k].astype(F32) + b_ref[k].astype(F32)).astype(out_ref.dtype)


def weights_kernel(units, scale, section_at, unit_at, *refs):
    tops, lows, others = refs[:units], refs[units : 2 * units], refs[2 * units : 3 * units]
    rate_ref, input_ref, vector_ref = refs[3 * units :]
    head = pl.program_id(0)
    size = rate_ref.shape[1]
    half_heads = units // 2
    section = section_at[0]
    mine = head // half_heads == section
    local = head % half_heads
    for gate, out_ref in enumerate((rate_ref, input_ref)):
        index = jnp.bitwise_xor(2 * local + gate, unit_at[0])
        for k in range(units):
            here = index == k
            sources = (
                (jnp.logical_and(mine, section == 1), tops[k]),
                (jnp.logical_and(mine, section == 0), lows[k]),
                (jnp.logical_not(mine), others[k]),
            )
            for wanted, source in sources:

                @pl.when(jnp.logical_and(here, wanted))
                def _(source=source, gate=gate, out_ref=out_ref):
                    out_ref[0] = source[:size, :].astype(F32) * scale
                    rows = source[size:, :].astype(F32) * scale
                    if gate == 0:
                        vector_ref[:, 0, :] = rows[:3]
                    else:
                        vector_ref[:, 0, :] += rows[:3]


def xor_moves(value, axis, k):
    return lax.ppermute(value, axis, [(i, i ^ k) for i in range(lax.axis_size(axis))])


def swap_sections(value):
    return lax.ppermute(value, "section", [(0, 1), (1, 0)])


def chan_parts(value):
    count = lax.axis_size("chan")
    if count & (count - 1):
        gathered = lax.all_gather(value, "chan")
        return [gathered[k] for k in range(count)]
    return [xor_moves(value, "chan", k) for k in reversed(range(1, count))] + [value]


def seq_pays(ahead, behind, near, far):
    if lax.axis_size("seq") != DIRECT_RANKS:
        return [lax.all_gather(jnp.concatenate([ahead, behind], axis=0), "seq")]
    return [xor_moves(far, "seq", 3), xor_moves(far, "seq", 2), xor_moves(near, "seq", 1)][::-1]


def add_units(value, *others):
    return pl.pallas_call(
        add_kernel,
        out_shape=jax.ShapeDtypeStruct(value.shape, value.dtype),
        compiler_params=params(),
        cost_estimate=cost(0, 8 * value.size),
    )(value, *others)


def add_pairs(a, b):
    return pl.pallas_call(
        add_pairs_kernel,
        out_shape=[jax.ShapeDtypeStruct(a.shape[1:], a.dtype)] * a.shape[0],
        compiler_params=params(),
        cost_estimate=cost(0, 6 * a.size),
    )(a, b)


def after(value, *others):
    return lax.optimization_barrier((value, *others))[0]


def on_device(
    layer_inputs,
    out_grad,
    rate_weight,
    input_weight,
    rate_bias,
    input_bias,
    decay_param,
    norm_gain,
    doc_starts,
):
    micro, tok_rows, chan_width = out_grad.shape
    seq_count = lax.axis_size("seq")
    heads, size = rate_weight.shape[1:3]
    half_heads = heads // 2
    half = chan_width // 2
    rows = micro * tok_rows
    full_width = chan_width * lax.axis_size("chan")
    grad_scale = 1.0 / math.sqrt(micro * tok_rows * seq_count)
    seq_at = lax.axis_index("seq").reshape(1).astype(jnp.int32)
    section = lax.axis_index("section")
    section_at = section.reshape(1).astype(jnp.int32)

    x_raw = layer_inputs.reshape(rows, chan_width)
    up_raw = out_grad.reshape(rows, chan_width)

    def shape(dims, dtype=F32):
        return jax.ShapeDtypeStruct(dims, dtype)

    smem = pl.BlockSpec(memory_space=pltpu.SMEM)
    whole = pl.BlockSpec(memory_space=pltpu.VMEM)

    def call(kernel, scalars, arrays, outs, scratch=(), flops=0, size_bytes=0, specs=None):
        return pl.pallas_call(
            kernel,
            in_specs=[smem] * len(scalars) + (specs or [whole] * len(arrays)),
            out_shape=outs,
            scratch_shapes=[
                pltpu.VMEM(*entry) if isinstance(entry, tuple) else entry for entry in scratch
            ],
            compiler_params=params(),
            cost_estimate=cost(flops, size_bytes),
        )(*scalars, *arrays)

    half_x = shape((rows, half), BF16)
    half_w = shape((heads, size, size), BF16)
    half_v = shape((8, half))
    square, x_keep, x_send, upstream, w_keep, w_send, v_keep, v_send, opened = call(
        functools.partial(prepare_kernel, micro, tok_rows),
        [section_at, seq_at],
        [
            pltpu.with_memory_space_constraint(array, pltpu.HBM)
            for array in (
                doc_starts, x_raw, up_raw, rate_weight[0], input_weight[0],
                rate_bias, input_bias, decay_param, norm_gain,
            )
        ],
        [shape((8, rows)), half_x, half_x, half_x, half_w, half_w, half_v, half_v, shape((rows, 128))],
        [
            (doc_starts.shape, jnp.int32),
            ((rows, chan_width), BF16),
            ((rows, half), BF16),
            ((4, 1, chan_width), F32),
            pltpu.SemaphoreType.DMA((11,)),
        ],
        specs=[pl.BlockSpec(memory_space=pltpu.HBM)] * 9,
        flops=4 * rows * rows * chan_width,
        size_bytes=12 * rows * chan_width,
    )
    own_squares = chan_parts(square)
    other_squares = swap_sections(add_units(*own_squares))
    x_got, w_got, v_got = (swap_sections(value) for value in (x_send, w_send, v_send))

    big = shape((rows, half))
    blocks = shape((micro * 8, half))
    pay = shape((2 * micro, half))

    def forward(layer, beside):
        return call(
            functools.partial(
                forward_kernel, micro, tok_rows, full_width, layer, len(own_squares)
            ),
            [seq_at, section_at],
            [
                *own_squares, other_squares, opened, x_keep, x_got, w_keep, w_got, v_keep, v_got,
                beside,
            ],
            [half_x, shape((5, rows, half)), shape((3, micro * 8, half)), pay, shape((rows, 128))]
            + ([blocks] + [pay] * 3) * layer,
            [((rows, size), F32)] * 2,
            flops=4 * rows * size * half,
            size_bytes=24 * rows * half,
        )

    direct = seq_count == DIRECT_RANKS and heads == DIRECT_RANKS
    unit_dims = {0: [()] * 4, 1: [(2,)] * 2} if direct else {0: [(heads,)], 1: [(heads,)]}

    def backward(layer, pays, upstream, kept, rgrad, before):
        normed, factors, block, _, inv = kept
        return call(
            functools.partial(
                backward_kernel, micro, tok_rows, seq_count, layer, direct, len(pays)
            ),
            [seq_at, section_at],
            [
                *pays, x_keep, x_got, upstream, normed, factors, block, rgrad, inv,
                v_keep, v_got, w_keep, w_got, before,
            ],
            [big, shape((8, rows))]
            + [shape(dims + (size + VECTOR_ROWS, size), BF16) for dims in unit_dims[layer]],
            [
                ((micro, half), F32),
                ((micro, half), F32),
                ((tok_rows, size), F32),
                ((rows, size), F32),
                ((rows, size), BF16),
                ((rows, size), BF16),
                ((rows, 128), F32),
                ((heads, size + VECTOR_ROWS, size), BF16),
            ],
            flops=8 * rows * size * half,
            size_bytes=30 * rows * half,
        )

    def chip_sum(value):
        return add_units(value, swap_sections(value))

    *top, top_rgrad, behind, near, far = forward(1, upstream)
    pays = seq_pays(top[3], behind, near, far)
    low = forward(0, top[1])
    part, cross, *top_parts = backward(1, pays, upstream, top, top_rgrad, low[3])
    parts = chan_parts(chip_sum(cross))
    if direct:
        arrived = xor_moves(top_parts[1], "seq", 1)
    early, low_rgrad, behind, near, far = call(
        functools.partial(late_kernel, micro, tok_rows, full_width, len(parts)),
        [seq_at, section_at],
        [part, x_keep, x_got, top[4], low[1], low[3], *parts],
        [half_x, blocks] + [pay] * 3,
        [((rows, 128), F32)],
        flops=8 * rows * half,
        size_bytes=12 * rows * half,
    )
    pays = seq_pays(low[3], behind, near, far)
    if direct:
        own_pair, far_pair = add_pairs(top_parts[0], after(arrived, near))
        arrived = xor_moves(far_pair, "seq", 2)
        top_own = add_units(own_pair, after(arrived, *pays))
        top_far = xor_moves(top_own, "seq", 2)
    part, cross, *low_parts = backward(
        0, pays, early, low, low_rgrad, top_own if direct else behind
    )
    parts = chan_parts(chip_sum(cross))
    if direct:
        place = lax.axis_index("seq")
        low_arrived = [xor_moves(low_parts[k], "seq", k) for k in (3, 2, 1)]
        low_arrived, parts = lax.optimization_barrier((low_arrived, parts))
        low_own = add_units(low_parts[0], *low_arrived)
        low_units = [low_own] + [xor_moves(low_own, "seq", k) for k in (1, 2, 3)]
        pair = xor_moves(jnp.stack([top_own, after(top_far, low_own)]), "seq", 1)
        top_units = [top_own, pair[0], top_far, pair[1]]
    else:
        place = jnp.zeros((), jnp.int32)
        top_units, low_units = (
            [total[k] for k in range(heads)]
            for total in (
                lax.psum(value.astype(F32), "seq").astype(BF16)
                for value in (top_parts[0], low_parts[0])
            )
        )
    grads_keep, grads_send = call(
        functools.partial(last_kernel, full_width, tok_rows, len(parts)),
        [section_at],
        [part, x_keep, x_got, low[4], early, *parts],
        [half_x, half_x],
        flops=4 * rows * rows * half,
        size_bytes=12 * rows * half,
    )
    grads = call(
        join_kernel, [section_at], [grads_keep, swap_sections(grads_send)],
        shape((rows, chan_width), BF16), size_bytes=4 * rows * chan_width,
    )
    if direct:
        grads, top_units, low_units = lax.optimization_barrier((grads, top_units, low_units))

    other_units = [
        swap_sections(jnp.where(section == 1, b, a)) for a, b in zip(top_units, low_units)
    ]
    out_block = pl.BlockSpec((1, size, size), lambda h: (h, 0, 0))
    rate_total, input_total, vector = pl.pallas_call(
        functools.partial(weights_kernel, heads, grad_scale),
        grid=(heads,),
        in_specs=[smem, smem] + [whole] * (3 * heads),
        out_specs=[out_block, out_block, pl.BlockSpec((3, 1, size), lambda h: (0, 0, h))],
        out_shape=[
            shape((heads, size, size)),
            shape((heads, size, size)),
            shape((3, 1, chan_width)),
        ],
        compiler_params=params(),
        cost_estimate=cost(0, 8 * heads * size * size),
    )(
        section_at, place.reshape(1).astype(jnp.int32), *top_units, *low_units, *other_units
    )
    return (
        grads.reshape(1, micro, tok_rows, chan_width),
        rate_total[None],
        input_total[None],
        jnp.swapaxes(vector, 0, 1),
    )


def solution(mesh):
    in_specs = (
        P("section", None, "seq", "chan"),
        P(None, "seq", "chan"),
        P("section", "chan", None, None),
        P("section", "chan", None, None),
        P("section", "chan"),
        P("section", "chan"),
        P("section", "chan"),
        P("section", "chan"),
        P(),
    )
    out_specs = (
        P("section", None, "seq", "chan"),
        P("section", "chan", None, None),
        P("section", "chan", None, None),
        P("section", None, "chan"),
    )
    return jax.shard_map(
        on_device, mesh=mesh, in_specs=in_specs, out_specs=out_specs, check_vma=False
    )
```

time: 946 us -> 87.6 us (0.09); the launches traced: 932 us -> 87.5 us
  local copies, waits for them, and re-layouts: 325 us -> 0.02 us
  blocking collectives: 306 us -> 0 us
  other arithmetic: 188 us -> 0.1 us
  waiting for transfers between devices: 66.3 us -> 35.9 us
  starting transfers between devices: 6.44 us -> 34.9 us
  matrix products: 20 us -> 0 us
  Pallas kernels: 0 us -> 15.7 us
  between operations: 14.1 us -> 0.78 us
    all_gather x15 -> x0, blocking collectives: 198 us -> none  [prefix(): everything = jax.tree.map(lambda part: lax.all_gather(part, axis), value)]
    slice x395 -> x0, local copies, waits for them, and re-layouts: 148 us -> none  [the longest x205 98.9 us: layer_step(): lax.associative_scan(pair_combine, (next_decay[::-1], upstream_wide[::-1]...]
    psum x11 -> x0, blocking collectives: 108 us -> none  [the longest x5 49 us: layer_step(): square_sum = lax.psum(jnp.sum(xfloat * xfloat, axis=1), 'chan')]
    psum x1 -> x0, waiting for transfers between devices: 66.3 us -> none  [on_device(): weight_sum, vector_sum = lax.psum((loop_out[2], loop_out[3]), 'seq')]
    pad x190 -> x0, local copies, waits for them, and re-layouts: 62 us -> none  [the longest x100 42.1 us: layer_step(): lax.associative_scan(pair_combine, (next_decay[::-1], upstream_wide[::-1]...]
    concatenate x86 -> x0, other arithmetic: 56.5 us -> none  [the longest x45 30 us: layer_step(): lax.associative_scan(pair_combine, (decay_eff, lru_drive), axis=0)]
    mul x97 -> x0, other arithmetic: 45.6 us -> none  [the longest x90 40.3 us: pair_combine(): first_pair[0] * second_pair[0]]
    rev x10 -> x0, local copies, waits for them, and re-layouts: 43.3 us -> none  [the longest x5 21.7 us: layer_step(): tail_decay = flip_decay[::-1]]
  transfers between devices with their start and end apart: 6 -> 36, of which waited for: 1 -> 23; matrix products, arithmetic and copies ran while one was open for 20% -> 0% of each run, Pallas kernels for 0% -> 6%
where the time goes in v2:
time: 87.6 us; the launch traced here: 87.5 us
  waiting for transfers between devices  35.9 us (41%)
  starting transfers between devices  34.9 us (40%)
  Pallas kernels  15.7 us (18%)
    ppermute x25, starting transfers between devices, xor_moves(): lax.ppermute(value, axis, [(i, i ^ k) for i in range(lax.axis_size(axis))])  32.9 us
    ppermute x25, waiting for transfers between devices, xor_moves(): lax.ppermute(value, axis, [(i, i ^ k) for i in range(lax.axis_size(axis))])  31.4 us
    pallas_call x8, Pallas kernels, call(): pl.pallas_call(kernel, in_specs=[smem] * len(scalars) + (specs or [whole]...  13.4 us
    ppermute x11, waiting for transfers between devices, swap_sections(): return lax.ppermute(value, 'section', [(0, 1), (1, 0)])  4.5 us
    pallas_call x1, Pallas kernels, on_device(): pl.pallas_call(functools.partial(weights_kernel, heads, grad_scale), grid...  2.11 us
    ppermute x11, starting transfers between devices, swap_sections(): return lax.ppermute(value, 'section', [(0, 1), (1, 0)])  1.99 us
  transfers between devices with their start and end apart: 36, of which 23 were waited for; matrix products, arithmetic and copies ran while one was open for 0% of the time, Pallas kernels for 6%

profile of v2, /device:TPU:0, one launch (start us, length us, event | category | flops | bytes accessed | tf_op | source)
XLA Modules:
  0.0 87.5 jit_solution(1413417731384306483)
XLA Ops:
  0.6 2.5 %shard_map.120 = (f32[8,256]{1,0:T(8,128)S(1)}, bf16[256,512]{1,0:T(8,128)(2,1)S(1)}, bf16[256,512]{1,0:T(8,128)(2,1)S(1)}, bf16[256,512]{1,0:T(8,128)(2,1)S(1)}...) custom-call(s32[1]{0:T(128)} %bitcast.section_at, ...), custom_call_target="tpu_custom_call" | custom-call | flops 268435456 | bytes 3145728 | tf_op jit(solution)/shard_map/pallas_call | solution.py:591
  3.2 0.5 collective-permute-start.5
  3.8 3.9 %collective-permute-start = (f32[8,256]{1,0:T(8,128)S(1)}, f32[8,256]{1,0:T(8,128)S(1)}, u32[]{:S(2)}, u32[]{:S(2)}) collective-permute-start(f32[8,256]{1,0:T(8,128)S(1)} %get-tuple-element.65.refs_3_), channel_id=1, source_target_pairs={{0,3},{1,2},{2,1},{3,0},{4,7},{5,6},{6,5},{7,4},{8,11},{9,10},{10,... | collective-permute-start | bytes 24584 | tf_op jit(solution)/shard_map/ppermute | solution.py:515
  7.7 0.5 collective-permute-start.1
  8.2 1.1 %collective-permute-done.refs_0_ = f32[8,256]{1,0:T(8,128)S(1)} collective-permute-done((f32[8,256]{1,0:T(8,128)S(1)}, f32[8,256]{1,0:T(8,128)S(1)}, u32[]{:S(2)}, u32[]{:S(2)}) %collective-permute-start) | collective-permute-done | bytes 8224 | tf_op jit(solution)/shard_map/ppermute | solution.py:515
  9.3 2.0 %collective-permute-done.1.refs_1_ = f32[8,256]{1,0:T(8,128)S(1)} collective-permute-done((f32[8,256]{1,0:T(8,128)S(1)}, f32[8,256]{1,0:T(8,128)S(1)}, u32[]{:S(2)}, u32[]{:S(2)}) %collective-permute-start.1) | collective-permute-done | bytes 8224 | tf_op jit(solution)/shard_map/ppermute | solution.py:515
  11.8 1.2 %collective-permute-done.3.refs_4_ = f32[8,256]{1,0:T(8,128)S(1)} collective-permute-done((f32[8,256]{1,0:T(8,128)S(1)}, f32[8,256]{1,0:T(8,128)S(1)}, u32[]{:S(2)}, u32[]{:S(2)}) %collective-permute-start.3) | collective-permute-done | bytes 8224 | tf_op jit(solution)/shard_map/ppermute | solution.py:519
  13.0 2.7 %shard_map.122 = (bf16[256,512]{1,0:T(8,128)(2,1)S(1)}, f32[5,256,512]{2,1,0:T(8,128)S(1)}, f32[3,32,512]{2,1,0:T(8,128)S(1)}, f32[8,512]{1,0:T(8,128)}, f32[256...) custom-call(s32[1]{0:T(128)} %bitcast.1.seq_at.unit_at, ...), custom_call_target="tpu_custom_call" | custom-call | flops 134217728 | bytes 3145728 | tf_op jit(solution)/shard_map/pallas_call | solution.py:591
  15.7 1.6 %collective-permute-start.7 = (f32[8,512]{1,0:T(8,128)S(1)}, f32[8,512]{1,0:T(8,128)S(1)}, u32[]{:S(2)}, u32[]{:S(2)}) collective-permute-start(f32[8,512]{1,0:T(8,128)S(1)} %get-tuple-element.74), channel_id=1, source_target_pairs={{0,4},{4,0},{8,12},{12,8},{1,5},{5,1},{9,13},{13,9},{2,6},{6,2},{1... | collective-permute-start | bytes 49160 | tf_op jit(solution)/shard_map/ppermute | solution.py:515
  17.3 2.6 %collective-permute-start.8 = (f32[8,512]{1,0:T(8,128)S(1)}, f32[8,512]{1,0:T(8,128)S(1)}, u32[]{:S(2)}, u32[]{:S(2)}) collective-permute-start(f32[8,512]{1,0:T(8,128)S(1)} %get-tuple-element.75), channel_id=1, source_target_pairs={{0,8},{4,12},{8,0},{12,4},{1,9},{5,13},{9,1},{13,5},{2,10},{6,14},... | collective-permute-start | bytes 49160 | tf_op jit(solution)/shard_map/ppermute | solution.py:515
  20.1 2.1 %shard_map.123 = (bf16[256,512]{1,0:T(8,128)(2,1)S(1)}, f32[5,256,512]{2,1,0:T(8,128)S(1)}, f32[3,32,512]{2,1,0:T(8,128)S(1)}, f32[8,512]{1,0:T(8,128)S(1)}, f32[256,128]{1,0:T(8,128)S(1)}) custom-call(s32[1]{0:T(128)} %bitcast.1.seq_at.unit_at, s32[1]{0:T(128)} %bitcast.section_at, f32[8,256]{1,0:T(8,128)S(1)} %collective-permute-done.refs_0_, ...), custom_call_target="tpu_custom_call" | custom-call | flops 134217728 | bytes 3145728 | tf_op jit(solution)/shard_map/pallas_call | solution.py:591
  22.2 3.2 %collective-permute-done.9.refs_2_ = f32[8,512]{1,0:T(8,128)S(1)} collective-permute-done((f32[8,512]{1,0:T(8,128)S(1)}, f32[8,512]{1,0:T(8,128)S(1)}, u32[]{:S(2)}, u32[]{:S(2)}) %collective-permute-start.9) | collective-permute-done | bytes 16416 | tf_op jit(solution)/shard_map/ppermute | solution.py:515
  25.4 1.6 %shard_map.124 = (f32[256,512]{1,0:T(8,128)S(1)}, f32[8,256]{1,0:T(8,128)S(1)}, bf16[2,272,256]{2,1,0:T(8,128)(2,1)S(1)}, bf16[2,272,256]{2,1,0:T(8,128)(2,1)S(1)}) custom-call(s32[1]{0:T(128)} %bitcast.1.seq_at.unit_at, s32[1]{0:T(128)} %bitcast.section_at, f32[8,512]{1,0:T(8,128)S(1)} %collective-permute-done.7.refs_0_, ...), custom_call_target="tpu_custom_call" | custom-call | flops 268435456 | bytes 3932160 | tf_op jit(solution)/shard_map/pallas_call | solution.py:591
  27.0 1.2 %collective-permute-done.10.refs_1_ = f32[8,256]{1,0:T(8,128)S(1)} collective-permute-done((f32[8,256]{1,0:T(8,128)S(1)}, f32[8,256]{1,0:T(8,128)S(1)}, u32[]{:S(2)}, u32[]{:S(2)}) %collective-permute-start.10) | collective-permute-done | bytes 8224 | tf_op jit(solution)/shard_map/ppermute | solution.py:519
  28.2 1.5 %collective-permute-start.11 = (f32[8,256]{1,0:T(8,128)S(1)}, f32[8,256]{1,0:T(8,128)S(1)}, u32[]{:S(2)}, u32[]{:S(2)}) collective-permute-start(f32[8,256]{1,0:T(8,128)S(1)} %shard_map.125.refs_3_), channel_id=1, source_target_pairs={{0,3},{1,2},{2,1},{3,0},{4,7},{5,6},{6,5},{7,4},{8,11},{9,10},{10,... | collective-permute-start | bytes 24584 | tf_op jit(solution)/shard_map/ppermute | solution.py:515
  29.7 0.5 collective-permute-start.12
  30.2 1.5 %collective-permute-start.13 = (f32[8,256]{1,0:T(8,128)S(1)}, f32[8,256]{1,0:T(8,128)S(1)}, u32[]{:S(2)}, u32[]{:S(2)}) collective-permute-start(f32[8,256]{1,0:T(8,128)S(1)} %shard_map.125.refs_3_), channel_id=1, source_target_pairs={{0,1},{1,0},{2,3},{3,2},{4,5},{5,4},{6,7},{7,6},{8,9},{9,8},{10,11... | collective-permute-start | bytes 24584 | tf_op jit(solution)/shard_map/ppermute | solution.py:515
  31.7 1.1 %collective-permute-done.11.refs_0_ = f32[8,256]{1,0:T(8,128)S(1)} collective-permute-done((f32[8,256]{1,0:T(8,128)S(1)}, f32[8,256]{1,0:T(8,128)S(1)}, u32[]{:S(2)}, u32[]{:S(2)}) %collective-permute-start.11) | collective-permute-done | bytes 8224 | tf_op jit(solution)/shard_map/ppermute | solution.py:515
  32.7 0.6 collective-permute-done.12.refs_1_
  33.3 0.5 collective-permute-done.13.refs_2_
  33.8 1.3 %shard_map.126 = (bf16[256,512]{1,0:T(8,128)(2,1)S(1)}, f32[32,512]{1,0:T(8,128)S(1)}, f32[8,512]{1,0:T(8,128)}, f32[8,512]{1,0:T(8,128)S(1)}, f32[8,512]{1,0:T(8,128)S(1)}) custom-call(s32[1]{0:T(128)} %bitcast.1.seq_at.unit_at, s32[1]{0:T(128)} %bitcast.section_at, f32[256,512]{1,0:T(8,128)S(1)} %get-tuple-element.82.part_ref, ...), custom_call_target="tpu_custom_call" | custom-call | flops 1048576 | bytes 1572864 | tf_op jit(solution)/shard_map/pallas_call | solution.py:591
  35.2 1.0 %collective-permute-start.18 = (bf16[272,256]{1,0:T(8,128)(2,1)S(1)}, bf16[272,256]{1,0:T(8,128)(2,1)S(1)}, u32[]{:S(2)}, u32[]{:S(2)}) collective-permute-start(bf16[272,256]{1,0:T(8,128)(2,1)S(1)} %get-tuple-element.96), channel_id=1, source_target_pairs={{0,8},{4,12},{8,0},{12,4},{1,9},{5,13},{9,1},{13,5},{2,10},{6,14},... | collective-permute-start | bytes 417800 | tf_op jit(solution)/shard_map/ppermute | solution.py:515
  36.2 1.1 %collective-permute-start.14 = (f32[8,512]{1,0:T(8,128)S(1)}, f32[8,512]{1,0:T(8,128)S(1)}, u32[]{:S(2)}, u32[]{:S(2)}) collective-permute-start(f32[8,512]{1,0:T(8,128)S(1)} %get-tuple-element.85), channel_id=1, source_target_pairs={{0,4},{4,0},{8,12},{12,8},{1,5},{5,1},{9,13},{13,9},{2,6},{6,2},{1... | collective-permute-start | bytes 49160 | tf_op jit(solution)/shard_map/ppermute | solution.py:515
  37.3 2.8 %collective-permute-start.15 = (f32[8,512]{1,0:T(8,128)S(1)}, f32[8,512]{1,0:T(8,128)S(1)}, u32[]{:S(2)}, u32[]{:S(2)}) collective-permute-start(f32[8,512]{1,0:T(8,128)S(1)} %get-tuple-element.86), channel_id=1, source_target_pairs={{0,8},{4,12},{8,0},{12,4},{1,9},{5,13},{9,1},{13,5},{2,10},{6,14},... | collective-permute-start | bytes 49160 | tf_op jit(solution)/shard_map/ppermute | solution.py:515
  40.6 3.9 %collective-permute-done.15.refs_1_ = f32[8,512]{1,0:T(8,128)S(1)} collective-permute-done((f32[8,512]{1,0:T(8,128)S(1)}, f32[8,512]{1,0:T(8,128)S(1)}, u32[]{:S(2)}, u32[]{:S(2)}) %collective-permute-start.15) | collective-permute-done | bytes 16416 | tf_op jit(solution)/shard_map/ppermute | solution.py:515
  44.5 1.2 %collective-permute-done.16.refs_2_ = f32[8,512]{1,0:T(8,128)S(1)} collective-permute-done((f32[8,512]{1,0:T(8,128)S(1)}, f32[8,512]{1,0:T(8,128)S(1)}, u32[]{:S(2)}, u32[]{:S(2)}) %collective-permute-start.16) | collective-permute-done | bytes 16416 | tf_op jit(solution)/shard_map/ppermute | solution.py:515
  45.8 1.6 %shard_map.129 = (f32[256,512]{1,0:T(8,128)S(1)}, f32[8,256]{1,0:T(8,128)S(1)}, bf16[272,256]{1,0:T(8,128)(2,1)S(1)}, bf16[272,256]{1,0:T(8,128)(2,1)S(1)}, bf16...) custom-call(s32[1]{0:T(128)} %bitcast.1.seq_at.unit_at, s32[1]{0:T(128)} %bitcast.section_at, ...), custom_call_target="tpu_custom_call" | custom-call | flops 268435456 | bytes 3932160 | tf_op jit(solution)/shard_map/pallas_call | solution.py:591
  47.4 0.7 collective-permute-start.19
  48.4 3.4 %collective-permute-start.21 = (bf16[272,256]{1,0:T(8,128)(2,1)S(1)}, bf16[272,256]{1,0:T(8,128)(2,1)S(1)}, u32[]{:S(2)}, u32[]{:S(2)}) collective-permute-start(bf16[272,256]{1,0:T(8,128)(2,1)S(1)} %get-tuple-element.101), channel_id=1, source_target_pairs={{0,4},{4,0},{8,12},{12,8},{1,5},{5,1},{9,13},{13,9},{2,6},{6,2},{1... | collective-permute-start | bytes 417800 | tf_op jit(solution)/shard_map/ppermute | solution.py:515
  51.8 1.2 %collective-permute-done.22.refs_1_ = f32[8,256]{1,0:T(8,128)S(1)} collective-permute-done((f32[8,256]{1,0:T(8,128)S(1)}, f32[8,256]{1,0:T(8,128)S(1)}, u32[]{:S(2)}, u32[]{:S(2)}) %collective-permute-start.22) | collective-permute-done | bytes 8224 | tf_op jit(solution)/shard_map/ppermute | solution.py:519
  53.0 2.4 %collective-permute-start.23 = (f32[8,256]{1,0:T(8,128)S(1)}, f32[8,256]{1,0:T(8,128)S(1)}, u32[]{:S(2)}, u32[]{:S(2)}) collective-permute-start(f32[8,256]{1,0:T(8,128)S(1)} %shard_map.130.refs_3_), channel_id=1, source_target_pairs={{0,3},{1,2},{2,1},{3,0},{4,7},{5,6},{6,5},{7,4},{8,11},{9,10},{10,... | collective-permute-start | bytes 24584 | tf_op jit(solution)/shard_map/ppermute | solution.py:515
  55.4 2.1 %collective-permute-done.23.refs_0_ = f32[8,256]{1,0:T(8,128)S(1)} collective-permute-done((f32[8,256]{1,0:T(8,128)S(1)}, f32[8,256]{1,0:T(8,128)S(1)}, u32[]{:S(2)}, u32[]{:S(2)}) %collective-permute-start.23) | collective-permute-done | bytes 8224 | tf_op jit(solution)/shard_map/ppermute | solution.py:515
  57.5 1.5 %collective-permute-start.24 = (f32[8,256]{1,0:T(8,128)S(1)}, f32[8,256]{1,0:T(8,128)S(1)}, u32[]{:S(2)}, u32[]{:S(2)}) collective-permute-start(f32[8,256]{1,0:T(8,128)S(1)} %shard_map.130.refs_3_), channel_id=1, source_target_pairs={{0,2},{1,3},{2,0},{3,1},{4,6},{5,7},{6,4},{7,5},{8,10},{9,11},{10,... | collective-permute-start | bytes 24584 | tf_op jit(solution)/shard_map/ppermute | solution.py:515
  59.0 2.1 %collective-permute-done.24.refs_1_ = f32[8,256]{1,0:T(8,128)S(1)} collective-permute-done((f32[8,256]{1,0:T(8,128)S(1)}, f32[8,256]{1,0:T(8,128)S(1)}, u32[]{:S(2)}, u32[]{:S(2)}) %collective-permute-start.24) | collective-permute-done | bytes 8224 | tf_op jit(solution)/shard_map/ppermute | solution.py:515
  61.2 1.5 %collective-permute-start.25 = (f32[8,256]{1,0:T(8,128)S(1)}, f32[8,256]{1,0:T(8,128)S(1)}, u32[]{:S(2)}, u32[]{:S(2)}) collective-permute-start(f32[8,256]{1,0:T(8,128)S(1)} %shard_map.130.refs_3_), channel_id=1, source_target_pairs={{0,1},{1,0},{2,3},{3,2},{4,5},{5,4},{6,7},{7,6},{8,9},{9,8},{10,11... | collective-permute-start | bytes 24584 | tf_op jit(solution)/shard_map/ppermute | solution.py:515
  62.6 2.2 %collective-permute-done.25.refs_2_ = f32[8,256]{1,0:T(8,128)S(1)} collective-permute-done((f32[8,256]{1,0:T(8,128)S(1)}, f32[8,256]{1,0:T(8,128)S(1)}, u32[]{:S(2)}, u32[]{:S(2)}) %collective-permute-start.25) | collective-permute-done | bytes 8224 | tf_op jit(solution)/shard_map/ppermute | solution.py:515
  65.4 0.9 %collective-permute-start.28 = (bf16[2,272,256]{2,1,0:T(8,128)(2,1)S(1)}, bf16[2,272,256]{2,1,0:T(8,128)(2,1)S(1)}, u32[]{:S(2)}, u32[]{:S(2)}) collective-permute-start(bf16[2,272,256]{2,1,0:T(8,128)(2,1)S(1)} %pad_maximum_fusion), channel_id=1, source_target_pairs={{0,4},{4,0},{8,12},{12,8},{1,5},{5,1},{9,13},{13,9},{2,6},{6,2},{1... | collective-permute-start | bytes 835592 | tf_op jit(solution)/shard_map/ppermute | solution.py:515
  66.3 0.8 shard_map.131
  67.2 1.3 %collective-permute-start.29 = (bf16[272,256]{1,0:T(8,128)(2,1)S(1)}, bf16[272,256]{1,0:T(8,128)(2,1)S(1)}, u32[]{:S(2)}, u32[]{:S(2)}) collective-permute-start(bf16[272,256]{1,0:T(8,128)(2,1)S(1)} %shard_map.133.refs_4_), channel_id=1, source_target_pairs={{0,4},{4,0},{8,12},{12,8},{1,5},{5,1},{9,13},{13,9},{2,6},{6,2},{1... | collective-permute-start | bytes 417800 | tf_op jit(solution)/shard_map/ppermute | solution.py:515
  68.4 2.5 %collective-permute-start.30 = (bf16[272,256]{1,0:T(8,128)(2,1)S(1)}, bf16[272,256]{1,0:T(8,128)(2,1)S(1)}, u32[]{:S(2)}, u32[]{:S(2)}) collective-permute-start(bf16[272,256]{1,0:T(8,128)(2,1)S(1)} %shard_map.133.refs_4_), channel_id=1, source_target_pairs={{0,8},{4,12},{8,0},{12,4},{1,9},{5,13},{9,1},{13,5},{2,10},{6,14},... | collective-permute-start | bytes 417800 | tf_op jit(solution)/shard_map/ppermute | solution.py:515
  70.9 0.7 collective-permute-start.31
  71.6 0.8 shard_map.132
  72.5 4.7 %collective-permute-done.28 = bf16[2,272,256]{2,1,0:T(8,128)(2,1)S(1)} collective-permute-done((bf16[2,272,256]{2,1,0:T(8,128)(2,1)S(1)}, bf16[2,272,256]{2,1,0:T(8,128)(2,1)S(1)}, u32[]{:S(2)}, u32[]{:S(2)}) %collective-permute-start.28) | collective-permute-done | bytes 278560 | tf_op jit(solution)/shard_map/ppermute | solution.py:515
  77.2 1.9 %collective-permute-done.29.refs_5_ = bf16[272,256]{1,0:T(8,128)(2,1)S(1)} collective-permute-done((bf16[272,256]{1,0:T(8,128)(2,1)S(1)}, bf16[272,256]{1,0:T(8,128)(2,1)S(1)}, u32[]{:S(2)}, u32[]{:S(2)}) %collective-permute-start.29) | collective-permute-done | bytes 139296 | tf_op jit(solution)/shard_map/ppermute | solution.py:515
  79.1 3.9 %collective-permute-done.31.refs_7_ = bf16[272,256]{1,0:T(8,128)(2,1)S(1)} collective-permute-done((bf16[272,256]{1,0:T(8,128)(2,1)S(1)}, bf16[272,256]{1,0:T(8,128)(2,1)S(1)}, u32[]{:S(2)}, u32[]{:S(2)}) %collective-permute-start.31) | collective-permute-done | bytes 139296 | tf_op jit(solution)/shard_map/ppermute | solution.py:515
  83.1 0.6 collective-permute-start.34
  83.8 0.6 collective-permute-start.32
  85.3 2.1 %shard_map.134 = (f32[4,256,256]{2,1,0:T(8,128)}, f32[4,256,256]{2,1,0:T(8,128)}, f32[3,1,1024]{2,1,0:T(1,128)}) custom-call(s32[1]{0:T(128)} %bitcast.section_at, s32[1]{0:T(128)} %bitcast.1.seq_at.unit_at, bf16[272,256]{1,0:T(8,128)(2,1)S(1)} %shard_map.128.refs_15_.refs_0_, bf16[272,256]{1,0:T(8,128)(2,1)S(1)} %get-tuple-element.116.refs_1_, ...), custom_call_target="tpu_custom_call" | custom-call | bytes 2097152 | tf_op jit(solution)/shard_map/pallas_call | solution.py:747
  (45 shorter events, 3.7 us)
Async XLA Ops:
  3.2 9.8 %collective-permute-start.5 = (bf16[4,256,256]{2,1,0:T(8,128)(2,1)S(1)}, bf16[4,256,256]{2,1,0:T(8,128)(2,1)S(1)}, u32[]{:S(2)}, u32[]{:S(2)}) collective-permute-start(bf16[4,256,256]{2,1,0:T(8,128)(2,1)S(1)} %get-tuple-element.70), channel_id=1, source_target_pairs={{0,16},{16,0},{1,17},{17,1},{2,18},{18,2},{3,19},{19,3},{4,20},{20... | collective-permute-start | bytes 1572872 | tf_op jit(solution)/shard_map/ppermute | solution.py:519
  3.7 9.3 %collective-permute-start.4 = (bf16[256,512]{1,0:T(8,128)(2,1)S(1)}, bf16[256,512]{1,0:T(8,128)(2,1)S(1)}, u32[]{:S(2)}, u32[]{:S(2)}) collective-permute-start(bf16[256,512]{1,0:T(8,128)(2,1)S(1)} %get-tuple-element.68), channel_id=1, source_target_pairs={{0,16},{16,0},{1,17},{17,1},{2,18},{18,2},{3,19},{19,3},{4,20},{20... | collective-permute-start | bytes 786440 | tf_op jit(solution)/shard_map/ppermute | solution.py:519
  3.8 5.5 %collective-permute-start = (f32[8,256]{1,0:T(8,128)S(1)}, f32[8,256]{1,0:T(8,128)S(1)}, u32[]{:S(2)}, u32[]{:S(2)}) collective-permute-start(f32[8,256]{1,0:T(8,128)S(1)} %get-tuple-element.65.refs_3_), channel_id=1, source_target_pairs={{0,3},{1,2},{2,1},{3,0},{4,7},{5,6},{6,5},{7,4},{8,11},{9,10},{10,... | collective-permute-start | bytes 24584 | tf_op jit(solution)/shard_map/ppermute | solution.py:515
  7.7 3.7 %collective-permute-start.1 = (f32[8,256]{1,0:T(8,128)S(1)}, f32[8,256]{1,0:T(8,128)S(1)}, u32[]{:S(2)}, u32[]{:S(2)}) collective-permute-start(f32[8,256]{1,0:T(8,128)S(1)} %get-tuple-element.65.refs_3_), channel_id=1, source_target_pairs={{0,2},{1,3},{2,0},{3,1},{4,6},{5,7},{6,4},{7,5},{8,10},{9,11},{10,... | collective-permute-start | bytes 24584 | tf_op jit(solution)/shard_map/ppermute | solution.py:515
  8.2 3.7 %collective-permute-start.2 = (f32[8,256]{1,0:T(8,128)S(1)}, f32[8,256]{1,0:T(8,128)S(1)}, u32[]{:S(2)}, u32[]{:S(2)}) collective-permute-start(f32[8,256]{1,0:T(8,128)S(1)} %get-tuple-element.65.refs_3_), channel_id=1, source_target_pairs={{0,1},{1,0},{2,3},{3,2},{4,5},{5,4},{6,7},{7,6},{8,9},{9,8},{10,11... | collective-permute-start | bytes 24584 | tf_op jit(solution)/shard_map/ppermute | solution.py:515
  9.3 3.7 %collective-permute-start.6 = (f32[8,512]{1,0:T(8,128)S(1)}, f32[8,512]{1,0:T(8,128)S(1)}, u32[]{:S(2)}, u32[]{:S(2)}) collective-permute-start(f32[8,512]{1,0:T(8,128)S(1)} %get-tuple-element.72), channel_id=1, source_target_pairs={{0,16},{16,0},{1,17},{17,1},{2,18},{18,2},{3,19},{19,3},{4,20},{20... | collective-permute-start | bytes 49160 | tf_op jit(solution)/shard_map/ppermute | solution.py:519
  11.8 1.2 %collective-permute-start.3 = (f32[8,256]{1,0:T(8,128)S(1)}, f32[8,256]{1,0:T(8,128)S(1)}, u32[]{:S(2)}, u32[]{:S(2)}) collective-permute-start(f32[8,256]{1,0:T(8,128)S(1)} %shard_map.121), channel_id=1, source_target_pairs={{0,16},{16,0},{1,17},{17,1},{2,18},{18,2},{3,19},{19,3},{4,20},{20... | collective-permute-start | bytes 24584 | tf_op jit(solution)/shard_map/ppermute | solution.py:519
  15.7 6.5 %collective-permute-start.7 = (f32[8,512]{1,0:T(8,128)S(1)}, f32[8,512]{1,0:T(8,128)S(1)}, u32[]{:S(2)}, u32[]{:S(2)}) collective-permute-start(f32[8,512]{1,0:T(8,128)S(1)} %get-tuple-element.74), channel_id=1, source_target_pairs={{0,4},{4,0},{8,12},{12,8},{1,5},{5,1},{9,13},{13,9},{2,6},{6,2},{1... | collective-permute-start | bytes 49160 | tf_op jit(solution)/shard_map/ppermute | solution.py:515
  17.3 4.9 %collective-permute-start.8 = (f32[8,512]{1,0:T(8,128)S(1)}, f32[8,512]{1,0:T(8,128)S(1)}, u32[]{:S(2)}, u32[]{:S(2)}) collective-permute-start(f32[8,512]{1,0:T(8,128)S(1)} %get-tuple-element.75), channel_id=1, source_target_pairs={{0,8},{4,12},{8,0},{12,4},{1,9},{5,13},{9,1},{13,5},{2,10},{6,14},... | collective-permute-start | bytes 49160 | tf_op jit(solution)/shard_map/ppermute | solution.py:515
  19.8 5.5 %collective-permute-start.9 = (f32[8,512]{1,0:T(8,128)S(1)}, f32[8,512]{1,0:T(8,128)S(1)}, u32[]{:S(2)}, u32[]{:S(2)}) collective-permute-start(f32[8,512]{1,0:T(8,128)S(1)} %get-tuple-element.75), channel_id=1, source_target_pairs={{0,12},{4,8},{8,4},{12,0},{1,13},{5,9},{9,5},{13,1},{2,14},{6,10},... | collective-permute-start | bytes 49160 | tf_op jit(solution)/shard_map/ppermute | solution.py:515
  27.0 8.2 %collective-permute-start.17 = (bf16[2,272,256]{2,1,0:T(8,128)(2,1)S(1)}, bf16[2,272,256]{2,1,0:T(8,128)(2,1)S(1)}, u32[]{:S(2)}, u32[]{:S(2)}) collective-permute-start(bf16[2,272,256]{2,1,0:T(8,128)(2,1)S(1)} %get-tuple-element.93), channel_id=1, source_target_pairs={{0,4},{4,0},{8,12},{12,8},{1,5},{5,1},{9,13},{13,9},{2,6},{6,2},{1... | collective-permute-start | bytes 835592 | tf_op jit(solution)/shard_map/ppermute | solution.py:515
  27.0 1.2 %collective-permute-start.10 = (f32[8,256]{1,0:T(8,128)S(1)}, f32[8,256]{1,0:T(8,128)S(1)}, u32[]{:S(2)}, u32[]{:S(2)}) collective-permute-start(f32[8,256]{1,0:T(8,128)S(1)} %get-tuple-element.84.refs_0_), channel_id=1, source_target_pairs={{0,16},{16,0},{1,17},{17,1},{2,18},{18,2},{3,19},{19,3},{4,20},{20... | collective-permute-start | bytes 24584 | tf_op jit(solution)/shard_map/ppermute | solution.py:519
  28.2 4.5 %collective-permute-start.11 = (f32[8,256]{1,0:T(8,128)S(1)}, f32[8,256]{1,0:T(8,128)S(1)}, u32[]{:S(2)}, u32[]{:S(2)}) collective-permute-start(f32[8,256]{1,0:T(8,128)S(1)} %shard_map.125.refs_3_), channel_id=1, source_target_pairs={{0,3},{1,2},{2,1},{3,0},{4,7},{5,6},{6,5},{7,4},{8,11},{9,10},{10,... | collective-permute-start | bytes 24584 | tf_op jit(solution)/shard_map/ppermute | solution.py:515
  29.7 3.7 %collective-permute-start.12 = (f32[8,256]{1,0:T(8,128)S(1)}, f32[8,256]{1,0:T(8,128)S(1)}, u32[]{:S(2)}, u32[]{:S(2)}) collective-permute-start(f32[8,256]{1,0:T(8,128)S(1)} %shard_map.125.refs_3_), channel_id=1, source_target_pairs={{0,2},{1,3},{2,0},{3,1},{4,6},{5,7},{6,4},{7,5},{8,10},{9,11},{10,... | collective-permute-start | bytes 24584 | tf_op jit(solution)/shard_map/ppermute | solution.py:515
  30.2 3.7 %collective-permute-start.13 = (f32[8,256]{1,0:T(8,128)S(1)}, f32[8,256]{1,0:T(8,128)S(1)}, u32[]{:S(2)}, u32[]{:S(2)}) collective-permute-start(f32[8,256]{1,0:T(8,128)S(1)} %shard_map.125.refs_3_), channel_id=1, source_target_pairs={{0,1},{1,0},{2,3},{3,2},{4,5},{5,4},{6,7},{7,6},{8,9},{9,8},{10,11... | collective-permute-start | bytes 24584 | tf_op jit(solution)/shard_map/ppermute | solution.py:515
  35.2 10.5 %collective-permute-start.18 = (bf16[272,256]{1,0:T(8,128)(2,1)S(1)}, bf16[272,256]{1,0:T(8,128)(2,1)S(1)}, u32[]{:S(2)}, u32[]{:S(2)}) collective-permute-start(bf16[272,256]{1,0:T(8,128)(2,1)S(1)} %get-tuple-element.96), channel_id=1, source_target_pairs={{0,8},{4,12},{8,0},{12,4},{1,9},{5,13},{9,1},{13,5},{2,10},{6,14},... | collective-permute-start | bytes 417800 | tf_op jit(solution)/shard_map/ppermute | solution.py:515
  36.2 4.4 %collective-permute-start.14 = (f32[8,512]{1,0:T(8,128)S(1)}, f32[8,512]{1,0:T(8,128)S(1)}, u32[]{:S(2)}, u32[]{:S(2)}) collective-permute-start(f32[8,512]{1,0:T(8,128)S(1)} %get-tuple-element.85), channel_id=1, source_target_pairs={{0,4},{4,0},{8,12},{12,8},{1,5},{5,1},{9,13},{13,9},{2,6},{6,2},{1... | collective-permute-start | bytes 49160 | tf_op jit(solution)/shard_map/ppermute | solution.py:515
  37.3 7.2 %collective-permute-start.15 = (f32[8,512]{1,0:T(8,128)S(1)}, f32[8,512]{1,0:T(8,128)S(1)}, u32[]{:S(2)}, u32[]{:S(2)}) collective-permute-start(f32[8,512]{1,0:T(8,128)S(1)} %get-tuple-element.86), channel_id=1, source_target_pairs={{0,8},{4,12},{8,0},{12,4},{1,9},{5,13},{9,1},{13,5},{2,10},{6,14},... | collective-permute-start | bytes 49160 | tf_op jit(solution)/shard_map/ppermute | solution.py:515
  40.2 5.5 %collective-permute-start.16 = (f32[8,512]{1,0:T(8,128)S(1)}, f32[8,512]{1,0:T(8,128)S(1)}, u32[]{:S(2)}, u32[]{:S(2)}) collective-permute-start(f32[8,512]{1,0:T(8,128)S(1)} %get-tuple-element.86), channel_id=1, source_target_pairs={{0,12},{4,8},{8,4},{12,0},{1,13},{5,9},{9,5},{13,1},{2,14},{6,10},... | collective-permute-start | bytes 49160 | tf_op jit(solution)/shard_map/ppermute | solution.py:515
  47.4 17.4 %collective-permute-start.19 = (bf16[272,256]{1,0:T(8,128)(2,1)S(1)}, bf16[272,256]{1,0:T(8,128)(2,1)S(1)}, u32[]{:S(2)}, u32[]{:S(2)}) collective-permute-start(bf16[272,256]{1,0:T(8,128)(2,1)S(1)} %get-tuple-element.99), channel_id=1, source_target_pairs={{0,12},{4,8},{8,4},{12,0},{1,13},{5,9},{9,5},{13,1},{2,14},{6,10},... | collective-permute-start | bytes 417800 | tf_op jit(solution)/shard_map/ppermute | solution.py:515
  48.1 16.7 %collective-permute-start.20 = (bf16[272,256]{1,0:T(8,128)(2,1)S(1)}, bf16[272,256]{1,0:T(8,128)(2,1)S(1)}, u32[]{:S(2)}, u32[]{:S(2)}) collective-permute-start(bf16[272,256]{1,0:T(8,128)(2,1)S(1)} %get-tuple-element.100), channel_id=1, source_target_pairs={{0,8},{4,12},{8,0},{12,4},{1,9},{5,13},{9,1},{13,5},{2,10},{6,14},... | collective-permute-start | bytes 417800 | tf_op jit(solution)/shard_map/ppermute | solution.py:515
  48.4 16.4 %collective-permute-start.21 = (bf16[272,256]{1,0:T(8,128)(2,1)S(1)}, bf16[272,256]{1,0:T(8,128)(2,1)S(1)}, u32[]{:S(2)}, u32[]{:S(2)}) collective-permute-start(bf16[272,256]{1,0:T(8,128)(2,1)S(1)} %get-tuple-element.101), channel_id=1, source_target_pairs={{0,4},{4,0},{8,12},{12,8},{1,5},{5,1},{9,13},{13,9},{2,6},{6,2},{1... | collective-permute-start | bytes 417800 | tf_op jit(solution)/shard_map/ppermute | solution.py:515
  51.8 13.6 %collective-permute-start.27 = (bf16[272,256]{1,0:T(8,128)(2,1)S(1)}, bf16[272,256]{1,0:T(8,128)(2,1)S(1)}, u32[]{:S(2)}, u32[]{:S(2)}) collective-permute-start(bf16[272,256]{1,0:T(8,128)(2,1)S(1)} %shard_map.128.refs_15_.refs_0_), channel_id=1, source_target_pairs={{0,8},{4,12},{8,0},{12,4},{1,9},{5,13},{9,1},{13,5},{2,10},{6,14},... | collective-permute-start | bytes 417800 | tf_op jit(solution)/shard_map/ppermute | solution.py:515
  51.8 1.2 %collective-permute-start.22 = (f32[8,256]{1,0:T(8,128)S(1)}, f32[8,256]{1,0:T(8,128)S(1)}, u32[]{:S(2)}, u32[]{:S(2)}) collective-permute-start(f32[8,256]{1,0:T(8,128)S(1)} %get-tuple-element.102.refs_0_), channel_id=1, source_target_pairs={{0,16},{16,0},{1,17},{17,1},{2,18},{18,2},{3,19},{19,3},{4,20},{20... | collective-permute-start | bytes 24584 | tf_op jit(solution)/shard_map/ppermute | solution.py:519
  53.0 4.5 %collective-permute-start.23 = (f32[8,256]{1,0:T(8,128)S(1)}, f32[8,256]{1,0:T(8,128)S(1)}, u32[]{:S(2)}, u32[]{:S(2)}) collective-permute-start(f32[8,256]{1,0:T(8,128)S(1)} %shard_map.130.refs_3_), channel_id=1, source_target_pairs={{0,3},{1,2},{2,1},{3,0},{4,7},{5,6},{6,5},{7,4},{8,11},{9,10},{10,... | collective-permute-start | bytes 24584 | tf_op jit(solution)/shard_map/ppermute | solution.py:515
  57.5 3.7 %collective-permute-start.24 = (f32[8,256]{1,0:T(8,128)S(1)}, f32[8,256]{1,0:T(8,128)S(1)}, u32[]{:S(2)}, u32[]{:S(2)}) collective-permute-start(f32[8,256]{1,0:T(8,128)S(1)} %shard_map.130.refs_3_), channel_id=1, source_target_pairs={{0,2},{1,3},{2,0},{3,1},{4,6},{5,7},{6,4},{7,5},{8,10},{9,11},{10,... | collective-permute-start | bytes 24584 | tf_op jit(solution)/shard_map/ppermute | solution.py:515
  61.2 3.7 %collective-permute-start.25 = (f32[8,256]{1,0:T(8,128)S(1)}, f32[8,256]{1,0:T(8,128)S(1)}, u32[]{:S(2)}, u32[]{:S(2)}) collective-permute-start(f32[8,256]{1,0:T(8,128)S(1)} %shard_map.130.refs_3_), channel_id=1, source_target_pairs={{0,1},{1,0},{2,3},{3,2},{4,5},{5,4},{6,7},{7,6},{8,9},{9,8},{10,11... | collective-permute-start | bytes 24584 | tf_op jit(solution)/shard_map/ppermute | solution.py:515
  65.4 11.7 %collective-permute-start.28 = (bf16[2,272,256]{2,1,0:T(8,128)(2,1)S(1)}, bf16[2,272,256]{2,1,0:T(8,128)(2,1)S(1)}, u32[]{:S(2)}, u32[]{:S(2)}) collective-permute-start(bf16[2,272,256]{2,1,0:T(8,128)(2,1)S(1)} %pad_maximum_fusion), channel_id=1, source_target_pairs={{0,4},{4,0},{8,12},{12,8},{1,5},{5,1},{9,13},{13,9},{2,6},{6,2},{1... | collective-permute-start | bytes 835592 | tf_op jit(solution)/shard_map/ppermute | solution.py:515
  67.1 4.5 %collective-permute-start.26 = (bf16[256,512]{1,0:T(8,128)(2,1)S(1)}, bf16[256,512]{1,0:T(8,128)(2,1)S(1)}, u32[]{:S(2)}, u32[]{:S(2)}) collective-permute-start(bf16[256,512]{1,0:T(8,128)(2,1)S(1)} %get-tuple-element.108), channel_id=1, source_target_pairs={{0,16},{16,0},{1,17},{17,1},{2,18},{18,2},{3,19},{19,3},{4,20},{20... | collective-permute-start | bytes 786440 | tf_op jit(solution)/shard_map/ppermute | solution.py:519
  67.2 11.9 %collective-permute-start.29 = (bf16[272,256]{1,0:T(8,128)(2,1)S(1)}, bf16[272,256]{1,0:T(8,128)(2,1)S(1)}, u32[]{:S(2)}, u32[]{:S(2)}) collective-permute-start(bf16[272,256]{1,0:T(8,128)(2,1)S(1)} %shard_map.133.refs_4_), channel_id=1, source_target_pairs={{0,4},{4,0},{8,12},{12,8},{1,5},{5,1},{9,13},{13,9},{2,6},{6,2},{1... | collective-permute-start | bytes 417800 | tf_op jit(solution)/shard_map/ppermute | solution.py:515
  68.4 10.7 %collective-permute-start.30 = (bf16[272,256]{1,0:T(8,128)(2,1)S(1)}, bf16[272,256]{1,0:T(8,128)(2,1)S(1)}, u32[]{:S(2)}, u32[]{:S(2)}) collective-permute-start(bf16[272,256]{1,0:T(8,128)(2,1)S(1)} %shard_map.133.refs_4_), channel_id=1, source_target_pairs={{0,8},{4,12},{8,0},{12,4},{1,9},{5,13},{9,1},{13,5},{2,10},{6,14},... | collective-permute-start | bytes 417800 | tf_op jit(solution)/shard_map/ppermute | solution.py:515
  70.9 12.1 %collective-permute-start.31 = (bf16[272,256]{1,0:T(8,128)(2,1)S(1)}, bf16[272,256]{1,0:T(8,128)(2,1)S(1)}, u32[]{:S(2)}, u32[]{:S(2)}) collective-permute-start(bf16[272,256]{1,0:T(8,128)(2,1)S(1)} %shard_map.133.refs_4_), channel_id=1, source_target_pairs={{0,12},{4,8},{8,4},{12,0},{1,13},{5,9},{9,5},{13,1},{2,14},{6,10},... | collective-permute-start | bytes 417800 | tf_op jit(solution)/shard_map/ppermute | solution.py:515
  83.0 1.4 %collective-permute-start.35 = (bf16[272,256]{1,0:T(8,128)(2,1)S(1)}, bf16[272,256]{1,0:T(8,128)(2,1)S(1)}, u32[]{:S(2)}, u32[]{:S(2)}) collective-permute-start(bf16[272,256]{1,0:T(8,128)(2,1)S(1)} %broadcast_select_fusion), channel_id=1, source_target_pairs={{0,16},{16,0},{1,17},{17,1},{2,18},{18,2},{3,19},{19,3},{4,20},{20... | collective-permute-start | bytes 417800 | tf_op jit(solution)/shard_map/ppermute | solution.py:519
  83.1 1.6 %collective-permute-start.34 = (bf16[272,256]{1,0:T(8,128)(2,1)S(1)}, bf16[272,256]{1,0:T(8,128)(2,1)S(1)}, u32[]{:S(2)}, u32[]{:S(2)}) collective-permute-start(bf16[272,256]{1,0:T(8,128)(2,1)S(1)} %broadcast_select_fusion.1), channel_id=1, source_target_pairs={{0,16},{16,0},{1,17},{17,1},{2,18},{18,2},{3,19},{19,3},{4,20},{20... | collective-permute-start | bytes 417800 | tf_op jit(solution)/shard_map/ppermute | solution.py:519
  83.7 1.4 %collective-permute-start.33 = (bf16[272,256]{1,0:T(8,128)(2,1)S(1)}, bf16[272,256]{1,0:T(8,128)(2,1)S(1)}, u32[]{:S(2)}, u32[]{:S(2)}) collective-permute-start(bf16[272,256]{1,0:T(8,128)(2,1)S(1)} %broadcast_select_fusion.2), channel_id=1, source_target_pairs={{0,16},{16,0},{1,17},{17,1},{2,18},{18,2},{3,19},{19,3},{4,20},{20... | collective-permute-start | bytes 417800 | tf_op jit(solution)/shard_map/ppermute | solution.py:519
  83.8 1.6 %collective-permute-start.32 = (bf16[272,256]{1,0:T(8,128)(2,1)S(1)}, bf16[272,256]{1,0:T(8,128)(2,1)S(1)}, u32[]{:S(2)}, u32[]{:S(2)}) collective-permute-start(bf16[272,256]{1,0:T(8,128)(2,1)S(1)} %broadcast_select_fusion.3), channel_id=1, source_target_pairs={{0,16},{16,0},{1,17},{17,1},{2,18},{18,2},{3,19},{19,3},{4,20},{20... | collective-permute-start | bytes 417800 | tf_op jit(solution)/shard_map/ppermute | solution.py:519

commit v3 on v2

--- a/solution.py
+++ b/solution.py
@@ -153,9 +153,14 @@
     return carry
 
 
-def send_rows(rank, ahead, behind, near_ref, far_ref):
-    near_ref[...] = jnp.where(jnp.bitwise_and(rank, 1) == 0, ahead, behind)
-    far_ref[...] = jnp.where(jnp.bitwise_and(rank, 2) == 0, ahead, behind)
+def pair_ends_kernel(micro, seq_at, own_ref, near_ref, out_ref):
+    own, near = own_ref[...], near_ref[...]
+    odd = jnp.bitwise_and(seq_at[0], 1) == 1
+    first = jnp.where(odd, near, own)
+    last = jnp.where(odd, own, near)
+    state = last[micro : 2 * micro] + last[:micro] * first[micro : 2 * micro]
+    grad = first[2 * micro :] + first[:micro] * last[2 * micro :]
+    out_ref[...] = jnp.where(jnp.bitwise_and(seq_at[0], 2) == 0, state, grad)
 
 
 def head_columns(head, width):
@@ -175,7 +180,7 @@
     decay_ref, p1_ref, p2_ref, p3_ref, p4_ref = (factor_ref.at[k] for k in range(5))
     fdecay_ref, fstate_ref, rdecay_ref = (block_ref.at[k] for k in range(3))
     if layer:
-        rgrad_ref, behind_ref, near_ref, far_ref, *refs = refs
+        rgrad_ref, *refs = refs
     prer_ref, prei_ref = refs
     width = wk_ref.shape[2]
     heads = xk_ref.shape[1] // width
@@ -240,8 +245,7 @@
                 leaving = reverse_blocks(decay_ref, up_ref, base, cols, tok_rows, width)
                 rdecay, rgrad = sublane_scan(product, leaving, True)
                 rgrad_ref[block_rows, cols] = rgrad
-                behind_ref[pl.ds(m, 1), cols] = fdecay[7:8]
-                behind_ref[pl.ds(micro_count + m, 1), cols] = rgrad[0:1]
+                ahead_ref[pl.ds(2 * micro_count + m, 1), cols] = rgrad[0:1]
             else:
                 rdecay, _unused = sublane_scan(product, product, True)
             rdecay_ref[block_rows, cols] = rdecay
@@ -251,8 +255,6 @@
         return 0
 
     lax.fori_loop(0, heads, per_head, 0)
-    if layer:
-        send_rows(seq_at[0], ahead_ref[...], behind_ref[...], near_ref, far_ref)
 
 
 def late_kernel(
@@ -260,7 +262,7 @@
     inv_ref, factor_ref, ahead_ref, *refs
 ):
     crosses = refs[:cross_count]
-    early_ref, rgrad_ref, behind_ref, near_ref, far_ref, scale_ref = refs[cross_count:]
+    early_ref, rgrad_ref, pay_ref, scale_ref = refs[cross_count:]
     decay_ref = factor_ref.at[0]
     width = 256
     column = to_column([part[...] for part in crosses]) / full_width
@@ -288,24 +290,14 @@
                 product = product * decay[8:] * decay[:8]
             _, rgrad = sublane_scan(product, carry, True)
             rgrad_ref[pl.ds(pl.multiple_of(m * 8, 8), 8), cols] = rgrad
-            behind_ref[pl.ds(m, 1), cols] = ahead_ref[pl.ds(m, 1), cols]
-            behind_ref[pl.ds(micro_count + m, 1), cols] = rgrad[0:1]
+            pay_ref[pl.ds(2 * micro_count + m, 1), cols] = rgrad[0:1]
             return 0
 
         lax.fori_loop(0, micro_count, per_micro, 0)
         return 0
 
+    pay_ref[: 2 * micro_count, :] = ahead_ref[...]
     lax.fori_loop(0, part_ref.shape[1] // width, per_head, 0)
-    send_rows(seq_at[0], ahead_ref[...], behind_ref[...], near_ref, far_ref)
-
-
-def ranked(refs, rank, at):
-    if len(refs) == 1:
-        return refs[0][at]
-    chosen = refs[0][...]
-    for k in range(2, len(refs) + 1):
-        chosen = jnp.where(jnp.bitwise_xor(rank, at) == k, refs[k - 1][...], chosen)
-    return chosen
 
 
 def backward_kernel(
@@ -325,20 +317,24 @@
     rank = seq_at[0]
     micro = micro_count
     own = section_at[0] == layer
-    behind = 2 * micro if pay_count == 1 else 0
-
+    decays, states, grads = (slice(k * micro, (k + 1) * micro) for k in range(3))
     state_in = jnp.zeros(enter_ref.shape, F32)
     grad_in = jnp.zeros(leave_ref.shape, F32)
-    for at in range(seq_count - 1):
-        pay = ranked(pays, rank, at)
-        state_in = jnp.where(
-            at < rank, pay[micro : 2 * micro] + pay[:micro] * state_in, state_in
-        )
-    for at in reversed(range(1, seq_count)):
-        pay = ranked(pays, rank, at)[behind:]
-        grad_in = jnp.where(
-            at > rank, pay[micro : 2 * micro] + pay[:micro] * grad_in, grad_in
-        )
+    if direct:
+        near, far = pays[0][...], pays[1][...]
+        late = jnp.bitwise_and(rank, 2) > 0
+        odd = jnp.bitwise_and(rank, 1) > 0
+        state_in = jnp.where(late, far, state_in)
+        state_in = jnp.where(odd, near[states] + near[decays] * state_in, state_in)
+        grad_in = jnp.where(late, grad_in, far)
+        grad_in = jnp.where(odd, grad_in, near[grads] + near[decays] * grad_in)
+    else:
+        for at in range(seq_count - 1):
+            pay = pays[0][at]
+            state_in = jnp.where(at < rank, pay[states] + pay[decays] * state_in, state_in)
+        for at in reversed(range(1, seq_count)):
+            pay = pays[0][at]
+            grad_in = jnp.where(at > rank, pay[grads] + pay[decays] * grad_in, grad_in)
     enter_ref[...] = state_in
     leave_ref[...] = grad_in
     fold_ref[...] = jnp.zeros(fold_ref.shape, F32)
@@ -483,32 +479,31 @@
 
 def weights_kernel(units, scale, section_at, unit_at, *refs):
     tops, lows, others = refs[:units], refs[units : 2 * units], refs[2 * units : 3 * units]
-    rate_ref, input_ref, vector_ref = refs[3 * units :]
-    head = pl.program_id(0)
+    rate_ref, input_ref, vector_ref, ordered_ref, wide_ref, rows_ref, sems = refs[3 * units :]
     size = rate_ref.shape[1]
     half_heads = units // 2
     section = section_at[0]
-    mine = head // half_heads == section
-    local = head % half_heads
-    for gate, out_ref in enumerate((rate_ref, input_ref)):
-        index = jnp.bitwise_xor(2 * local + gate, unit_at[0])
-        for k in range(units):
-            here = index == k
-            sources = (
-                (jnp.logical_and(mine, section == 1), tops[k]),
-                (jnp.logical_and(mine, section == 0), lows[k]),
-                (jnp.logical_not(mine), others[k]),
-            )
-            for wanted, source in sources:
-
-                @pl.when(jnp.logical_and(here, wanted))
-                def _(source=source, gate=gate, out_ref=out_ref):
-                    out_ref[0] = source[:size, :].astype(F32) * scale
-                    rows = source[size:, :].astype(F32) * scale
-                    if gate == 0:
-                        vector_ref[:, 0, :] = rows[:3]
-                    else:
-                        vector_ref[:, 0, :] += rows[:3]
+    mine = section * units
+    for k in range(units):
+        place = jnp.bitwise_xor(unit_at[0], k)
+        ordered_ref[mine + place] = jnp.where(section == 1, tops[k][...], lows[k][...])
+        ordered_ref[units - mine + place] = others[k][...]
+    copies = []
+    for index in range(2 * units):
+        head, gate = index // 2, index % 2
+        wide_ref[index] = ordered_ref[index, :size, :].astype(F32) * scale
+        target = (rate_ref, input_ref)[gate].at[head]
+        copies.append(pltpu.make_async_copy(wide_ref.at[index], target, sems.at[index]))
+        copies[-1].start()
+    for head in range(2 * half_heads):
+        rows = ordered_ref[2 * head, size:, :].astype(F32)
+        rows = rows + ordered_ref[2 * head + 1, size:, :].astype(F32)
+        for k in range(3):
+            rows_ref[k, :, head * size : (head + 1) * size] = rows[k : k + 1] * scale
+    copies.append(pltpu.make_async_copy(rows_ref, vector_ref, sems.at[2 * units]))
+    copies[-1].start()
+    for copy in copies:
+        copy.wait()
 
 
 def xor_moves(value, axis, k):
@@ -527,10 +522,22 @@
     return [xor_moves(value, "chan", k) for k in reversed(range(1, count))] + [value]
 
 
-def seq_pays(ahead, behind, near, far):
+def seq_pays(pay, seq_at, micro):
     if lax.axis_size("seq") != DIRECT_RANKS:
-        return [lax.all_gather(jnp.concatenate([ahead, behind], axis=0), "seq")]
-    return [xor_moves(far, "seq", 3), xor_moves(far, "seq", 2), xor_moves(near, "seq", 1)][::-1]
+        return [lax.all_gather(pay, "seq")]
+    near = xor_moves(pay, "seq", 1)
+    ends = pl.pallas_call(
+        functools.partial(pair_ends_kernel, micro),
+        in_specs=[
+            pl.BlockSpec(memory_space=pltpu.SMEM),
+            pl.BlockSpec(memory_space=pltpu.VMEM),
+            pl.BlockSpec(memory_space=pltpu.VMEM),
+        ],
+        out_shape=jax.ShapeDtypeStruct((micro, pay.shape[1]), F32),
+        compiler_params=params(),
+        cost_estimate=cost(0, 8 * pay.size),
+    )(seq_at, pay, near)
+    return [near, xor_moves(ends, "seq", 2)]
 
 
 def add_units(value, *others):
@@ -630,7 +637,6 @@
 
     big = shape((rows, half))
     blocks = shape((micro * 8, half))
-    pay = shape((2 * micro, half))
 
     def forward(layer, beside):
         return call(
@@ -642,8 +648,14 @@
                 *own_squares, other_squares, opened, x_keep, x_got, w_keep, w_got, v_keep, v_got,
                 beside,
             ],
-            [half_x, shape((5, rows, half)), shape((3, micro * 8, half)), pay, shape((rows, 128))]
-            + ([blocks] + [pay] * 3) * layer,
+            [
+                half_x,
+                shape((5, rows, half)),
+                shape((3, micro * 8, half)),
+                shape(((2 + layer) * micro, half)),
+                shape((rows, 128)),
+            ]
+            + [blocks] * layer,
             [((rows, size), F32)] * 2,
             flops=4 * rows * size * half,
             size_bytes=24 * rows * half,
@@ -682,40 +694,43 @@
     def chip_sum(value):
         return add_units(value, swap_sections(value))
 
-    *top, top_rgrad, behind, near, far = forward(1, upstream)
-    pays = seq_pays(top[3], behind, near, far)
+    *top, top_rgrad = forward(1, upstream)
+    pays = seq_pays(top[3], seq_at, micro)
     low = forward(0, top[1])
     part, cross, *top_parts = backward(1, pays, upstream, top, top_rgrad, low[3])
-    parts = chan_parts(chip_sum(cross))
+    cross = chip_sum(cross)
+    parts = chan_parts(cross)
     if direct:
+        top_parts[1] = after(top_parts[1], cross)
         arrived = xor_moves(top_parts[1], "seq", 1)
-    early, low_rgrad, behind, near, far = call(
+    early, low_rgrad, low_pay = call(
         functools.partial(late_kernel, micro, tok_rows, full_width, len(parts)),
         [seq_at, section_at],
         [part, x_keep, x_got, top[4], low[1], low[3], *parts],
-        [half_x, blocks] + [pay] * 3,
+        [half_x, blocks, shape((3 * micro, half))],
         [((rows, 128), F32)],
         flops=8 * rows * half,
         size_bytes=12 * rows * half,
     )
-    pays = seq_pays(low[3], behind, near, far)
+    pays = seq_pays(low_pay, seq_at, micro)
     if direct:
-        own_pair, far_pair = add_pairs(top_parts[0], after(arrived, near))
+        own_pair, far_pair = add_pairs(top_parts[0], after(arrived, pays[0]))
         arrived = xor_moves(far_pair, "seq", 2)
         top_own = add_units(own_pair, after(arrived, *pays))
         top_far = xor_moves(top_own, "seq", 2)
     part, cross, *low_parts = backward(
-        0, pays, early, low, low_rgrad, top_own if direct else behind
-    )
-    parts = chan_parts(chip_sum(cross))
+        0, pays, early, low, low_rgrad, top_own if direct else low_pay
+    )
+    parts = chan_parts(after(chip_sum(cross), top_far) if direct else chip_sum(cross))
     if direct:
         place = lax.axis_index("seq")
         low_arrived = [xor_moves(low_parts[k], "seq", k) for k in (3, 2, 1)]
         low_arrived, parts = lax.optimization_barrier((low_arrived, parts))
         low_own = add_units(low_parts[0], *low_arrived)
         low_units = [low_own] + [xor_moves(low_own, "seq", k) for k in (1, 2, 3)]
-        pair = xor_moves(jnp.stack([top_own, after(top_far, low_own)]), "seq", 1)
-        top_units = [top_own, pair[0], top_far, pair[1]]
+        top_near = xor_moves(top_own, "seq", 1)
+        top_last = xor_moves(top_far, "seq", 1)
+        top_units = [top_own, top_near, top_far, top_last]
     else:
         place = jnp.zeros((), jnp.int32)
         top_units, low_units = (
@@ -737,22 +752,24 @@
         join_kernel, [section_at], [grads_keep, swap_sections(grads_send)],
         shape((rows, chan_width), BF16), size_bytes=4 * rows * chan_width,
     )
-    if direct:
-        grads, top_units, low_units = lax.optimization_barrier((grads, top_units, low_units))
 
     other_units = [
         swap_sections(jnp.where(section == 1, b, a)) for a, b in zip(top_units, low_units)
     ]
-    out_block = pl.BlockSpec((1, size, size), lambda h: (h, 0, 0))
     rate_total, input_total, vector = pl.pallas_call(
         functools.partial(weights_kernel, heads, grad_scale),
-        grid=(heads,),
         in_specs=[smem, smem] + [whole] * (3 * heads),
-        out_specs=[out_block, out_block, pl.BlockSpec((3, 1, size), lambda h: (0, 0, h))],
+        out_specs=[pl.BlockSpec(memory_space=pltpu.HBM)] * 3,
         out_shape=[
             shape((heads, size, size)),
             shape((heads, size, size)),
             shape((3, 1, chan_width)),
+        ],
+        scratch_shapes=[
+            pltpu.VMEM((2 * heads, size + VECTOR_ROWS, size), BF16),
+            pltpu.VMEM((2 * heads, size, size), F32),
+            pltpu.VMEM((3, 1, chan_width), F32),
+            pltpu.SemaphoreType.DMA((2 * heads + 1,)),
         ],
         compiler_params=params(),
         cost_estimate=cost(0, 8 * heads * size * size),

time: 87.6 us -> 83.3 us (0.951)
  waiting for transfers between devices: 35.9 us -> 32.9 us
  Pallas kernels: 15.7 us -> 13.9 us
    ppermute x25 -> x24, waiting for transfers between devices: 31.4 us -> 28.9 us  [xor_moves(): lax.ppermute(value, axis, [(i, i ^ k) for i in range(lax.axis_size(axis))])]
    pallas_call x8, Pallas kernels: 13.4 us -> 12.2 us  [call(): pl.pallas_call(kernel, in_specs=[smem] * len(scalars) + (specs or [whole]...]
    ppermute x25 -> x24, starting transfers between devices: 32.9 us -> 33.7 us  [xor_moves(): lax.ppermute(value, axis, [(i, i ^ k) for i in range(lax.axis_size(axis))])]
    pallas_call x1 -> x3, Pallas kernels: 2.11 us -> 1.54 us  [the longest x1 1.51 us: on_device(): pl.pallas_call(functools.partial(weights_kernel, heads, grad_scale), in_s...]
  transfers between devices with their start and end apart: 36 -> 35, of which waited for: 23 -> 18; matrix products, arithmetic and copies ran while one was open for 0% -> 0% of each run, Pallas kernels for 6% -> 7%
where the time goes in v3:
time: 83.3 us; the launch traced here: 83.1 us
  starting transfers between devices  35.5 us (43%)
  waiting for transfers between devices  32.9 us (39%)
  Pallas kernels  13.9 us (17%)
    ppermute x24, starting transfers between devices, xor_moves(): lax.ppermute(value, axis, [(i, i ^ k) for i in range(lax.axis_size(axis))])  33.7 us
    ppermute x24, waiting for transfers between devices, xor_moves(): lax.ppermute(value, axis, [(i, i ^ k) for i in range(lax.axis_size(axis))])  28.9 us
    pallas_call x8, Pallas kernels, call(): pl.pallas_call(kernel, in_specs=[smem] * len(scalars) + (specs or [whole]...  12.2 us
    ppermute x11, waiting for transfers between devices, swap_sections(): return lax.ppermute(value, 'section', [(0, 1), (1, 0)])  4.01 us
    ppermute x11, starting transfers between devices, swap_sections(): return lax.ppermute(value, 'section', [(0, 1), (1, 0)])  1.79 us
  transfers between devices with their start and end apart: 35, of which 18 were waited for; matrix products, arithmetic and copies ran while one was open for 0% of the time, Pallas kernels for 7%

profile of v3, /device:TPU:0, one launch (start us, length us, event | category | flops | bytes accessed | tf_op | source)
XLA Modules:
  0.0 83.1 jit_solution(12054063637967422669)
XLA Ops:
  0.6 2.5 %shard_map.120 = (f32[8,256]{1,0:T(8,128)S(1)}, bf16[256,512]{1,0:T(8,128)(2,1)S(1)}, bf16[256,512]{1,0:T(8,128)(2,1)S(1)}, bf16[256,512]{1,0:T(8,128)(2,1)S(1)}...) custom-call(s32[1]{0:T(128)} %bitcast.section_at, ...), custom_call_target="tpu_custom_call" | custom-call | flops 268435456 | bytes 3145728 | tf_op jit(solution)/shard_map/pallas_call | solution.py:598
  3.2 0.5 collective-permute-start.5
  3.8 3.9 %collective-permute-start = (f32[8,256]{1,0:T(8,128)S(1)}, f32[8,256]{1,0:T(8,128)S(1)}, u32[]{:S(2)}, u32[]{:S(2)}) collective-permute-start(f32[8,256]{1,0:T(8,128)S(1)} %get-tuple-element.55.refs_3_), channel_id=1, source_target_pairs={{0,3},{1,2},{2,1},{3,0},{4,7},{5,6},{6,5},{7,4},{8,11},{9,10},{10,... | collective-permute-start | bytes 24584 | tf_op jit(solution)/shard_map/ppermute | solution.py:510
  7.7 0.5 collective-permute-start.1
  8.2 1.1 %collective-permute-done.refs_0_ = f32[8,256]{1,0:T(8,128)S(1)} collective-permute-done((f32[8,256]{1,0:T(8,128)S(1)}, f32[8,256]{1,0:T(8,128)S(1)}, u32[]{:S(2)}, u32[]{:S(2)}) %collective-permute-start) | collective-permute-done | bytes 8224 | tf_op jit(solution)/shard_map/ppermute | solution.py:510
  9.3 2.0 %collective-permute-done.1.refs_1_ = f32[8,256]{1,0:T(8,128)S(1)} collective-permute-done((f32[8,256]{1,0:T(8,128)S(1)}, f32[8,256]{1,0:T(8,128)S(1)}, u32[]{:S(2)}, u32[]{:S(2)}) %collective-permute-start.1) | collective-permute-done | bytes 8224 | tf_op jit(solution)/shard_map/ppermute | solution.py:510
  11.3 0.5 collective-permute-done.2.refs_2_
  11.8 1.2 %collective-permute-done.3.refs_4_ = f32[8,256]{1,0:T(8,128)S(1)} collective-permute-done((f32[8,256]{1,0:T(8,128)S(1)}, f32[8,256]{1,0:T(8,128)S(1)}, u32[]{:S(2)}, u32[]{:S(2)}) %collective-permute-start.3) | collective-permute-done | bytes 8224 | tf_op jit(solution)/shard_map/ppermute | solution.py:514
  13.0 2.0 %shard_map.122 = (bf16[256,512]{1,0:T(8,128)(2,1)S(1)}, f32[5,256,512]{2,1,0:T(8,128)S(1)}, f32[3,32,512]{2,1,0:T(8,128)S(1)}, f32[12,512]{1,0:T(8,128)S(1)}, f3...) custom-call(s32[1]{0:T(128)} %bitcast.1.seq_at.unit_at, s32[1]{0:T(128)} %bitcast.section_at, ...), custom_call_target="tpu_custom_call" | custom-call | flops 134217728 | bytes 3145728 | tf_op jit(solution)/shard_map/pallas_call | solution.py:598
  15.1 1.6 %collective-permute-start.7 = (f32[12,512]{1,0:T(8,128)S(1)}, f32[12,512]{1,0:T(8,128)S(1)}, u32[]{:S(2)}, u32[]{:S(2)}) collective-permute-start(f32[12,512]{1,0:T(8,128)S(1)} %get-tuple-element.64.own_ref), channel_id=1, source_target_pairs={{0,4},{4,0},{8,12},{12,8},{1,5},{5,1},{9,13},{13,9},{2,6},{6,2},{1... | collective-permute-start | bytes 73736 | tf_op jit(solution)/shard_map/ppermute | solution.py:510
  16.7 2.3 %collective-permute-done.7.near_ref.refs_0_ = f32[12,512]{1,0:T(8,128)S(1)} collective-permute-done((f32[12,512]{1,0:T(8,128)S(1)}, f32[12,512]{1,0:T(8,128)S(1)}, u32[]{:S(2)}, u32[]{:S(2)}) %collective-permute-start.7) | collective-permute-done | bytes 24608 | tf_op jit(solution)/shard_map/ppermute | solution.py:510
  19.1 2.6 %collective-permute-start.8 = (f32[4,512]{1,0:T(4,128)S(1)}, f32[4,512]{1,0:T(4,128)S(1)}, u32[]{:S(2)}, u32[]{:S(2)}) collective-permute-start(f32[4,512]{1,0:T(4,128)S(1)} %shard_map.123), channel_id=1, source_target_pairs={{0,8},{4,12},{8,0},{12,4},{1,9},{5,13},{9,1},{13,5},{2,10},{6,14},... | collective-permute-start | bytes 24584 | tf_op jit(solution)/shard_map/ppermute | solution.py:510
  21.7 2.1 %shard_map.124 = (bf16[256,512]{1,0:T(8,128)(2,1)S(1)}, f32[5,256,512]{2,1,0:T(8,128)S(1)}, f32[3,32,512]{2,1,0:T(8,128)S(1)}, f32[8,512]{1,0:T(8,128)S(1)}, f32[256,128]{1,0:T(8,128)S(1)}) custom-call(s32[1]{0:T(128)} %bitcast.1.seq_at.unit_at, s32[1]{0:T(128)} %bitcast.section_at, f32[8,256]{1,0:T(8,128)S(1)} %collective-permute-done.refs_0_, ...), custom_call_target="tpu_custom_call" | custom-call | flops 134217728 | bytes 3145728 | tf_op jit(solution)/shard_map/pallas_call | solution.py:598
  23.8 1.6 %shard_map.125 = (f32[256,512]{1,0:T(8,128)S(1)}, f32[8,256]{1,0:T(8,128)S(1)}, bf16[2,272,256]{2,1,0:T(8,128)(2,1)S(1)}, bf16[2,272,256]{2,1,0:T(8,128)(2,1)S(1)}) custom-call(s32[1]{0:T(128)} %bitcast.1.seq_at.unit_at, s32[1]{0:T(128)} %bitcast.section_at, f32[12,512]{1,0:T(8,128)S(1)} %collective-permute-done.7.near_ref.refs_0_, ...), custom_call_target="tpu_custom_call" | custom-call | flops 268435456 | bytes 3932160 | tf_op jit(solution)/shard_map/pallas_call | solution.py:598
  25.4 1.2 %collective-permute-done.9.refs_1_ = f32[8,256]{1,0:T(8,128)S(1)} collective-permute-done((f32[8,256]{1,0:T(8,128)S(1)}, f32[8,256]{1,0:T(8,128)S(1)}, u32[]{:S(2)}, u32[]{:S(2)}) %collective-permute-start.9) | collective-permute-done | bytes 8224 | tf_op jit(solution)/shard_map/ppermute | solution.py:514
  26.6 1.6 %collective-permute-start.15 = (bf16[2,272,256]{2,1,0:T(8,128)(2,1)S(1)}, bf16[2,272,256]{2,1,0:T(8,128)(2,1)S(1)}, u32[]{:S(2)}, u32[]{:S(2)}) collective-permute-start(bf16[2,272,256]{2,1,0:T(8,128)(2,1)S(1)} %get-tuple-element.82), channel_id=1, source_target_pairs={{0,4},{4,0},{8,12},{12,8},{1,5},{5,1},{9,13},{13,9},{2,6},{6,2},{1... | collective-permute-start | bytes 835592 | tf_op jit(solution)/shard_map/ppermute | solution.py:510
  28.2 1.5 %collective-permute-start.10 = (f32[8,256]{1,0:T(8,128)S(1)}, f32[8,256]{1,0:T(8,128)S(1)}, u32[]{:S(2)}, u32[]{:S(2)}) collective-permute-start(f32[8,256]{1,0:T(8,128)S(1)} %shard_map.126.refs_3_), channel_id=1, source_target_pairs={{0,3},{1,2},{2,1},{3,0},{4,7},{5,6},{6,5},{7,4},{8,11},{9,10},{10,... | collective-permute-start | bytes 24584 | tf_op jit(solution)/shard_map/ppermute | solution.py:510
  29.6 0.5 collective-permute-start.11
  30.2 1.5 %collective-permute-start.12 = (f32[8,256]{1,0:T(8,128)S(1)}, f32[8,256]{1,0:T(8,128)S(1)}, u32[]{:S(2)}, u32[]{:S(2)}) collective-permute-start(f32[8,256]{1,0:T(8,128)S(1)} %shard_map.126.refs_3_), channel_id=1, source_target_pairs={{0,1},{1,0},{2,3},{3,2},{4,5},{5,4},{6,7},{7,6},{8,9},{9,8},{10,11... | collective-permute-start | bytes 24584 | tf_op jit(solution)/shard_map/ppermute | solution.py:510
  31.6 1.1 %collective-permute-done.10.refs_0_ = f32[8,256]{1,0:T(8,128)S(1)} collective-permute-done((f32[8,256]{1,0:T(8,128)S(1)}, f32[8,256]{1,0:T(8,128)S(1)}, u32[]{:S(2)}, u32[]{:S(2)}) %collective-permute-start.10) | collective-permute-done | bytes 8224 | tf_op jit(solution)/shard_map/ppermute | solution.py:510
  32.7 0.6 collective-permute-done.11.refs_1_
  33.3 0.5 collective-permute-done.12.refs_2_
  33.8 0.7 shard_map.127
  34.5 0.5 collective-permute-start.13
  35.0 3.5 %collective-permute-done.13.near_ref.refs_0_ = f32[12,512]{1,0:T(8,128)S(1)} collective-permute-done((f32[12,512]{1,0:T(8,128)S(1)}, f32[12,512]{1,0:T(8,128)S(1)}, u32[]{:S(2)}, u32[]{:S(2)}) %collective-permute-start.13) | collective-permute-done | bytes 24608 | tf_op jit(solution)/shard_map/ppermute | solution.py:510
  38.6 2.8 %collective-permute-start.16 = (bf16[272,256]{1,0:T(8,128)(2,1)S(1)}, bf16[272,256]{1,0:T(8,128)(2,1)S(1)}, u32[]{:S(2)}, u32[]{:S(2)}) collective-permute-start(bf16[272,256]{1,0:T(8,128)(2,1)S(1)} %get-tuple-element.85), channel_id=1, source_target_pairs={{0,8},{4,12},{8,0},{12,4},{1,9},{5,13},{9,1},{13,5},{2,10},{6,14},... | collective-permute-start | bytes 417800 | tf_op jit(solution)/shard_map/ppermute | solution.py:510
  41.6 4.5 %collective-permute-done.14.refs_1_ = f32[4,512]{1,0:T(4,128)S(1)} collective-permute-done((f32[4,512]{1,0:T(4,128)S(1)}, f32[4,512]{1,0:T(4,128)S(1)}, u32[]{:S(2)}, u32[]{:S(2)}) %collective-permute-start.14) | collective-permute-done | bytes 8224 | tf_op jit(solution)/shard_map/ppermute | solution.py:510
  46.2 2.0 %collective-permute-start.21 = (bf16[272,256]{1,0:T(8,128)(2,1)S(1)}, bf16[272,256]{1,0:T(8,128)(2,1)S(1)}, u32[]{:S(2)}, u32[]{:S(2)}) collective-permute-start(bf16[272,256]{1,0:T(8,128)(2,1)S(1)} %shard_map.130.refs_14_.refs_0_), channel_id=1, source_target_pairs={{0,8},{4,12},{8,0},{12,4},{1,9},{5,13},{9,1},{13,5},{2,10},{6,14},... | collective-permute-start | bytes 417800 | tf_op jit(solution)/shard_map/ppermute | solution.py:510
  48.2 1.6 %shard_map.131 = (f32[256,512]{1,0:T(8,128)S(1)}, f32[8,256]{1,0:T(8,128)S(1)}, bf16[272,256]{1,0:T(8,128)(2,1)S(1)}, bf16[272,256]{1,0:T(8,128)(2,1)S(1)}, bf16...) custom-call(s32[1]{0:T(128)} %bitcast.1.seq_at.unit_at, s32[1]{0:T(128)} %bitcast.section_at, ...), custom_call_target="tpu_custom_call" | custom-call | flops 268435456 | bytes 3932160 | tf_op jit(solution)/shard_map/pallas_call | solution.py:598
  49.7 2.4 %collective-permute-start.17 = (bf16[272,256]{1,0:T(8,128)(2,1)S(1)}, bf16[272,256]{1,0:T(8,128)(2,1)S(1)}, u32[]{:S(2)}, u32[]{:S(2)}) collective-permute-start(bf16[272,256]{1,0:T(8,128)(2,1)S(1)} %get-tuple-element.88), channel_id=1, source_target_pairs={{0,12},{4,8},{8,4},{12,0},{1,13},{5,9},{9,5},{13,1},{2,14},{6,10},... | collective-permute-start | bytes 417800 | tf_op jit(solution)/shard_map/ppermute | solution.py:510
  52.2 2.0 %collective-permute-start.18 = (bf16[272,256]{1,0:T(8,128)(2,1)S(1)}, bf16[272,256]{1,0:T(8,128)(2,1)S(1)}, u32[]{:S(2)}, u32[]{:S(2)}) collective-permute-start(bf16[272,256]{1,0:T(8,128)(2,1)S(1)} %get-tuple-element.89), channel_id=1, source_target_pairs={{0,8},{4,12},{8,0},{12,4},{1,9},{5,13},{9,1},{13,5},{2,10},{6,14},... | collective-permute-start | bytes 417800 | tf_op jit(solution)/shard_map/ppermute | solution.py:510
  54.2 1.2 %collective-permute-done.20.refs_1_ = f32[8,256]{1,0:T(8,128)S(1)} collective-permute-done((f32[8,256]{1,0:T(8,128)S(1)}, f32[8,256]{1,0:T(8,128)S(1)}, u32[]{:S(2)}, u32[]{:S(2)}) %collective-permute-start.20) | collective-permute-done | bytes 8224 | tf_op jit(solution)/shard_map/ppermute | solution.py:514
  55.4 4.4 %collective-permute-done.21.refs_2_ = bf16[272,256]{1,0:T(8,128)(2,1)S(1)} collective-permute-done((bf16[272,256]{1,0:T(8,128)(2,1)S(1)}, bf16[272,256]{1,0:T(8,128)(2,1)S(1)}, u32[]{:S(2)}, u32[]{:S(2)}) %collective-permute-start.21) | collective-permute-done | bytes 139296 | tf_op jit(solution)/shard_map/ppermute | solution.py:510
  59.8 2.4 %collective-permute-start.22 = (f32[8,256]{1,0:T(8,128)S(1)}, f32[8,256]{1,0:T(8,128)S(1)}, u32[]{:S(2)}, u32[]{:S(2)}) collective-permute-start(f32[8,256]{1,0:T(8,128)S(1)} %shard_map.132.refs_3_), channel_id=1, source_target_pairs={{0,3},{1,2},{2,1},{3,0},{4,7},{5,6},{6,5},{7,4},{8,11},{9,10},{10,... | collective-permute-start | bytes 24584 | tf_op jit(solution)/shard_map/ppermute | solution.py:510
  62.2 0.5 collective-permute-start.23
  62.7 0.6 collective-permute-start.24
  63.3 0.8 collective-permute-done.18.refs_2_
  64.1 0.5 collective-permute-start.26
  64.6 1.5 %collective-permute-start.27 = (bf16[272,256]{1,0:T(8,128)(2,1)S(1)}, bf16[272,256]{1,0:T(8,128)(2,1)S(1)}, u32[]{:S(2)}, u32[]{:S(2)}) collective-permute-start(bf16[272,256]{1,0:T(8,128)(2,1)S(1)} %collective-permute-done.21.refs_2_), channel_id=1, source_target_pairs={{0,4},{4,0},{8,12},{12,8},{1,5},{5,1},{9,13},{13,9},{2,6},{6,2},{1... | collective-permute-start | bytes 417800 | tf_op jit(solution)/shard_map/ppermute | solution.py:510
  66.5 2.4 %collective-permute-start.30 = (bf16[272,256]{1,0:T(8,128)(2,1)S(1)}, bf16[272,256]{1,0:T(8,128)(2,1)S(1)}, u32[]{:S(2)}, u32[]{:S(2)}) collective-permute-start(bf16[272,256]{1,0:T(8,128)(2,1)S(1)} %shard_map.135.refs_4_), channel_id=1, source_target_pairs={{0,12},{4,8},{8,4},{12,0},{1,13},{5,9},{9,5},{13,1},{2,14},{6,10},... | collective-permute-start | bytes 417800 | tf_op jit(solution)/shard_map/ppermute | solution.py:510
  68.8 2.1 %collective-permute-start.28 = (bf16[272,256]{1,0:T(8,128)(2,1)S(1)}, bf16[272,256]{1,0:T(8,128)(2,1)S(1)}, u32[]{:S(2)}, u32[]{:S(2)}) collective-permute-start(bf16[272,256]{1,0:T(8,128)(2,1)S(1)} %shard_map.135.refs_4_), channel_id=1, source_target_pairs={{0,4},{4,0},{8,12},{12,8},{1,5},{5,1},{9,13},{13,9},{2,6},{6,2},{1... | collective-permute-start | bytes 417800 | tf_op jit(solution)/shard_map/ppermute | solution.py:510
  70.9 0.8 shard_map.133
  71.7 6.0 %collective-permute-done.27.refs_3_ = bf16[272,256]{1,0:T(8,128)(2,1)S(1)} collective-permute-done((bf16[272,256]{1,0:T(8,128)(2,1)S(1)}, bf16[272,256]{1,0:T(8,128)(2,1)S(1)}, u32[]{:S(2)}, u32[]{:S(2)}) %collective-permute-start.27) | collective-permute-done | bytes 139296 | tf_op jit(solution)/shard_map/ppermute | solution.py:510
  77.8 0.5 collective-permute-start.25
  78.3 1.3 %collective-permute-done.29.refs_6_ = bf16[272,256]{1,0:T(8,128)(2,1)S(1)} collective-permute-done((bf16[272,256]{1,0:T(8,128)(2,1)S(1)}, bf16[272,256]{1,0:T(8,128)(2,1)S(1)}, u32[]{:S(2)}, u32[]{:S(2)}) %collective-permute-start.29) | collective-permute-done | bytes 139296 | tf_op jit(solution)/shard_map/ppermute | solution.py:510
  79.6 0.6 collective-permute-start.33
  80.3 0.8 %shard_map.134 = bf16[256,1024]{1,0:T(8,128)(2,1)} custom-call(s32[1]{0:T(128)} %bitcast.section_at, bf16[256,512]{1,0:T(8,128)(2,1)S(1)} %get-tuple-element.97.keep_ref, bf16[256,512]{1,0:T(8,128)(2,1)S(1)} %collective-permute-done.25.arrived_ref), custom_call_target="tpu_custom_call" | custom-call | bytes 1048576 | tf_op jit(solution)/shard_map/pallas_call | solution.py:598
  81.6 1.5 %shard_map.136 = (f32[4,256,256]{2,1,0:T(8,128)}, f32[4,256,256]{2,1,0:T(8,128)}, f32[3,1,1024]{2,1,0:T(1,128)}) custom-call(s32[1]{0:T(128)} %bitcast.section_at, s32[1]{0:T(128)} %bitcast.1.seq_at.unit_at, bf16[272,256]{1,0:T(8,128)(2,1)S(1)} %shard_map.130.refs_14_.refs_0_, bf16[272,256]{1,0:T(8,128)(2,1)S(1)} %collective-permute-done.26.refs_1_, ...), custom_call_target="tpu_custom_call" | custom-call | bytes 2097152 | tf_op jit(solution)/shard_map/pallas_call | solution.py:759
  (43 shorter events, 1.5 us)
Async XLA Ops:
  3.2 9.8 %collective-permute-start.5 = (bf16[4,256,256]{2,1,0:T(8,128)(2,1)S(1)}, bf16[4,256,256]{2,1,0:T(8,128)(2,1)S(1)}, u32[]{:S(2)}, u32[]{:S(2)}) collective-permute-start(bf16[4,256,256]{2,1,0:T(8,128)(2,1)S(1)} %get-tuple-element.60), channel_id=1, source_target_pairs={{0,16},{16,0},{1,17},{17,1},{2,18},{18,2},{3,19},{19,3},{4,20},{20... | collective-permute-start | bytes 1572872 | tf_op jit(solution)/shard_map/ppermute | solution.py:514
  3.7 9.3 %collective-permute-start.4 = (bf16[256,512]{1,0:T(8,128)(2,1)S(1)}, bf16[256,512]{1,0:T(8,128)(2,1)S(1)}, u32[]{:S(2)}, u32[]{:S(2)}) collective-permute-start(bf16[256,512]{1,0:T(8,128)(2,1)S(1)} %get-tuple-element.58), channel_id=1, source_target_pairs={{0,16},{16,0},{1,17},{17,1},{2,18},{18,2},{3,19},{19,3},{4,20},{20... | collective-permute-start | bytes 786440 | tf_op jit(solution)/shard_map/ppermute | solution.py:514
  3.8 5.5 %collective-permute-start = (f32[8,256]{1,0:T(8,128)S(1)}, f32[8,256]{1,0:T(8,128)S(1)}, u32[]{:S(2)}, u32[]{:S(2)}) collective-permute-start(f32[8,256]{1,0:T(8,128)S(1)} %get-tuple-element.55.refs_3_), channel_id=1, source_target_pairs={{0,3},{1,2},{2,1},{3,0},{4,7},{5,6},{6,5},{7,4},{8,11},{9,10},{10,... | collective-permute-start | bytes 24584 | tf_op jit(solution)/shard_map/ppermute | solution.py:510
  7.7 3.7 %collective-permute-start.1 = (f32[8,256]{1,0:T(8,128)S(1)}, f32[8,256]{1,0:T(8,128)S(1)}, u32[]{:S(2)}, u32[]{:S(2)}) collective-permute-start(f32[8,256]{1,0:T(8,128)S(1)} %get-tuple-element.55.refs_3_), channel_id=1, source_target_pairs={{0,2},{1,3},{2,0},{3,1},{4,6},{5,7},{6,4},{7,5},{8,10},{9,11},{10,... | collective-permute-start | bytes 24584 | tf_op jit(solution)/shard_map/ppermute | solution.py:510
  8.2 3.7 %collective-permute-start.2 = (f32[8,256]{1,0:T(8,128)S(1)}, f32[8,256]{1,0:T(8,128)S(1)}, u32[]{:S(2)}, u32[]{:S(2)}) collective-permute-start(f32[8,256]{1,0:T(8,128)S(1)} %get-tuple-element.55.refs_3_), channel_id=1, source_target_pairs={{0,1},{1,0},{2,3},{3,2},{4,5},{5,4},{6,7},{7,6},{8,9},{9,8},{10,11... | collective-permute-start | bytes 24584 | tf_op jit(solution)/shard_map/ppermute | solution.py:510
  9.3 3.7 %collective-permute-start.6 = (f32[8,512]{1,0:T(8,128)S(1)}, f32[8,512]{1,0:T(8,128)S(1)}, u32[]{:S(2)}, u32[]{:S(2)}) collective-permute-start(f32[8,512]{1,0:T(8,128)S(1)} %get-tuple-element.62), channel_id=1, source_target_pairs={{0,16},{16,0},{1,17},{17,1},{2,18},{18,2},{3,19},{19,3},{4,20},{20... | collective-permute-start | bytes 49160 | tf_op jit(solution)/shard_map/ppermute | solution.py:514
  11.8 1.2 %collective-permute-start.3 = (f32[8,256]{1,0:T(8,128)S(1)}, f32[8,256]{1,0:T(8,128)S(1)}, u32[]{:S(2)}, u32[]{:S(2)}) collective-permute-start(f32[8,256]{1,0:T(8,128)S(1)} %shard_map.121), channel_id=1, source_target_pairs={{0,16},{16,0},{1,17},{17,1},{2,18},{18,2},{3,19},{19,3},{4,20},{20... | collective-permute-start | bytes 24584 | tf_op jit(solution)/shard_map/ppermute | solution.py:514
  15.1 4.0 %collective-permute-start.7 = (f32[12,512]{1,0:T(8,128)S(1)}, f32[12,512]{1,0:T(8,128)S(1)}, u32[]{:S(2)}, u32[]{:S(2)}) collective-permute-start(f32[12,512]{1,0:T(8,128)S(1)} %get-tuple-element.64.own_ref), channel_id=1, source_target_pairs={{0,4},{4,0},{8,12},{12,8},{1,5},{5,1},{9,13},{13,9},{2,6},{6,2},{1... | collective-permute-start | bytes 73736 | tf_op jit(solution)/shard_map/ppermute | solution.py:510
  19.1 4.7 %collective-permute-start.8 = (f32[4,512]{1,0:T(4,128)S(1)}, f32[4,512]{1,0:T(4,128)S(1)}, u32[]{:S(2)}, u32[]{:S(2)}) collective-permute-start(f32[4,512]{1,0:T(4,128)S(1)} %shard_map.123), channel_id=1, source_target_pairs={{0,8},{4,12},{8,0},{12,4},{1,9},{5,13},{9,1},{13,5},{2,10},{6,14},... | collective-permute-start | bytes 24584 | tf_op jit(solution)/shard_map/ppermute | solution.py:510
  25.4 1.2 %collective-permute-start.9 = (f32[8,256]{1,0:T(8,128)S(1)}, f32[8,256]{1,0:T(8,128)S(1)}, u32[]{:S(2)}, u32[]{:S(2)}) collective-permute-start(f32[8,256]{1,0:T(8,128)S(1)} %get-tuple-element.73.refs_0_), channel_id=1, source_target_pairs={{0,16},{16,0},{1,17},{17,1},{2,18},{18,2},{3,19},{19,3},{4,20},{20... | collective-permute-start | bytes 24584 | tf_op jit(solution)/shard_map/ppermute | solution.py:514
  26.6 11.9 %collective-permute-start.15 = (bf16[2,272,256]{2,1,0:T(8,128)(2,1)S(1)}, bf16[2,272,256]{2,1,0:T(8,128)(2,1)S(1)}, u32[]{:S(2)}, u32[]{:S(2)}) collective-permute-start(bf16[2,272,256]{2,1,0:T(8,128)(2,1)S(1)} %get-tuple-element.82), channel_id=1, source_target_pairs={{0,4},{4,0},{8,12},{12,8},{1,5},{5,1},{9,13},{13,9},{2,6},{6,2},{1... | collective-permute-start | bytes 835592 | tf_op jit(solution)/shard_map/ppermute | solution.py:510
  28.2 4.5 %collective-permute-start.10 = (f32[8,256]{1,0:T(8,128)S(1)}, f32[8,256]{1,0:T(8,128)S(1)}, u32[]{:S(2)}, u32[]{:S(2)}) collective-permute-start(f32[8,256]{1,0:T(8,128)S(1)} %shard_map.126.refs_3_), channel_id=1, source_target_pairs={{0,3},{1,2},{2,1},{3,0},{4,7},{5,6},{6,5},{7,4},{8,11},{9,10},{10,... | collective-permute-start | bytes 24584 | tf_op jit(solution)/shard_map/ppermute | solution.py:510
  29.6 3.7 %collective-permute-start.11 = (f32[8,256]{1,0:T(8,128)S(1)}, f32[8,256]{1,0:T(8,128)S(1)}, u32[]{:S(2)}, u32[]{:S(2)}) collective-permute-start(f32[8,256]{1,0:T(8,128)S(1)} %shard_map.126.refs_3_), channel_id=1, source_target_pairs={{0,2},{1,3},{2,0},{3,1},{4,6},{5,7},{6,4},{7,5},{8,10},{9,11},{10,... | collective-permute-start | bytes 24584 | tf_op jit(solution)/shard_map/ppermute | solution.py:510
  30.2 3.7 %collective-permute-start.12 = (f32[8,256]{1,0:T(8,128)S(1)}, f32[8,256]{1,0:T(8,128)S(1)}, u32[]{:S(2)}, u32[]{:S(2)}) collective-permute-start(f32[8,256]{1,0:T(8,128)S(1)} %shard_map.126.refs_3_), channel_id=1, source_target_pairs={{0,1},{1,0},{2,3},{3,2},{4,5},{5,4},{6,7},{7,6},{8,9},{9,8},{10,11... | collective-permute-start | bytes 24584 | tf_op jit(solution)/shard_map/ppermute | solution.py:510
  34.5 4.0 %collective-permute-start.13 = (f32[12,512]{1,0:T(8,128)S(1)}, f32[12,512]{1,0:T(8,128)S(1)}, u32[]{:S(2)}, u32[]{:S(2)}) collective-permute-start(f32[12,512]{1,0:T(8,128)S(1)} %get-tuple-element.74.own_ref), channel_id=1, source_target_pairs={{0,4},{4,0},{8,12},{12,8},{1,5},{5,1},{9,13},{13,9},{2,6},{6,2},{1... | collective-permute-start | bytes 73736 | tf_op jit(solution)/shard_map/ppermute | solution.py:510
  38.6 7.6 %collective-permute-start.16 = (bf16[272,256]{1,0:T(8,128)(2,1)S(1)}, bf16[272,256]{1,0:T(8,128)(2,1)S(1)}, u32[]{:S(2)}, u32[]{:S(2)}) collective-permute-start(bf16[272,256]{1,0:T(8,128)(2,1)S(1)} %get-tuple-element.85), channel_id=1, source_target_pairs={{0,8},{4,12},{8,0},{12,4},{1,9},{5,13},{9,1},{13,5},{2,10},{6,14},... | collective-permute-start | bytes 417800 | tf_op jit(solution)/shard_map/ppermute | solution.py:510
  41.4 4.8 %collective-permute-start.14 = (f32[4,512]{1,0:T(4,128)S(1)}, f32[4,512]{1,0:T(4,128)S(1)}, u32[]{:S(2)}, u32[]{:S(2)}) collective-permute-start(f32[4,512]{1,0:T(4,128)S(1)} %shard_map.128), channel_id=1, source_target_pairs={{0,8},{4,12},{8,0},{12,4},{1,9},{5,13},{9,1},{13,5},{2,10},{6,14},... | collective-permute-start | bytes 24584 | tf_op jit(solution)/shard_map/ppermute | solution.py:510
  46.2 13.6 %collective-permute-start.21 = (bf16[272,256]{1,0:T(8,128)(2,1)S(1)}, bf16[272,256]{1,0:T(8,128)(2,1)S(1)}, u32[]{:S(2)}, u32[]{:S(2)}) collective-permute-start(bf16[272,256]{1,0:T(8,128)(2,1)S(1)} %shard_map.130.refs_14_.refs_0_), channel_id=1, source_target_pairs={{0,8},{4,12},{8,0},{12,4},{1,9},{5,13},{9,1},{13,5},{2,10},{6,14},... | collective-permute-start | bytes 417800 | tf_op jit(solution)/shard_map/ppermute | solution.py:510
  49.7 13.0 %collective-permute-start.17 = (bf16[272,256]{1,0:T(8,128)(2,1)S(1)}, bf16[272,256]{1,0:T(8,128)(2,1)S(1)}, u32[]{:S(2)}, u32[]{:S(2)}) collective-permute-start(bf16[272,256]{1,0:T(8,128)(2,1)S(1)} %get-tuple-element.88), channel_id=1, source_target_pairs={{0,12},{4,8},{8,4},{12,0},{1,13},{5,9},{9,5},{13,1},{2,14},{6,10},... | collective-permute-start | bytes 417800 | tf_op jit(solution)/shard_map/ppermute | solution.py:510
  52.2 11.9 %collective-permute-start.18 = (bf16[272,256]{1,0:T(8,128)(2,1)S(1)}, bf16[272,256]{1,0:T(8,128)(2,1)S(1)}, u32[]{:S(2)}, u32[]{:S(2)}) collective-permute-start(bf16[272,256]{1,0:T(8,128)(2,1)S(1)} %get-tuple-element.89), channel_id=1, source_target_pairs={{0,8},{4,12},{8,0},{12,4},{1,9},{5,13},{9,1},{13,5},{2,10},{6,14},... | collective-permute-start | bytes 417800 | tf_op jit(solution)/shard_map/ppermute | solution.py:510
  54.2 10.4 %collective-permute-start.19 = (bf16[272,256]{1,0:T(8,128)(2,1)S(1)}, bf16[272,256]{1,0:T(8,128)(2,1)S(1)}, u32[]{:S(2)}, u32[]{:S(2)}) collective-permute-start(bf16[272,256]{1,0:T(8,128)(2,1)S(1)} %get-tuple-element.90), channel_id=1, source_target_pairs={{0,4},{4,0},{8,12},{12,8},{1,5},{5,1},{9,13},{13,9},{2,6},{6,2},{1... | collective-permute-start | bytes 417800 | tf_op jit(solution)/shard_map/ppermute | solution.py:510
  54.2 1.2 %collective-permute-start.20 = (f32[8,256]{1,0:T(8,128)S(1)}, f32[8,256]{1,0:T(8,128)S(1)}, u32[]{:S(2)}, u32[]{:S(2)}) collective-permute-start(f32[8,256]{1,0:T(8,128)S(1)} %get-tuple-element.91.refs_0_), channel_id=1, source_target_pairs={{0,16},{16,0},{1,17},{17,1},{2,18},{18,2},{3,19},{19,3},{4,20},{20... | collective-permute-start | bytes 24584 | tf_op jit(solution)/shard_map/ppermute | solution.py:514
  59.8 6.3 %collective-permute-start.22 = (f32[8,256]{1,0:T(8,128)S(1)}, f32[8,256]{1,0:T(8,128)S(1)}, u32[]{:S(2)}, u32[]{:S(2)}) collective-permute-start(f32[8,256]{1,0:T(8,128)S(1)} %shard_map.132.refs_3_), channel_id=1, source_target_pairs={{0,3},{1,2},{2,1},{3,0},{4,7},{5,6},{6,5},{7,4},{8,11},{9,10},{10,... | collective-permute-start | bytes 24584 | tf_op jit(solution)/shard_map/ppermute | solution.py:510
  62.2 3.9 %collective-permute-start.23 = (f32[8,256]{1,0:T(8,128)S(1)}, f32[8,256]{1,0:T(8,128)S(1)}, u32[]{:S(2)}, u32[]{:S(2)}) collective-permute-start(f32[8,256]{1,0:T(8,128)S(1)} %shard_map.132.refs_3_), channel_id=1, source_target_pairs={{0,2},{1,3},{2,0},{3,1},{4,6},{5,7},{6,4},{7,5},{8,10},{9,11},{10,... | collective-permute-start | bytes 24584 | tf_op jit(solution)/shard_map/ppermute | solution.py:510
  62.7 3.7 %collective-permute-start.24 = (f32[8,256]{1,0:T(8,128)S(1)}, f32[8,256]{1,0:T(8,128)S(1)}, u32[]{:S(2)}, u32[]{:S(2)}) collective-permute-start(f32[8,256]{1,0:T(8,128)S(1)} %shard_map.132.refs_3_), channel_id=1, source_target_pairs={{0,1},{1,0},{2,3},{3,2},{4,5},{5,4},{6,7},{7,6},{8,9},{9,8},{10,11... | collective-permute-start | bytes 24584 | tf_op jit(solution)/shard_map/ppermute | solution.py:510
  64.1 15.5 %collective-permute-start.26 = (bf16[272,256]{1,0:T(8,128)(2,1)S(1)}, bf16[272,256]{1,0:T(8,128)(2,1)S(1)}, u32[]{:S(2)}, u32[]{:S(2)}) collective-permute-start(bf16[272,256]{1,0:T(8,128)(2,1)S(1)} %shard_map.130.refs_14_.refs_0_), channel_id=1, source_target_pairs={{0,4},{4,0},{8,12},{12,8},{1,5},{5,1},{9,13},{13,9},{2,6},{6,2},{1... | collective-permute-start | bytes 417800 | tf_op jit(solution)/shard_map/ppermute | solution.py:510
  64.6 13.2 %collective-permute-start.27 = (bf16[272,256]{1,0:T(8,128)(2,1)S(1)}, bf16[272,256]{1,0:T(8,128)(2,1)S(1)}, u32[]{:S(2)}, u32[]{:S(2)}) collective-permute-start(bf16[272,256]{1,0:T(8,128)(2,1)S(1)} %collective-permute-done.21.refs_2_), channel_id=1, source_target_pairs={{0,4},{4,0},{8,12},{12,8},{1,5},{5,1},{9,13},{13,9},{2,6},{6,2},{1... | collective-permute-start | bytes 417800 | tf_op jit(solution)/shard_map/ppermute | solution.py:510
  66.5 11.3 %collective-permute-start.30 = (bf16[272,256]{1,0:T(8,128)(2,1)S(1)}, bf16[272,256]{1,0:T(8,128)(2,1)S(1)}, u32[]{:S(2)}, u32[]{:S(2)}) collective-permute-start(bf16[272,256]{1,0:T(8,128)(2,1)S(1)} %shard_map.135.refs_4_), channel_id=1, source_target_pairs={{0,12},{4,8},{8,4},{12,0},{1,13},{5,9},{9,5},{13,1},{2,14},{6,10},... | collective-permute-start | bytes 417800 | tf_op jit(solution)/shard_map/ppermute | solution.py:510
  68.8 10.7 %collective-permute-start.29 = (bf16[272,256]{1,0:T(8,128)(2,1)S(1)}, bf16[272,256]{1,0:T(8,128)(2,1)S(1)}, u32[]{:S(2)}, u32[]{:S(2)}) collective-permute-start(bf16[272,256]{1,0:T(8,128)(2,1)S(1)} %shard_map.135.refs_4_), channel_id=1, source_target_pairs={{0,8},{4,12},{8,0},{12,4},{1,9},{5,13},{9,1},{13,5},{2,10},{6,14},... | collective-permute-start | bytes 417800 | tf_op jit(solution)/shard_map/ppermute | solution.py:510
  68.8 11.3 %collective-permute-start.28 = (bf16[272,256]{1,0:T(8,128)(2,1)S(1)}, bf16[272,256]{1,0:T(8,128)(2,1)S(1)}, u32[]{:S(2)}, u32[]{:S(2)}) collective-permute-start(bf16[272,256]{1,0:T(8,128)(2,1)S(1)} %shard_map.135.refs_4_), channel_id=1, source_target_pairs={{0,4},{4,0},{8,12},{12,8},{1,5},{5,1},{9,13},{13,9},{2,6},{6,2},{1... | collective-permute-start | bytes 417800 | tf_op jit(solution)/shard_map/ppermute | solution.py:510
  77.8 3.4 %collective-permute-start.31 = (bf16[272,256]{1,0:T(8,128)(2,1)S(1)}, bf16[272,256]{1,0:T(8,128)(2,1)S(1)}, u32[]{:S(2)}, u32[]{:S(2)}) collective-permute-start(bf16[272,256]{1,0:T(8,128)(2,1)S(1)} %broadcast_select_fusion.3), channel_id=1, source_target_pairs={{0,16},{16,0},{1,17},{17,1},{2,18},{18,2},{3,19},{19,3},{4,20},{20... | collective-permute-start | bytes 417800 | tf_op jit(solution)/shard_map/ppermute | solution.py:514
  77.8 2.5 %collective-permute-start.25 = (bf16[256,512]{1,0:T(8,128)(2,1)S(1)}, bf16[256,512]{1,0:T(8,128)(2,1)S(1)}, u32[]{:S(2)}, u32[]{:S(2)}) collective-permute-start(bf16[256,512]{1,0:T(8,128)(2,1)S(1)} %get-tuple-element.98), channel_id=1, source_target_pairs={{0,16},{16,0},{1,17},{17,1},{2,18},{18,2},{3,19},{19,3},{4,20},{20... | collective-permute-start | bytes 786440 | tf_op jit(solution)/shard_map/ppermute | solution.py:514
  79.6 1.6 %collective-permute-start.34 = (bf16[272,256]{1,0:T(8,128)(2,1)S(1)}, bf16[272,256]{1,0:T(8,128)(2,1)S(1)}, u32[]{:S(2)}, u32[]{:S(2)}) collective-permute-start(bf16[272,256]{1,0:T(8,128)(2,1)S(1)} %broadcast_select_fusion), channel_id=1, source_target_pairs={{0,16},{16,0},{1,17},{17,1},{2,18},{18,2},{3,19},{19,3},{4,20},{20... | collective-permute-start | bytes 417800 | tf_op jit(solution)/shard_map/ppermute | solution.py:514
  79.6 1.6 %collective-permute-start.33 = (bf16[272,256]{1,0:T(8,128)(2,1)S(1)}, bf16[272,256]{1,0:T(8,128)(2,1)S(1)}, u32[]{:S(2)}, u32[]{:S(2)}) collective-permute-start(bf16[272,256]{1,0:T(8,128)(2,1)S(1)} %broadcast_select_fusion.1), channel_id=1, source_target_pairs={{0,16},{16,0},{1,17},{17,1},{2,18},{18,2},{3,19},{19,3},{4,20},{20... | collective-permute-start | bytes 417800 | tf_op jit(solution)/shard_map/ppermute | solution.py:514
  80.2 1.4 %collective-permute-start.32 = (bf16[272,256]{1,0:T(8,128)(2,1)S(1)}, bf16[272,256]{1,0:T(8,128)(2,1)S(1)}, u32[]{:S(2)}, u32[]{:S(2)}) collective-permute-start(bf16[272,256]{1,0:T(8,128)(2,1)S(1)} %broadcast_select_fusion.2), channel_id=1, source_target_pairs={{0,16},{16,0},{1,17},{17,1},{2,18},{18,2},{3,19},{19,3},{4,20},{20... | collective-permute-start | bytes 417800 | tf_op jit(solution)/shard_map/ppermute | solution.py:514

commit v4 on v3

--- a/solution.py
+++ b/solution.py
@@ -519,7 +519,7 @@
     if count & (count - 1):
         gathered = lax.all_gather(value, "chan")
         return [gathered[k] for k in range(count)]
-    return [xor_moves(value, "chan", k) for k in reversed(range(1, count))] + [value]
+    return [xor_moves(value, "chan", k) for k in ((3, 2, 1) if count == 4 else range(1, count))] + [value]
 
 
 def seq_pays(pay, seq_at, micro):
@@ -701,7 +701,6 @@
     cross = chip_sum(cross)
     parts = chan_parts(cross)
     if direct:
-        top_parts[1] = after(top_parts[1], cross)
         arrived = xor_moves(top_parts[1], "seq", 1)
     early, low_rgrad, low_pay = call(
         functools.partial(late_kernel, micro, tok_rows, full_width, len(parts)),
@@ -721,14 +720,16 @@
     part, cross, *low_parts = backward(
         0, pays, early, low, low_rgrad, top_own if direct else low_pay
     )
-    parts = chan_parts(after(chip_sum(cross), top_far) if direct else chip_sum(cross))
+    sw = swap_sections(cross)
+    cross = add_units(cross, after(sw, top_far) if direct else sw)
+    parts = chan_parts(cross)
     if direct:
         place = lax.axis_index("seq")
-        low_arrived = [xor_moves(low_parts[k], "seq", k) for k in (3, 2, 1)]
+        low_arrived = [xor_moves(low_parts[k], "seq", k) for k in (2, 1, 3)]
         low_arrived, parts = lax.optimization_barrier((low_arrived, parts))
         low_own = add_units(low_parts[0], *low_arrived)
         low_units = [low_own] + [xor_moves(low_own, "seq", k) for k in (1, 2, 3)]
-        top_near = xor_moves(top_own, "seq", 1)
+        top_near = xor_moves(after(top_own, cross), "seq", 1)
         top_last = xor_moves(top_far, "seq", 1)
         top_units = [top_own, top_near, top_far, top_last]
     else:

time: 83.3 us -> 82.1 us (0.986)
  starting transfers between devices: 35.5 us -> 34.1 us
    ppermute x24, starting transfers between devices: 33.7 us -> 32.8 us  [xor_moves(): lax.ppermute(value, axis, [(i, i ^ k) for i in range(lax.axis_size(axis))])]
  transfers between devices with their start and end apart: 35 -> 35, of which waited for: 18 -> 19; matrix products, arithmetic and copies ran while one was open for 0% -> 0% of each run, Pallas kernels for 7% -> 7%
where the time goes in v4:
time: 82.1 us; the launch traced here: 81.9 us
  starting transfers between devices  34.1 us (42%)
  waiting for transfers between devices  33.1 us (40%)
  Pallas kernels  13.9 us (17%)
    ppermute x24, starting transfers between devices, xor_moves(): lax.ppermute(value, axis, [(i, i ^ k) for i in range(lax.axis_size(axis))])  32.8 us
    ppermute x24, waiting for transfers between devices, xor_moves(): lax.ppermute(value, axis, [(i, i ^ k) for i in range(lax.axis_size(axis))])  29.1 us
    pallas_call x8, Pallas kernels, call(): pl.pallas_call(kernel, in_specs=[smem] * len(scalars) + (specs or [whole]...  12.2 us
    ppermute x11, waiting for transfers between devices, swap_sections(): return lax.ppermute(value, 'section', [(0, 1), (1, 0)])  4.01 us
  transfers between devices with their start and end apart: 35, of which 19 were waited for; matrix products, arithmetic and copies ran while one was open for 0% of the time, Pallas kernels for 7%

profile of v4, /device:TPU:0, one launch (start us, length us, event | category | flops | bytes accessed | tf_op | source)
XLA Modules:
  0.0 81.9 jit_solution(14705527462056484013)
XLA Ops:
  0.6 2.5 %shard_map.120 = (f32[8,256]{1,0:T(8,128)S(1)}, bf16[256,512]{1,0:T(8,128)(2,1)S(1)}, bf16[256,512]{1,0:T(8,128)(2,1)S(1)}, bf16[256,512]{1,0:T(8,128)(2,1)S(1)}...) custom-call(s32[1]{0:T(128)} %bitcast.section_at, ...), custom_call_target="tpu_custom_call" | custom-call | flops 268435456 | bytes 3145728 | tf_op jit(solution)/shard_map/pallas_call | solution.py:598
  3.2 0.5 collective-permute-start.5
  3.8 3.9 %collective-permute-start = (f32[8,256]{1,0:T(8,128)S(1)}, f32[8,256]{1,0:T(8,128)S(1)}, u32[]{:S(2)}, u32[]{:S(2)}) collective-permute-start(f32[8,256]{1,0:T(8,128)S(1)} %get-tuple-element.55.refs_3_), channel_id=1, source_target_pairs={{0,3},{1,2},{2,1},{3,0},{4,7},{5,6},{6,5},{7,4},{8,11},{9,10},{10,... | collective-permute-start | bytes 24584 | tf_op jit(solution)/shard_map/ppermute | solution.py:510
  7.7 0.5 collective-permute-start.1
  8.2 1.1 %collective-permute-done.refs_0_ = f32[8,256]{1,0:T(8,128)S(1)} collective-permute-done((f32[8,256]{1,0:T(8,128)S(1)}, f32[8,256]{1,0:T(8,128)S(1)}, u32[]{:S(2)}, u32[]{:S(2)}) %collective-permute-start) | collective-permute-done | bytes 8224 | tf_op jit(solution)/shard_map/ppermute | solution.py:510
  9.3 2.0 %collective-permute-done.1.refs_1_ = f32[8,256]{1,0:T(8,128)S(1)} collective-permute-done((f32[8,256]{1,0:T(8,128)S(1)}, f32[8,256]{1,0:T(8,128)S(1)}, u32[]{:S(2)}, u32[]{:S(2)}) %collective-permute-start.1) | collective-permute-done | bytes 8224 | tf_op jit(solution)/shard_map/ppermute | solution.py:510
  11.3 0.5 collective-permute-done.2.refs_2_
  11.8 1.2 %collective-permute-done.3.refs_4_ = f32[8,256]{1,0:T(8,128)S(1)} collective-permute-done((f32[8,256]{1,0:T(8,128)S(1)}, f32[8,256]{1,0:T(8,128)S(1)}, u32[]{:S(2)}, u32[]{:S(2)}) %collective-permute-start.3) | collective-permute-done | bytes 8224 | tf_op jit(solution)/shard_map/ppermute | solution.py:514
  13.0 2.0 %shard_map.122 = (bf16[256,512]{1,0:T(8,128)(2,1)S(1)}, f32[5,256,512]{2,1,0:T(8,128)S(1)}, f32[3,32,512]{2,1,0:T(8,128)S(1)}, f32[12,512]{1,0:T(8,128)S(1)}, f3...) custom-call(s32[1]{0:T(128)} %bitcast.1.seq_at.unit_at, s32[1]{0:T(128)} %bitcast.section_at, ...), custom_call_target="tpu_custom_call" | custom-call | flops 134217728 | bytes 3145728 | tf_op jit(solution)/shard_map/pallas_call | solution.py:598
  15.1 1.6 %collective-permute-start.7 = (f32[12,512]{1,0:T(8,128)S(1)}, f32[12,512]{1,0:T(8,128)S(1)}, u32[]{:S(2)}, u32[]{:S(2)}) collective-permute-start(f32[12,512]{1,0:T(8,128)S(1)} %get-tuple-element.64.own_ref), channel_id=1, source_target_pairs={{0,4},{4,0},{8,12},{12,8},{1,5},{5,1},{9,13},{13,9},{2,6},{6,2},{1... | collective-permute-start | bytes 73736 | tf_op jit(solution)/shard_map/ppermute | solution.py:510
  16.7 2.3 %collective-permute-done.7.near_ref.refs_0_ = f32[12,512]{1,0:T(8,128)S(1)} collective-permute-done((f32[12,512]{1,0:T(8,128)S(1)}, f32[12,512]{1,0:T(8,128)S(1)}, u32[]{:S(2)}, u32[]{:S(2)}) %collective-permute-start.7) | collective-permute-done | bytes 24608 | tf_op jit(solution)/shard_map/ppermute | solution.py:510
  19.1 2.6 %collective-permute-start.8 = (f32[4,512]{1,0:T(4,128)S(1)}, f32[4,512]{1,0:T(4,128)S(1)}, u32[]{:S(2)}, u32[]{:S(2)}) collective-permute-start(f32[4,512]{1,0:T(4,128)S(1)} %shard_map.123), channel_id=1, source_target_pairs={{0,8},{4,12},{8,0},{12,4},{1,9},{5,13},{9,1},{13,5},{2,10},{6,14},... | collective-permute-start | bytes 24584 | tf_op jit(solution)/shard_map/ppermute | solution.py:510
  21.7 2.1 %shard_map.124 = (bf16[256,512]{1,0:T(8,128)(2,1)S(1)}, f32[5,256,512]{2,1,0:T(8,128)S(1)}, f32[3,32,512]{2,1,0:T(8,128)S(1)}, f32[8,512]{1,0:T(8,128)S(1)}, f32[256,128]{1,0:T(8,128)S(1)}) custom-call(s32[1]{0:T(128)} %bitcast.1.seq_at.unit_at, s32[1]{0:T(128)} %bitcast.section_at, f32[8,256]{1,0:T(8,128)S(1)} %collective-permute-done.refs_0_, ...), custom_call_target="tpu_custom_call" | custom-call | flops 134217728 | bytes 3145728 | tf_op jit(solution)/shard_map/pallas_call | solution.py:598
  23.8 1.6 %shard_map.125 = (f32[256,512]{1,0:T(8,128)S(1)}, f32[8,256]{1,0:T(8,128)S(1)}, bf16[2,272,256]{2,1,0:T(8,128)(2,1)S(1)}, bf16[2,272,256]{2,1,0:T(8,128)(2,1)S(1)}) custom-call(s32[1]{0:T(128)} %bitcast.1.seq_at.unit_at, s32[1]{0:T(128)} %bitcast.section_at, f32[12,512]{1,0:T(8,128)S(1)} %collective-permute-done.7.near_ref.refs_0_, ...), custom_call_target="tpu_custom_call" | custom-call | flops 268435456 | bytes 3932160 | tf_op jit(solution)/shard_map/pallas_call | solution.py:598
  25.4 1.6 %collective-permute-start.15 = (bf16[2,272,256]{2,1,0:T(8,128)(2,1)S(1)}, bf16[2,272,256]{2,1,0:T(8,128)(2,1)S(1)}, u32[]{:S(2)}, u32[]{:S(2)}) collective-permute-start(bf16[2,272,256]{2,1,0:T(8,128)(2,1)S(1)} %get-tuple-element.81), channel_id=1, source_target_pairs={{0,4},{4,0},{8,12},{12,8},{1,5},{5,1},{9,13},{13,9},{2,6},{6,2},{1... | collective-permute-start | bytes 835592 | tf_op jit(solution)/shard_map/ppermute | solution.py:510
  27.0 1.2 %collective-permute-done.9.refs_1_ = f32[8,256]{1,0:T(8,128)S(1)} collective-permute-done((f32[8,256]{1,0:T(8,128)S(1)}, f32[8,256]{1,0:T(8,128)S(1)}, u32[]{:S(2)}, u32[]{:S(2)}) %collective-permute-start.9) | collective-permute-done | bytes 8224 | tf_op jit(solution)/shard_map/ppermute | solution.py:514
  28.2 1.5 %collective-permute-start.10 = (f32[8,256]{1,0:T(8,128)S(1)}, f32[8,256]{1,0:T(8,128)S(1)}, u32[]{:S(2)}, u32[]{:S(2)}) collective-permute-start(f32[8,256]{1,0:T(8,128)S(1)} %shard_map.126.refs_3_), channel_id=1, source_target_pairs={{0,3},{1,2},{2,1},{3,0},{4,7},{5,6},{6,5},{7,4},{8,11},{9,10},{10,... | collective-permute-start | bytes 24584 | tf_op jit(solution)/shard_map/ppermute | solution.py:510
  29.6 0.5 collective-permute-start.11
  30.2 1.5 %collective-permute-start.12 = (f32[8,256]{1,0:T(8,128)S(1)}, f32[8,256]{1,0:T(8,128)S(1)}, u32[]{:S(2)}, u32[]{:S(2)}) collective-permute-start(f32[8,256]{1,0:T(8,128)S(1)} %shard_map.126.refs_3_), channel_id=1, source_target_pairs={{0,1},{1,0},{2,3},{3,2},{4,5},{5,4},{6,7},{7,6},{8,9},{9,8},{10,11... | collective-permute-start | bytes 24584 | tf_op jit(solution)/shard_map/ppermute | solution.py:510
  31.6 1.1 %collective-permute-done.10.refs_0_ = f32[8,256]{1,0:T(8,128)S(1)} collective-permute-done((f32[8,256]{1,0:T(8,128)S(1)}, f32[8,256]{1,0:T(8,128)S(1)}, u32[]{:S(2)}, u32[]{:S(2)}) %collective-permute-start.10) | collective-permute-done | bytes 8224 | tf_op jit(solution)/shard_map/ppermute | solution.py:510
  32.7 0.6 collective-permute-done.11.refs_1_
  33.3 0.5 collective-permute-done.12.refs_2_
  33.8 0.7 shard_map.127
  34.5 0.5 collective-permute-start.13
  35.0 3.5 %collective-permute-done.13.near_ref.refs_0_ = f32[12,512]{1,0:T(8,128)S(1)} collective-permute-done((f32[12,512]{1,0:T(8,128)S(1)}, f32[12,512]{1,0:T(8,128)S(1)}, u32[]{:S(2)}, u32[]{:S(2)}) %collective-permute-start.13) | collective-permute-done | bytes 24608 | tf_op jit(solution)/shard_map/ppermute | solution.py:510
  38.6 2.8 %collective-permute-start.16 = (bf16[272,256]{1,0:T(8,128)(2,1)S(1)}, bf16[272,256]{1,0:T(8,128)(2,1)S(1)}, u32[]{:S(2)}, u32[]{:S(2)}) collective-permute-start(bf16[272,256]{1,0:T(8,128)(2,1)S(1)} %get-tuple-element.84), channel_id=1, source_target_pairs={{0,8},{4,12},{8,0},{12,4},{1,9},{5,13},{9,1},{13,5},{2,10},{6,14},... | collective-permute-start | bytes 417800 | tf_op jit(solution)/shard_map/ppermute | solution.py:510
  41.6 6.1 %collective-permute-done.14.refs_1_ = f32[4,512]{1,0:T(4,128)S(1)} collective-permute-done((f32[4,512]{1,0:T(4,128)S(1)}, f32[4,512]{1,0:T(4,128)S(1)}, u32[]{:S(2)}, u32[]{:S(2)}) %collective-permute-start.14) | collective-permute-done | bytes 8224 | tf_op jit(solution)/shard_map/ppermute | solution.py:510
  47.8 1.6 %shard_map.131 = (f32[256,512]{1,0:T(8,128)S(1)}, f32[8,256]{1,0:T(8,128)S(1)}, bf16[272,256]{1,0:T(8,128)(2,1)S(1)}, bf16[272,256]{1,0:T(8,128)(2,1)S(1)}, bf16...) custom-call(s32[1]{0:T(128)} %bitcast.1.seq_at.unit_at, s32[1]{0:T(128)} %bitcast.section_at, ...), custom_call_target="tpu_custom_call" | custom-call | flops 268435456 | bytes 3932160 | tf_op jit(solution)/shard_map/pallas_call | solution.py:598
  49.4 2.9 %collective-permute-start.17 = (bf16[272,256]{1,0:T(8,128)(2,1)S(1)}, bf16[272,256]{1,0:T(8,128)(2,1)S(1)}, u32[]{:S(2)}, u32[]{:S(2)}) collective-permute-start(bf16[272,256]{1,0:T(8,128)(2,1)S(1)} %get-tuple-element.87), channel_id=1, source_target_pairs={{0,8},{4,12},{8,0},{12,4},{1,9},{5,13},{9,1},{13,5},{2,10},{6,14},... | collective-permute-start | bytes 417800 | tf_op jit(solution)/shard_map/ppermute | solution.py:510
  52.5 2.3 %collective-permute-start.19 = (bf16[272,256]{1,0:T(8,128)(2,1)S(1)}, bf16[272,256]{1,0:T(8,128)(2,1)S(1)}, u32[]{:S(2)}, u32[]{:S(2)}) collective-permute-start(bf16[272,256]{1,0:T(8,128)(2,1)S(1)} %get-tuple-element.89), channel_id=1, source_target_pairs={{0,12},{4,8},{8,4},{12,0},{1,13},{5,9},{9,5},{13,1},{2,14},{6,10},... | collective-permute-start | bytes 417800 | tf_op jit(solution)/shard_map/ppermute | solution.py:510
  54.8 1.2 %collective-permute-done.20.refs_1_ = f32[8,256]{1,0:T(8,128)S(1)} collective-permute-done((f32[8,256]{1,0:T(8,128)S(1)}, f32[8,256]{1,0:T(8,128)S(1)}, u32[]{:S(2)}, u32[]{:S(2)}) %collective-permute-start.20) | collective-permute-done | bytes 8224 | tf_op jit(solution)/shard_map/ppermute | solution.py:514
  56.0 5.1 %collective-permute-done.21.refs_2_ = bf16[272,256]{1,0:T(8,128)(2,1)S(1)} collective-permute-done((bf16[272,256]{1,0:T(8,128)(2,1)S(1)}, bf16[272,256]{1,0:T(8,128)(2,1)S(1)}, u32[]{:S(2)}, u32[]{:S(2)}) %collective-permute-start.21) | collective-permute-done | bytes 139296 | tf_op jit(solution)/shard_map/ppermute | solution.py:510
  61.1 2.4 %collective-permute-start.22 = (f32[8,256]{1,0:T(8,128)S(1)}, f32[8,256]{1,0:T(8,128)S(1)}, u32[]{:S(2)}, u32[]{:S(2)}) collective-permute-start(f32[8,256]{1,0:T(8,128)S(1)} %shard_map.132.refs_3_), channel_id=1, source_target_pairs={{0,3},{1,2},{2,1},{3,0},{4,7},{5,6},{6,5},{7,4},{8,11},{9,10},{10,... | collective-permute-start | bytes 24584 | tf_op jit(solution)/shard_map/ppermute | solution.py:510
  63.5 0.5 collective-permute-start.23
  64.0 0.5 collective-permute-start.24
  64.6 2.0 %collective-permute-start.27 = (bf16[272,256]{1,0:T(8,128)(2,1)S(1)}, bf16[272,256]{1,0:T(8,128)(2,1)S(1)}, u32[]{:S(2)}, u32[]{:S(2)}) collective-permute-start(bf16[272,256]{1,0:T(8,128)(2,1)S(1)} %collective-permute-done.21.refs_2_), channel_id=1, source_target_pairs={{0,4},{4,0},{8,12},{12,8},{1,5},{5,1},{9,13},{13,9},{2,6},{6,2},{1... | collective-permute-start | bytes 417800 | tf_op jit(solution)/shard_map/ppermute | solution.py:510
  66.6 0.6 collective-permute-done.23.refs_1_
  67.1 0.5 collective-permute-done.24.refs_2_
  67.7 2.2 %collective-permute-start.30 = (bf16[272,256]{1,0:T(8,128)(2,1)S(1)}, bf16[272,256]{1,0:T(8,128)(2,1)S(1)}, u32[]{:S(2)}, u32[]{:S(2)}) collective-permute-start(bf16[272,256]{1,0:T(8,128)(2,1)S(1)} %shard_map.135.refs_4_), channel_id=1, source_target_pairs={{0,12},{4,8},{8,4},{12,0},{1,13},{5,9},{9,5},{13,1},{2,14},{6,10},... | collective-permute-start | bytes 417800 | tf_op jit(solution)/shard_map/ppermute | solution.py:510
  69.9 2.3 %collective-permute-start.28 = (bf16[272,256]{1,0:T(8,128)(2,1)S(1)}, bf16[272,256]{1,0:T(8,128)(2,1)S(1)}, u32[]{:S(2)}, u32[]{:S(2)}) collective-permute-start(bf16[272,256]{1,0:T(8,128)(2,1)S(1)} %shard_map.135.refs_4_), channel_id=1, source_target_pairs={{0,4},{4,0},{8,12},{12,8},{1,5},{5,1},{9,13},{13,9},{2,6},{6,2},{1... | collective-permute-start | bytes 417800 | tf_op jit(solution)/shard_map/ppermute | solution.py:510
  72.2 0.8 shard_map.133
  73.0 0.8 %collective-permute-done.27.refs_3_ = bf16[272,256]{1,0:T(8,128)(2,1)S(1)} collective-permute-done((bf16[272,256]{1,0:T(8,128)(2,1)S(1)}, bf16[272,256]{1,0:T(8,128)(2,1)S(1)}, u32[]{:S(2)}, u32[]{:S(2)}) %collective-permute-start.27) | collective-permute-done | bytes 139296 | tf_op jit(solution)/shard_map/ppermute | solution.py:510
  73.8 1.7 %collective-permute-done.30.refs_7_ = bf16[272,256]{1,0:T(8,128)(2,1)S(1)} collective-permute-done((bf16[272,256]{1,0:T(8,128)(2,1)S(1)}, bf16[272,256]{1,0:T(8,128)(2,1)S(1)}, u32[]{:S(2)}, u32[]{:S(2)}) %collective-permute-start.30) | collective-permute-done | bytes 139296 | tf_op jit(solution)/shard_map/ppermute | solution.py:510
  75.6 2.8 %collective-permute-done.29.refs_6_ = bf16[272,256]{1,0:T(8,128)(2,1)S(1)} collective-permute-done((bf16[272,256]{1,0:T(8,128)(2,1)S(1)}, bf16[272,256]{1,0:T(8,128)(2,1)S(1)}, u32[]{:S(2)}, u32[]{:S(2)}) %collective-permute-start.29) | collective-permute-done | bytes 139296 | tf_op jit(solution)/shard_map/ppermute | solution.py:510
  78.4 0.6 collective-permute-start.33
  79.1 0.8 %shard_map.134 = bf16[256,1024]{1,0:T(8,128)(2,1)} custom-call(s32[1]{0:T(128)} %bitcast.section_at, bf16[256,512]{1,0:T(8,128)(2,1)S(1)} %get-tuple-element.96.keep_ref, bf16[256,512]{1,0:T(8,128)(2,1)S(1)} %collective-permute-done.25.arrived_ref), custom_call_target="tpu_custom_call" | custom-call | bytes 1048576 | tf_op jit(solution)/shard_map/pallas_call | solution.py:598
  80.0 0.5 collective-permute-done.32.refs_9_
  80.4 1.5 %shard_map.136 = (f32[4,256,256]{2,1,0:T(8,128)}, f32[4,256,256]{2,1,0:T(8,128)}, f32[3,1,1024]{2,1,0:T(1,128)}) custom-call(s32[1]{0:T(128)} %bitcast.section_at, s32[1]{0:T(128)} %bitcast.1.seq_at.unit_at, bf16[272,256]{1,0:T(8,128)(2,1)S(1)} %shard_map.130.refs_14_.refs_0_, bf16[272,256]{1,0:T(8,128)(2,1)S(1)} %collective-permute-done.26.refs_1_, ...), custom_call_target="tpu_custom_call" | custom-call | bytes 2097152 | tf_op jit(solution)/shard_map/pallas_call | solution.py:760
  (43 shorter events, 1.1 us)
Async XLA Ops:
  3.2 9.8 %collective-permute-start.5 = (bf16[4,256,256]{2,1,0:T(8,128)(2,1)S(1)}, bf16[4,256,256]{2,1,0:T(8,128)(2,1)S(1)}, u32[]{:S(2)}, u32[]{:S(2)}) collective-permute-start(bf16[4,256,256]{2,1,0:T(8,128)(2,1)S(1)} %get-tuple-element.60), channel_id=1, source_target_pairs={{0,16},{16,0},{1,17},{17,1},{2,18},{18,2},{3,19},{19,3},{4,20},{20... | collective-permute-start | bytes 1572872 | tf_op jit(solution)/shard_map/ppermute | solution.py:514
  3.7 9.3 %collective-permute-start.4 = (bf16[256,512]{1,0:T(8,128)(2,1)S(1)}, bf16[256,512]{1,0:T(8,128)(2,1)S(1)}, u32[]{:S(2)}, u32[]{:S(2)}) collective-permute-start(bf16[256,512]{1,0:T(8,128)(2,1)S(1)} %get-tuple-element.58), channel_id=1, source_target_pairs={{0,16},{16,0},{1,17},{17,1},{2,18},{18,2},{3,19},{19,3},{4,20},{20... | collective-permute-start | bytes 786440 | tf_op jit(solution)/shard_map/ppermute | solution.py:514
  3.8 5.5 %collective-permute-start = (f32[8,256]{1,0:T(8,128)S(1)}, f32[8,256]{1,0:T(8,128)S(1)}, u32[]{:S(2)}, u32[]{:S(2)}) collective-permute-start(f32[8,256]{1,0:T(8,128)S(1)} %get-tuple-element.55.refs_3_), channel_id=1, source_target_pairs={{0,3},{1,2},{2,1},{3,0},{4,7},{5,6},{6,5},{7,4},{8,11},{9,10},{10,... | collective-permute-start | bytes 24584 | tf_op jit(solution)/shard_map/ppermute | solution.py:510
  7.7 3.7 %collective-permute-start.1 = (f32[8,256]{1,0:T(8,128)S(1)}, f32[8,256]{1,0:T(8,128)S(1)}, u32[]{:S(2)}, u32[]{:S(2)}) collective-permute-start(f32[8,256]{1,0:T(8,128)S(1)} %get-tuple-element.55.refs_3_), channel_id=1, source_target_pairs={{0,2},{1,3},{2,0},{3,1},{4,6},{5,7},{6,4},{7,5},{8,10},{9,11},{10,... | collective-permute-start | bytes 24584 | tf_op jit(solution)/shard_map/ppermute | solution.py:510
  8.2 3.7 %collective-permute-start.2 = (f32[8,256]{1,0:T(8,128)S(1)}, f32[8,256]{1,0:T(8,128)S(1)}, u32[]{:S(2)}, u32[]{:S(2)}) collective-permute-start(f32[8,256]{1,0:T(8,128)S(1)} %get-tuple-element.55.refs_3_), channel_id=1, source_target_pairs={{0,1},{1,0},{2,3},{3,2},{4,5},{5,4},{6,7},{7,6},{8,9},{9,8},{10,11... | collective-permute-start | bytes 24584 | tf_op jit(solution)/shard_map/ppermute | solution.py:510
  9.3 3.7 %collective-permute-start.6 = (f32[8,512]{1,0:T(8,128)S(1)}, f32[8,512]{1,0:T(8,128)S(1)}, u32[]{:S(2)}, u32[]{:S(2)}) collective-permute-start(f32[8,512]{1,0:T(8,128)S(1)} %get-tuple-element.62), channel_id=1, source_target_pairs={{0,16},{16,0},{1,17},{17,1},{2,18},{18,2},{3,19},{19,3},{4,20},{20... | collective-permute-start | bytes 49160 | tf_op jit(solution)/shard_map/ppermute | solution.py:514
  11.8 1.2 %collective-permute-start.3 = (f32[8,256]{1,0:T(8,128)S(1)}, f32[8,256]{1,0:T(8,128)S(1)}, u32[]{:S(2)}, u32[]{:S(2)}) collective-permute-start(f32[8,256]{1,0:T(8,128)S(1)} %shard_map.121), channel_id=1, source_target_pairs={{0,16},{16,0},{1,17},{17,1},{2,18},{18,2},{3,19},{19,3},{4,20},{20... | collective-permute-start | bytes 24584 | tf_op jit(solution)/shard_map/ppermute | solution.py:514
  15.1 4.0 %collective-permute-start.7 = (f32[12,512]{1,0:T(8,128)S(1)}, f32[12,512]{1,0:T(8,128)S(1)}, u32[]{:S(2)}, u32[]{:S(2)}) collective-permute-start(f32[12,512]{1,0:T(8,128)S(1)} %get-tuple-element.64.own_ref), channel_id=1, source_target_pairs={{0,4},{4,0},{8,12},{12,8},{1,5},{5,1},{9,13},{13,9},{2,6},{6,2},{1... | collective-permute-start | bytes 73736 | tf_op jit(solution)/shard_map/ppermute | solution.py:510
  19.1 4.7 %collective-permute-start.8 = (f32[4,512]{1,0:T(4,128)S(1)}, f32[4,512]{1,0:T(4,128)S(1)}, u32[]{:S(2)}, u32[]{:S(2)}) collective-permute-start(f32[4,512]{1,0:T(4,128)S(1)} %shard_map.123), channel_id=1, source_target_pairs={{0,8},{4,12},{8,0},{12,4},{1,9},{5,13},{9,1},{13,5},{2,10},{6,14},... | collective-permute-start | bytes 24584 | tf_op jit(solution)/shard_map/ppermute | solution.py:510
  25.4 13.1 %collective-permute-start.15 = (bf16[2,272,256]{2,1,0:T(8,128)(2,1)S(1)}, bf16[2,272,256]{2,1,0:T(8,128)(2,1)S(1)}, u32[]{:S(2)}, u32[]{:S(2)}) collective-permute-start(bf16[2,272,256]{2,1,0:T(8,128)(2,1)S(1)} %get-tuple-element.81), channel_id=1, source_target_pairs={{0,4},{4,0},{8,12},{12,8},{1,5},{5,1},{9,13},{13,9},{2,6},{6,2},{1... | collective-permute-start | bytes 835592 | tf_op jit(solution)/shard_map/ppermute | solution.py:510
  27.0 1.2 %collective-permute-start.9 = (f32[8,256]{1,0:T(8,128)S(1)}, f32[8,256]{1,0:T(8,128)S(1)}, u32[]{:S(2)}, u32[]{:S(2)}) collective-permute-start(f32[8,256]{1,0:T(8,128)S(1)} %get-tuple-element.73.refs_0_), channel_id=1, source_target_pairs={{0,16},{16,0},{1,17},{17,1},{2,18},{18,2},{3,19},{19,3},{4,20},{20... | collective-permute-start | bytes 24584 | tf_op jit(solution)/shard_map/ppermute | solution.py:514
  28.2 4.5 %collective-permute-start.10 = (f32[8,256]{1,0:T(8,128)S(1)}, f32[8,256]{1,0:T(8,128)S(1)}, u32[]{:S(2)}, u32[]{:S(2)}) collective-permute-start(f32[8,256]{1,0:T(8,128)S(1)} %shard_map.126.refs_3_), channel_id=1, source_target_pairs={{0,3},{1,2},{2,1},{3,0},{4,7},{5,6},{6,5},{7,4},{8,11},{9,10},{10,... | collective-permute-start | bytes 24584 | tf_op jit(solution)/shard_map/ppermute | solution.py:510
  29.6 3.7 %collective-permute-start.11 = (f32[8,256]{1,0:T(8,128)S(1)}, f32[8,256]{1,0:T(8,128)S(1)}, u32[]{:S(2)}, u32[]{:S(2)}) collective-permute-start(f32[8,256]{1,0:T(8,128)S(1)} %shard_map.126.refs_3_), channel_id=1, source_target_pairs={{0,2},{1,3},{2,0},{3,1},{4,6},{5,7},{6,4},{7,5},{8,10},{9,11},{10,... | collective-permute-start | bytes 24584 | tf_op jit(solution)/shard_map/ppermute | solution.py:510
  30.2 3.7 %collective-permute-start.12 = (f32[8,256]{1,0:T(8,128)S(1)}, f32[8,256]{1,0:T(8,128)S(1)}, u32[]{:S(2)}, u32[]{:S(2)}) collective-permute-start(f32[8,256]{1,0:T(8,128)S(1)} %shard_map.126.refs_3_), channel_id=1, source_target_pairs={{0,1},{1,0},{2,3},{3,2},{4,5},{5,4},{6,7},{7,6},{8,9},{9,8},{10,11... | collective-permute-start | bytes 24584 | tf_op jit(solution)/shard_map/ppermute | solution.py:510
  34.5 4.0 %collective-permute-start.13 = (f32[12,512]{1,0:T(8,128)S(1)}, f32[12,512]{1,0:T(8,128)S(1)}, u32[]{:S(2)}, u32[]{:S(2)}) collective-permute-start(f32[12,512]{1,0:T(8,128)S(1)} %get-tuple-element.74.own_ref), channel_id=1, source_target_pairs={{0,4},{4,0},{8,12},{12,8},{1,5},{5,1},{9,13},{13,9},{2,6},{6,2},{1... | collective-permute-start | bytes 73736 | tf_op jit(solution)/shard_map/ppermute | solution.py:510
  38.6 9.2 %collective-permute-start.16 = (bf16[272,256]{1,0:T(8,128)(2,1)S(1)}, bf16[272,256]{1,0:T(8,128)(2,1)S(1)}, u32[]{:S(2)}, u32[]{:S(2)}) collective-permute-start(bf16[272,256]{1,0:T(8,128)(2,1)S(1)} %get-tuple-element.84), channel_id=1, source_target_pairs={{0,8},{4,12},{8,0},{12,4},{1,9},{5,13},{9,1},{13,5},{2,10},{6,14},... | collective-permute-start | bytes 417800 | tf_op jit(solution)/shard_map/ppermute | solution.py:510
  41.3 6.4 %collective-permute-start.14 = (f32[4,512]{1,0:T(4,128)S(1)}, f32[4,512]{1,0:T(4,128)S(1)}, u32[]{:S(2)}, u32[]{:S(2)}) collective-permute-start(f32[4,512]{1,0:T(4,128)S(1)} %shard_map.128), channel_id=1, source_target_pairs={{0,8},{4,12},{8,0},{12,4},{1,9},{5,13},{9,1},{13,5},{2,10},{6,14},... | collective-permute-start | bytes 24584 | tf_op jit(solution)/shard_map/ppermute | solution.py:510
  47.7 13.3 %collective-permute-start.21 = (bf16[272,256]{1,0:T(8,128)(2,1)S(1)}, bf16[272,256]{1,0:T(8,128)(2,1)S(1)}, u32[]{:S(2)}, u32[]{:S(2)}) collective-permute-start(bf16[272,256]{1,0:T(8,128)(2,1)S(1)} %shard_map.130.refs_14_.refs_0_), channel_id=1, source_target_pairs={{0,8},{4,12},{8,0},{12,4},{1,9},{5,13},{9,1},{13,5},{2,10},{6,14},... | collective-permute-start | bytes 417800 | tf_op jit(solution)/shard_map/ppermute | solution.py:510
  49.4 14.6 %collective-permute-start.17 = (bf16[272,256]{1,0:T(8,128)(2,1)S(1)}, bf16[272,256]{1,0:T(8,128)(2,1)S(1)}, u32[]{:S(2)}, u32[]{:S(2)}) collective-permute-start(bf16[272,256]{1,0:T(8,128)(2,1)S(1)} %get-tuple-element.87), channel_id=1, source_target_pairs={{0,8},{4,12},{8,0},{12,4},{1,9},{5,13},{9,1},{13,5},{2,10},{6,14},... | collective-permute-start | bytes 417800 | tf_op jit(solution)/shard_map/ppermute | solution.py:510
  52.3 12.2 %collective-permute-start.18 = (bf16[272,256]{1,0:T(8,128)(2,1)S(1)}, bf16[272,256]{1,0:T(8,128)(2,1)S(1)}, u32[]{:S(2)}, u32[]{:S(2)}) collective-permute-start(bf16[272,256]{1,0:T(8,128)(2,1)S(1)} %get-tuple-element.88), channel_id=1, source_target_pairs={{0,4},{4,0},{8,12},{12,8},{1,5},{5,1},{9,13},{13,9},{2,6},{6,2},{1... | collective-permute-start | bytes 417800 | tf_op jit(solution)/shard_map/ppermute | solution.py:510
  52.5 12.1 %collective-permute-start.19 = (bf16[272,256]{1,0:T(8,128)(2,1)S(1)}, bf16[272,256]{1,0:T(8,128)(2,1)S(1)}, u32[]{:S(2)}, u32[]{:S(2)}) collective-permute-start(bf16[272,256]{1,0:T(8,128)(2,1)S(1)} %get-tuple-element.89), channel_id=1, source_target_pairs={{0,12},{4,8},{8,4},{12,0},{1,13},{5,9},{9,5},{13,1},{2,14},{6,10},... | collective-permute-start | bytes 417800 | tf_op jit(solution)/shard_map/ppermute | solution.py:510
  54.8 1.2 %collective-permute-start.20 = (f32[8,256]{1,0:T(8,128)S(1)}, f32[8,256]{1,0:T(8,128)S(1)}, u32[]{:S(2)}, u32[]{:S(2)}) collective-permute-start(f32[8,256]{1,0:T(8,128)S(1)} %get-tuple-element.90.refs_0_), channel_id=1, source_target_pairs={{0,16},{16,0},{1,17},{17,1},{2,18},{18,2},{3,19},{19,3},{4,20},{20... | collective-permute-start | bytes 24584 | tf_op jit(solution)/shard_map/ppermute | solution.py:514
  61.1 5.5 %collective-permute-start.22 = (f32[8,256]{1,0:T(8,128)S(1)}, f32[8,256]{1,0:T(8,128)S(1)}, u32[]{:S(2)}, u32[]{:S(2)}) collective-permute-start(f32[8,256]{1,0:T(8,128)S(1)} %shard_map.132.refs_3_), channel_id=1, source_target_pairs={{0,3},{1,2},{2,1},{3,0},{4,7},{5,6},{6,5},{7,4},{8,11},{9,10},{10,... | collective-permute-start | bytes 24584 | tf_op jit(solution)/shard_map/ppermute | solution.py:510
  63.5 3.7 %collective-permute-start.23 = (f32[8,256]{1,0:T(8,128)S(1)}, f32[8,256]{1,0:T(8,128)S(1)}, u32[]{:S(2)}, u32[]{:S(2)}) collective-permute-start(f32[8,256]{1,0:T(8,128)S(1)} %shard_map.132.refs_3_), channel_id=1, source_target_pairs={{0,2},{1,3},{2,0},{3,1},{4,6},{5,7},{6,4},{7,5},{8,10},{9,11},{10,... | collective-permute-start | bytes 24584 | tf_op jit(solution)/shard_map/ppermute | solution.py:510
  64.0 3.7 %collective-permute-start.24 = (f32[8,256]{1,0:T(8,128)S(1)}, f32[8,256]{1,0:T(8,128)S(1)}, u32[]{:S(2)}, u32[]{:S(2)}) collective-permute-start(f32[8,256]{1,0:T(8,128)S(1)} %shard_map.132.refs_3_), channel_id=1, source_target_pairs={{0,1},{1,0},{2,3},{3,2},{4,5},{5,4},{6,7},{7,6},{8,9},{9,8},{10,11... | collective-permute-start | bytes 24584 | tf_op jit(solution)/shard_map/ppermute | solution.py:510
  64.5 13.8 %collective-permute-start.26 = (bf16[272,256]{1,0:T(8,128)(2,1)S(1)}, bf16[272,256]{1,0:T(8,128)(2,1)S(1)}, u32[]{:S(2)}, u32[]{:S(2)}) collective-permute-start(bf16[272,256]{1,0:T(8,128)(2,1)S(1)} %shard_map.130.refs_14_.refs_0_), channel_id=1, source_target_pairs={{0,4},{4,0},{8,12},{12,8},{1,5},{5,1},{9,13},{13,9},{2,6},{6,2},{1... | collective-permute-start | bytes 417800 | tf_op jit(solution)/shard_map/ppermute | solution.py:510
  64.6 9.3 %collective-permute-start.27 = (bf16[272,256]{1,0:T(8,128)(2,1)S(1)}, bf16[272,256]{1,0:T(8,128)(2,1)S(1)}, u32[]{:S(2)}, u32[]{:S(2)}) collective-permute-start(bf16[272,256]{1,0:T(8,128)(2,1)S(1)} %collective-permute-done.21.refs_2_), channel_id=1, source_target_pairs={{0,4},{4,0},{8,12},{12,8},{1,5},{5,1},{9,13},{13,9},{2,6},{6,2},{1... | collective-permute-start | bytes 417800 | tf_op jit(solution)/shard_map/ppermute | solution.py:510
  67.7 7.8 %collective-permute-start.30 = (bf16[272,256]{1,0:T(8,128)(2,1)S(1)}, bf16[272,256]{1,0:T(8,128)(2,1)S(1)}, u32[]{:S(2)}, u32[]{:S(2)}) collective-permute-start(bf16[272,256]{1,0:T(8,128)(2,1)S(1)} %shard_map.135.refs_4_), channel_id=1, source_target_pairs={{0,12},{4,8},{8,4},{12,0},{1,13},{5,9},{9,5},{13,1},{2,14},{6,10},... | collective-permute-start | bytes 417800 | tf_op jit(solution)/shard_map/ppermute | solution.py:510
  69.9 8.4 %collective-permute-start.29 = (bf16[272,256]{1,0:T(8,128)(2,1)S(1)}, bf16[272,256]{1,0:T(8,128)(2,1)S(1)}, u32[]{:S(2)}, u32[]{:S(2)}) collective-permute-start(bf16[272,256]{1,0:T(8,128)(2,1)S(1)} %shard_map.135.refs_4_), channel_id=1, source_target_pairs={{0,8},{4,12},{8,0},{12,4},{1,9},{5,13},{9,1},{13,5},{2,10},{6,14},... | collective-permute-start | bytes 417800 | tf_op jit(solution)/shard_map/ppermute | solution.py:510
  69.9 9.0 %collective-permute-start.28 = (bf16[272,256]{1,0:T(8,128)(2,1)S(1)}, bf16[272,256]{1,0:T(8,128)(2,1)S(1)}, u32[]{:S(2)}, u32[]{:S(2)}) collective-permute-start(bf16[272,256]{1,0:T(8,128)(2,1)S(1)} %shard_map.135.refs_4_), channel_id=1, source_target_pairs={{0,4},{4,0},{8,12},{12,8},{1,5},{5,1},{9,13},{13,9},{2,6},{6,2},{1... | collective-permute-start | bytes 417800 | tf_op jit(solution)/shard_map/ppermute | solution.py:510
  73.8 6.1 %collective-permute-start.31 = (bf16[272,256]{1,0:T(8,128)(2,1)S(1)}, bf16[272,256]{1,0:T(8,128)(2,1)S(1)}, u32[]{:S(2)}, u32[]{:S(2)}) collective-permute-start(bf16[272,256]{1,0:T(8,128)(2,1)S(1)} %broadcast_select_fusion.3), channel_id=1, source_target_pairs={{0,16},{16,0},{1,17},{17,1},{2,18},{18,2},{3,19},{19,3},{4,20},{20... | collective-permute-start | bytes 417800 | tf_op jit(solution)/shard_map/ppermute | solution.py:514
  75.5 3.5 %collective-permute-start.25 = (bf16[256,512]{1,0:T(8,128)(2,1)S(1)}, bf16[256,512]{1,0:T(8,128)(2,1)S(1)}, u32[]{:S(2)}, u32[]{:S(2)}) collective-permute-start(bf16[256,512]{1,0:T(8,128)(2,1)S(1)} %get-tuple-element.97), channel_id=1, source_target_pairs={{0,16},{16,0},{1,17},{17,1},{2,18},{18,2},{3,19},{19,3},{4,20},{20... | collective-permute-start | bytes 786440 | tf_op jit(solution)/shard_map/ppermute | solution.py:514
  78.4 1.6 %collective-permute-start.34 = (bf16[272,256]{1,0:T(8,128)(2,1)S(1)}, bf16[272,256]{1,0:T(8,128)(2,1)S(1)}, u32[]{:S(2)}, u32[]{:S(2)}) collective-permute-start(bf16[272,256]{1,0:T(8,128)(2,1)S(1)} %broadcast_select_fusion), channel_id=1, source_target_pairs={{0,16},{16,0},{1,17},{17,1},{2,18},{18,2},{3,19},{19,3},{4,20},{20... | collective-permute-start | bytes 417800 | tf_op jit(solution)/shard_map/ppermute | solution.py:514
  78.4 1.6 %collective-permute-start.33 = (bf16[272,256]{1,0:T(8,128)(2,1)S(1)}, bf16[272,256]{1,0:T(8,128)(2,1)S(1)}, u32[]{:S(2)}, u32[]{:S(2)}) collective-permute-start(bf16[272,256]{1,0:T(8,128)(2,1)S(1)} %broadcast_select_fusion.1), channel_id=1, source_target_pairs={{0,16},{16,0},{1,17},{17,1},{2,18},{18,2},{3,19},{19,3},{4,20},{20... | collective-permute-start | bytes 417800 | tf_op jit(solution)/shard_map/ppermute | solution.py:514
  79.0 1.4 %collective-permute-start.32 = (bf16[272,256]{1,0:T(8,128)(2,1)S(1)}, bf16[272,256]{1,0:T(8,128)(2,1)S(1)}, u32[]{:S(2)}, u32[]{:S(2)}) collective-permute-start(bf16[272,256]{1,0:T(8,128)(2,1)S(1)} %broadcast_select_fusion.2), channel_id=1, source_target_pairs={{0,16},{16,0},{1,17},{17,1},{2,18},{18,2},{3,19},{19,3},{4,20},{20... | collective-permute-start | bytes 417800 | tf_op jit(solution)/shard_map/ppermute | solution.py:514
